TPU v7x, 256 devices: a whole 4x4x8 slice. The times are simulated.
256 devices in a mesh: slab: 32 (over y_hi, z, core), blk: 8 (over x, y_lo).
Axes of the slice: x: 4, y: 4 (y_hi: 2, y_lo: 2; y = y_hi * 2 + y_lo), z: 8, core: 2. Of those that a mesh axis runs over, the one named last changes fastest.
Arguments:
- current: bfloat16 [768, 3, 96, 9, 128], P('blk', None, 'slab'), may hold values from -6 to 6
- search: bfloat16 [768, 3, 96, 9, 128], P('blk', None, 'slab'), may hold values from -6 to 6
- previous: bfloat16 [768, 3, 96, 9, 128], P('blk', None, 'slab'), may hold values from -6 to 6
- coefficients: bfloat16 [2304, 768], P('slab', 'blk'), may hold values from -0.125 to 0.125
- material: int32 [96, 9, 128], P('slab'), may hold values from 0 to 3
- inverse_permittivity: float32 [4, 3, 3], replicated, may hold values from -0.25 to 1, as said below
Outputs:
- applied: bfloat16 [768, 3, 96, 9, 128], P('blk', None, 'slab')
- rotated: bfloat16 [768, 3, 96, 9, 128], P('blk', None, 'slab')
- direction: bfloat16 [768, 3, 96, 9, 128], P('blk', None, 'slab')
Inputs may be any that keep to these rules, and one draw needn't show every extreme that they name: `inverse_permittivity`: each material's tensor is symmetric; its diagonal entries lie in 0.08 to 1 and each entry off the diagonal is at most a quarter of the geometric mean of the two diagonal entries of its row and column.
All inputs are finite; a program needn't handle non-finite values.
Results may differ from a plain program's by a relative error of at most 0.003.
Values may be sent and summed in bfloat16 or wider, within the bound.
No kernel may reach another device: no remote copies, remote signals or barrier semaphores. Data moves between devices by JAX's collectives and lax.ppermute only.
A program may use at most 256 MiB of HBM per device.

v0:
```python
import jax
import jax.numpy as jnp
from jax import lax
from jax.sharding import PartitionSpec as P

M = 768
NMAT = 4


def shifted(x, axis, by):
    count = lax.axis_size(axis)
    return lax.ppermute(x, axis, [(i, (i + by) % count) for i in range(count)])


def combine_curl(along_x, along_y, along_z):
    curl_x = along_y[:, 2] - along_z[:, 1]
    curl_y = along_z[:, 0] - along_x[:, 2]
    curl_z = along_x[:, 1] - along_y[:, 0]
    return (curl_x, curl_y, curl_z)


def forward_curl(field, tensor):
    centre = field[:, :, :-1]
    along_z = 0.5 * (field[:, :, 1:] - centre)
    along_y = 0.5 * (jnp.roll(centre, -1, axis=3) - centre)
    along_x = 0.5 * (jnp.roll(centre, -1, axis=4) - centre)
    curl_x, curl_y, curl_z = combine_curl(along_x, along_y, along_z)
    stacked = [
        tensor[which, 0] * curl_x + tensor[which, 1] * curl_y + tensor[which, 2] * curl_z
        for which in range(3)
    ]
    return jnp.stack(stacked, axis=1)


def backward_curl(field):
    centre = field[:, :, 1:]
    along_z = 0.5 * (centre - field[:, :, :-1])
    along_y = 0.5 * (centre - jnp.roll(centre, 1, axis=3))
    along_x = 0.5 * (centre - jnp.roll(centre, 1, axis=4))
    curl_x, curl_y, curl_z = combine_curl(along_x, along_y, along_z)
    return jnp.stack([curl_x, curl_y, curl_z], axis=1)


def cell_tensor(marks, inverse_permittivity):
    levels = jnp.arange(NMAT, dtype=jnp.float32)[:, None, None, None]
    one_hot = (marks.astype(jnp.float32)[None] == levels).astype(jnp.float32)
    return jnp.einsum(
        "mcd,mzyx->cdzyx", inverse_permittivity, one_hot, precision=lax.Precision.HIGHEST
    )


def contract(coef, block):
    return lax.dot_general(
        coef, block, (((0,), (0,)), ((), ())), preferred_element_type=jnp.float32
    )


def per_device(current, search, previous, coefficients, material, inverse_permittivity):
    tensor = cell_tensor(material, inverse_permittivity)
    upper_rim = shifted(search[:, :, :1], "slab", -1)
    extended = jnp.concatenate([search, upper_rim], axis=2).astype(jnp.float32)
    electric = forward_curl(extended, tensor)
    lower_rim = shifted(electric[:, :, -1:].astype(jnp.bfloat16), "slab", 1).astype(jnp.float32)
    padded = jnp.concatenate([lower_rim, electric], axis=2)
    applied = backward_curl(padded).astype(jnp.bfloat16)
    shape = current.shape
    panel = shape[0]
    flat_current = current.reshape(panel, -1)
    flat_search = search.reshape(panel, -1)
    flat_previous = previous.reshape(panel, -1)
    current_cells, search_cells, previous_cells = (
        lax.all_to_all(flat_current, "blk", split_axis=1, concat_axis=0, tiled=True),
        lax.all_to_all(flat_search, "blk", split_axis=1, concat_axis=0, tiled=True),
        lax.all_to_all(flat_previous, "blk", split_axis=1, concat_axis=0, tiled=True),
    )
    tiles = lax.all_gather(coefficients[None], ("slab", "blk"), axis=0, tiled=True)
    rows_local, cols_local = coefficients.shape
    full_coeffs = (
        tiles.reshape(lax.axis_size("slab"), lax.axis_size("blk"), rows_local, cols_local)
        .transpose(0, 2, 1, 3)
        .reshape(3 * M, M)
    )
    direction_sum = contract(full_coeffs[M : 2 * M], search_cells) + contract(
        full_coeffs[2 * M :], previous_cells
    )
    rotated_sum = contract(full_coeffs[:M], current_cells) + direction_sum
    rotated_back, direction_back = (
        lax.all_to_all(
            rotated_sum.astype(jnp.bfloat16), "blk", split_axis=0, concat_axis=1, tiled=True
        ),
        lax.all_to_all(
            direction_sum.astype(jnp.bfloat16), "blk", split_axis=0, concat_axis=1, tiled=True
        ),
    )
    return (applied, rotated_back.reshape(shape), direction_back.reshape(shape))


def solution(mesh):
    in_specs = (
        P("blk", None, "slab", None, None),
        P("blk", None, "slab", None, None),
        P("blk", None, "slab", None, None),
        P("slab", "blk"),
        P("slab", None, None),
        P(),
    )
    out_specs = (
        P("blk", None, "slab", None, None),
        P("blk", None, "slab", None, None),
        P("blk", None, "slab", None, None),
    )
    return jax.shard_map(
        per_device, mesh=mesh, in_specs=in_specs, out_specs=out_specs, check_vma=False
    )
```

profile of v0, /device:TPU:16, one launch (start us, length us, event | category | flops | bytes accessed | tf_op | source)
XLA Modules:
  0.0 867.4 jit_solution(18167701997363642619)
XLA Ops:
  7.9 3.0 copy.67
  11.0 2.6 copy.68
  13.6 5.0 all-to-all-start.1
  18.6 3.0 copy.69
  21.6 2.6 copy.70
  24.2 26.8 %all-to-all-done.1 = bf16[96,8,1296]{2,0,1:T(8,128)(2,1)} async-done(((bf16[96,8,1296]{2,0,1:T(8,128)(2,1)}), bf16[96,8,1296]{2,0,1:T(8,128)(2,1)}, u32[]{:S(2)}, u32[]{:S(2)}) %all-to-all-start.1) | async-done | bytes 1990688 | tf_op jit(solution)/shard_map/all_to_all | solution.py:73
  51.0 4.3 all-to-all-start.2
  55.4 4.4 collective-permute-start
  59.9 4.2 copy.65
  64.1 4.4 copy.66
  69.5 16.9 %all-to-all-done.2 = bf16[96,8,1296]{2,0,1:T(8,128)(2,1)} async-done(((bf16[96,8,1296]{2,0,1:T(8,128)(2,1)}), bf16[96,8,1296]{2,0,1:T(8,128)(2,1)}, u32[]{:S(2)}, u32[]{:S(2)}) %all-to-all-start.2) | async-done | bytes 1990688 | tf_op jit(solution)/shard_map/all_to_all | solution.py:74
  86.4 4.5 all-to-all-start
  92.2 3.5 slice.169
  100.1 633.1 %all-gather.3.cloned.1.call-done = bf16[18432,96]{1,0:T(8,128)(2,1)} async-done(((bf16[72,96]{1,0:T(8,128)(2,1)}), bf16[18432,96]{1,0:T(8,128)(2,1)}) %all-gather.3.cloned.1.call-update) | async-done | bytes 3538960 | tf_op jit(solution)/shard_map/all_gather | solution.py:76
  733.2 5.4 copy.90
  738.6 8.3 reshape.52
  746.8 3.8 fusion.11
  750.7 6.5 fusion.19
  757.2 6.2 add_convert_fusion
  763.3 4.1 copy.71
  767.4 16.9 %all-to-all-start.3 = ((bf16[8,96,1296]{2,1,0:T(8,128)(2,1)}), bf16[8,96,1296]{2,1,0:T(8,128)(2,1)}, u32[]{:S(2)}, u32[]{:S(2)}) async-start(bf16[8,96,1296]{2,1,0:T(8,128)(2,1)} %bitcast.65), calls=%async_computation.3 | async-start | bytes 4325376 | tf_op jit(solution)/shard_map/all_to_all | solution.py:88
  784.4 7.6 fusion.4
  797.8 4.1 copy.73
  801.9 11.0 %all-to-all-done.3 = bf16[8,96,1296]{2,1,0:T(8,128)(2,1)} async-done(((bf16[8,96,1296]{2,1,0:T(8,128)(2,1)}), bf16[8,96,1296]{2,1,0:T(8,128)(2,1)}, u32[]{:S(2)}, u32[]{:S(2)}) %all-to-all-start.3) | async-done | bytes 1990688 | tf_op jit(solution)/shard_map/all_to_all | solution.py:88
  812.8 4.8 all-to-all-start.4
  817.6 3.4 slice.187
  821.4 5.0 collective-permute-done.1
  827.6 4.4 fusion.1
  832.0 3.2 fusion.9
  836.7 3.2 copy.72
  842.3 12.6 %all-to-all-done.4 = bf16[8,96,1296]{2,1,0:T(8,128)(2,1)} async-done(((bf16[8,96,1296]{2,1,0:T(8,128)(2,1)}), bf16[8,96,1296]{2,1,0:T(8,128)(2,1)}, u32[]{:S(2)}, u32[]{:S(2)}) %all-to-all-start.4) | async-done | bytes 1990688 | tf_op jit(solution)/shard_map/all_to_all | solution.py:91
  854.9 3.2 copy.74
  (56 shorter events, 21.0 us)
Async XLA Ops:
  7.2 61.3 %copy-start = (f32[4,3,3]{2,0,1:T(4,128)S(1)}, f32[4,3,3]{2,0,1:T(4,128)}, u32[]{:S(2)}) copy-start(f32[4,3,3]{2,0,1:T(4,128)} %param.11) | copy-start | bytes 436
  7.2 726.0 %all-gather.3.cloned.1.call-start = ((), (), s32[]{:S(2)}) async-start(), calls=%async_computation.5 | async-start | bytes 4737024 | tf_op jit(solution)/shard_map/all_gather | solution.py:76
  13.6 37.4 %all-to-all-start.1 = ((bf16[96,8,1296]{2,0,1:T(8,128)(2,1)}), bf16[96,8,1296]{2,0,1:T(8,128)(2,1)}, u32[]{:S(2)}, u32[]{:S(2)}) async-start(bf16[96,8,1296]{2,0,1:T(8,128)(2,1)} %copy.68), calls=%async_computation.1 | async-start | bytes 4325376 | tf_op jit(solution)/shard_map/all_to_all | solution.py:73
  24.2 31.1 %copy-start.5 = (bf16[96,3,3,9,128]{4,0,3,2,1:T(8,128)(2,1)S(1)}, bf16[96,3,3,9,128]{4,0,3,2,1:T(8,128)(2,1)}, u32[]{:S(2)}) copy-start(bf16[96,3,3,9,128]{4,0,3,2,1:T(8,128)(2,1)} %param.7) | copy-start | bytes 5971972
  24.2 35.6 %copy-start.8 = (s32[3,9,128]{2,0,1:T(4,128)S(1)}, s32[3,9,128]{2,0,1:T(4,128)}, u32[]{:S(2)}) copy-start(s32[3,9,128]{2,0,1:T(4,128)} %param.10) | copy-start | bytes 41476
  51.0 35.4 %all-to-all-start.2 = ((bf16[96,8,1296]{2,0,1:T(8,128)(2,1)}), bf16[96,8,1296]{2,0,1:T(8,128)(2,1)}, u32[]{:S(2)}, u32[]{:S(2)}) async-start(bf16[96,8,1296]{2,0,1:T(8,128)(2,1)} %copy.70), calls=%async_computation.2 | async-start | bytes 4325376 | tf_op jit(solution)/shard_map/all_to_all | solution.py:74
  55.4 36.4 %collective-permute-start = (bf16[96,3,1,9,128]{4,0,3,2,1:T(8,128)(2,1)S(1)}, bf16[96,3,1,9,128]{4,0,3,2,1:T(8,128)(2,1)S(1)}, u32[]{:S(2)}, u32[]{:S(2)}) collective-permute-start(bf16[96,3,1,9,128]{4,0,3,2,1:T(8,128)(2,1)S(1)} %slice.125), channel_id=1, source_target_pairs={{0,248},{8,0},{16,8},{24,16},{32,24},{40,32},{48,40},{56,48},{64,5... | collective-permute-start | bytes 1990664 | tf_op jit(solution)/shard_map/ppermute | solution.py:12
  86.4 670.8 %all-to-all-start = ((bf16[96,8,1296]{2,0,1:T(8,128)(2,1)}), bf16[96,8,1296]{2,0,1:T(8,128)(2,1)}, u32[]{:S(2)}, u32[]{:S(2)}) async-start(bf16[96,8,1296]{2,0,1:T(8,128)(2,1)} %copy.66), calls=%async_computation | async-start | bytes 4325376 | tf_op jit(solution)/shard_map/all_to_all | solution.py:72
  92.2 5.9 copy-start.2
  767.4 45.4 %all-to-all-start.3 = ((bf16[8,96,1296]{2,1,0:T(8,128)(2,1)}), bf16[8,96,1296]{2,1,0:T(8,128)(2,1)}, u32[]{:S(2)}, u32[]{:S(2)}) async-start(bf16[8,96,1296]{2,1,0:T(8,128)(2,1)} %bitcast.65), calls=%async_computation.3 | async-start | bytes 4325376 | tf_op jit(solution)/shard_map/all_to_all | solution.py:88
  794.5 1.1 copy-start.6
  795.6 2.0 copy-start.3
  797.7 28.7 %collective-permute-start.1 = (bf16[96,3,1,9,128]{4,0,3,2,1:T(8,128)(2,1)S(1)}, bf16[96,3,1,9,128]{4,0,3,2,1:T(8,128)(2,1)}, u32[]{:S(2)}, u32[]{:S(2)}) collective-permute-start(bf16[96,3,1,9,128]{4,0,3,2,1:T(8,128)(2,1)S(1)} %slice.262), channel_id=1, source_target_pairs={{0,8},{8,16},{16,24},{24,32},{32,40},{40,48},{48,56},{56,64},{64,7... | collective-permute-start | bytes 1990664 | tf_op jit(solution)/shard_map/ppermute | solution.py:12
  812.8 42.1 %all-to-all-start.4 = ((bf16[8,96,1296]{2,1,0:T(8,128)(2,1)}), bf16[8,96,1296]{2,1,0:T(8,128)(2,1)}, u32[]{:S(2)}, u32[]{:S(2)}) async-start(bf16[8,96,1296]{2,1,0:T(8,128)(2,1)} %bitcast.64), calls=%async_computation.4 | async-start | bytes 4325376 | tf_op jit(solution)/shard_map/all_to_all | solution.py:91
  817.6 3.4 copy-start.4
  821.3 6.3 copy-start.7
  858.1 2.4 copy-start.1
Sparse Core Ops, SparseCore 0:
  9.9 723.2 all-gather.2
where the time goes:
time: 884 us; the launch traced here: 867 us
  waiting for transfers between devices  706 us (80%)
  local copies, waits for them, and re-layouts  68.8 us (8%)
  starting transfers between devices  40.2 us (5%)
  other arithmetic  21.2 us (2%)
  matrix products  16.8 us (2%)
  between operations  14.4 us (2%)
    all_gather x1, waiting for transfers between devices, per_device(): lax.all_gather(coefficients[None], ('slab', 'blk'), axis=0, tiled=True)  633 us
    all_to_all x1, waiting for transfers between devices, per_device(): lax.all_to_all(flat_search, 'blk', split_axis=1, concat_axis=0, tiled=True)  26.8 us
    unnamed x23, local copies, waits for them, and re-layouts  17.9 us
  transfers between devices with their start and end apart: 8, of which 6 were waited for; matrix products, arithmetic and copies ran while one was open for 10% of the time, Pallas kernels for 0%

commit v1 on v0

v1 whole, which is shorter than its diff:
```python
import functools
import itertools

import jax
import jax.numpy as jnp
from jax import lax
from jax.experimental import pallas as pl
from jax.experimental.pallas import tpu as pltpu
from jax.sharding import PartitionSpec as P

M = 768
NMAT = 4
V = 96
NB = 8
ROWS = 81
SHARE = 10
LANES = 128 // NB
SLAB = (2, 8, 2)
BLK = (4, 2)
ANY = pl.BlockSpec(memory_space=pl.ANY)
VMEM_LIMIT = 56 * 1024 * 1024


def move(x, axis, sizes, steps):
    pairs = []
    for place in itertools.product(*[range(n) for n in sizes]):
        src = dst = 0
        for n, p, s in zip(sizes, place, steps):
            src = src * n + p
            dst = dst * n + (p + s) % n
        pairs.append((src, dst))
    return lax.ppermute(x, axis, pairs)


def ring_shift(x, axis, by):
    count = lax.axis_size(axis)
    return lax.ppermute(x, axis, [(i, (i + by) % count) for i in range(count)])


def in_order(parts, me):
    count = len(parts)
    if count == 2:
        first = jnp.where(me == 0, parts[0], parts[1])
        second = jnp.where(me == 0, parts[1], parts[0])
        return jnp.stack([first, second])
    twice = jnp.stack(parts + parts)
    return lax.dynamic_slice_in_dim(twice, (count - me) % count, count, 0)


def gather_coefficients(tile):
    slab, blk = lax.axis_index("slab"), lax.axis_index("blk")
    y_hi, z, core = slab // 16, (slab // 2) % 8, slab % 2
    x, y_lo = blk // 2, blk % 2
    t = in_order([tile, move(tile, "blk", BLK, (0, 1))], y_lo)
    t = in_order([t] + [move(t, "blk", BLK, (-k, 0)) for k in (1, 2, 3)], x)
    t = in_order([t, move(t, "slab", SLAB, (1, 0, 0))], y_hi)
    got = {0: t}
    for k in (1, 2, 3, 4):
        got[k] = move(got[k - 1], "slab", SLAB, (0, -1, 0))
        if k < 4:
            got[-k] = move(got[1 - k], "slab", SLAB, (0, 1, 0))
    t = in_order([got[k if k <= 4 else k - 8] for k in range(8)], z)
    t = in_order([t, move(t, "slab", SLAB, (0, 0, 1))], core)
    return t.transpose(3, 4, 6, 2, 1, 0, 5).reshape(M, 3 * M)


def lane_index(shape):
    return lax.broadcasted_iota(jnp.int32, shape, len(shape) - 1)


def rolled(x, by):
    by %= 128
    return x if by == 0 else pltpu.roll(x, by, x.ndim - 1)


def pack_kernel(w_ref, p_ref, x_ref, out_ref, tail, mixed, sems, tail_sems, out_sems):
    fields = (w_ref, p_ref, x_ref)
    copies = []
    for d in range(NB):
        for k, ref in enumerate(fields):
            copies.append(
                pltpu.make_async_copy(
                    ref.at[pl.ds(SHARE * d, SHARE)],
                    out_ref.at[d, pl.ds(SHARE * k, SHARE)],
                    sems.at[3 * d + k],
                )
            )
    last = [
        pltpu.make_async_copy(ref.at[ROWS - 1], tail.at[k], tail_sems.at[k])
        for k, ref in enumerate(fields)
    ]
    for c in last + copies:
        c.start()
    for c in last:
        c.wait()
    lane = lane_index((V, 128))
    w, p, x = (tail[k].astype(jnp.float32) for k in range(3))
    sends = []
    for d in range(NB):
        row = jnp.where(lane < 3 * LANES, rolled(x, LANES * (2 - d)), 0.0)
        row = jnp.where(lane < 2 * LANES, rolled(p, LANES * (1 - d)), row)
        row = jnp.where(lane < LANES, rolled(w, LANES * (0 - d)), row)
        mixed[d] = row.astype(jnp.bfloat16)
        sends.append(
            pltpu.make_async_copy(mixed.at[d], out_ref.at[d, 3 * SHARE], out_sems.at[d])
        )
        sends[-1].start()
    for c in copies + sends:
        c.wait()


def pack(w, p, x):
    return pl.pallas_call(
        pack_kernel,
        out_shape=jax.ShapeDtypeStruct((NB, 3 * SHARE + 1, V, 128), jnp.bfloat16),
        in_specs=[ANY] * 3,
        out_specs=ANY,
        scratch_shapes=[
            pltpu.VMEM((3, V, 128), jnp.bfloat16),
            pltpu.VMEM((NB, V, 128), jnp.bfloat16),
            pltpu.SemaphoreType.DMA((3 * NB,)),
            pltpu.SemaphoreType.DMA((3,)),
            pltpu.SemaphoreType.DMA((NB,)),
        ],
        compiler_params=pltpu.CompilerParams(vmem_limit_bytes=VMEM_LIMIT),
        name="pack",
    )(w, p, x)


def rotate_kernel(cells_ref, coef_ref, out_ref, cells, out, in_sems, out_sems):
    def fetch(k, i):
        rows = pl.ds(SHARE * k + 2 * i, 2)
        return pltpu.make_async_copy(
            cells_ref.at[:, rows], cells.at[:, rows], in_sems.at[k, i]
        )

    def put(k, i):
        rows = pl.ds(SHARE * k + 2 * i, 2)
        return pltpu.make_async_copy(
            out.at[:, rows], out_ref.at[:, rows], out_sems.at[k, i]
        )

    steps = SHARE // 2
    fetch_tail = pltpu.make_async_copy(
        cells_ref.at[:, pl.ds(3 * SHARE, 1)],
        cells.at[:, pl.ds(3 * SHARE, 1)],
        in_sems.at[0, steps],
    )
    put_tail = pltpu.make_async_copy(
        out.at[:, pl.ds(2 * SHARE, 1)],
        out_ref.at[:, pl.ds(2 * SHARE, 1)],
        out_sems.at[0, steps],
    )
    for i in range(steps):
        for k in range(3):
            fetch(k, i).start()
    fetch_tail.start()

    def product(w, p, x):
        wp = jnp.concatenate([w, p], axis=0)
        direction = jnp.dot(
            coef_ref[:, M:], wp, preferred_element_type=jnp.float32
        )
        rotated = direction + jnp.dot(
            coef_ref[:, :M], x, preferred_element_type=jnp.float32
        )
        return direction, rotated

    def step(i, carry):
        for k in range(3):
            fetch(k, i).wait()

        def row_pair(k):
            first = cells[:, SHARE * k + 2 * i].reshape(M, 128)
            second = cells[:, SHARE * k + 2 * i + 1].reshape(M, 128)
            return jnp.concatenate([first, second], axis=1)

        results = product(row_pair(0), row_pair(1), row_pair(2))
        for k, result in enumerate(results):
            result = result.astype(jnp.bfloat16)
            for j in range(2):
                part = result[:, 128 * j : 128 * (j + 1)]
                out[:, SHARE * k + 2 * i + j] = part.reshape(NB, V, 128)
            put(k, i).start()
        return carry

    lax.fori_loop(0, steps, step, 0)
    fetch_tail.wait()
    tail = cells[:, 3 * SHARE].reshape(M, 128)
    wide = tail.astype(jnp.float32)
    shifted = [rolled(wide, -LANES * k).astype(jnp.bfloat16) for k in (1, 2)]
    direction, rotated = product(tail, *shifted)
    mixed = jnp.where(
        lane_index((M, 128)) < LANES, direction, rolled(rotated, LANES)
    )
    out[:, 2 * SHARE] = mixed.astype(jnp.bfloat16).reshape(NB, V, 128)
    put_tail.start()
    for k in range(2):
        for i in range(steps):
            put(k, i).wait()
    put_tail.wait()


def rotate(cells, coef):
    return pl.pallas_call(
        rotate_kernel,
        out_shape=jax.ShapeDtypeStruct((NB, 2 * SHARE + 1, V, 128), jnp.bfloat16),
        in_specs=[ANY, pl.BlockSpec(memory_space=pltpu.VMEM)],
        out_specs=ANY,
        scratch_shapes=[
            pltpu.VMEM((NB, 3 * SHARE + 1, V, 128), jnp.bfloat16),
            pltpu.VMEM((NB, 2 * SHARE + 1, V, 128), jnp.bfloat16),
            pltpu.SemaphoreType.DMA((3, SHARE // 2 + 1)),
            pltpu.SemaphoreType.DMA((2, SHARE // 2 + 1)),
        ],
        compiler_params=pltpu.CompilerParams(vmem_limit_bytes=VMEM_LIMIT),
        cost_estimate=pl.CostEstimate(
            flops=6 * M * M * 128 * (SHARE + 1), bytes_accessed=14_000_000, transcendentals=0
        ),
        name="rotate",
    )(cells, coef)


def unpack_kernel(in_ref, d_ref, r_ref, tail, last, sems, tail_sems, last_sems):
    copies = []
    for s in range(NB):
        for k, ref in enumerate((d_ref, r_ref)):
            copies.append(
                pltpu.make_async_copy(
                    in_ref.at[s, pl.ds(SHARE * k, SHARE)],
                    ref.at[pl.ds(SHARE * s, SHARE)],
                    sems.at[2 * s + k],
                )
            )
    tails = [
        pltpu.make_async_copy(in_ref.at[s, 2 * SHARE], tail.at[s], tail_sems.at[s])
        for s in range(NB)
    ]
    for c in tails + copies:
        c.start()
    for c in tails:
        c.wait()
    which = lane_index((V, 128)) // LANES
    direction = rotated = jnp.zeros((V, 128), jnp.float32)
    for s in range(NB):
        row = tail[s].astype(jnp.float32)
        direction = jnp.where(which == s, rolled(row, LANES * s), direction)
        rotated = jnp.where(which == s, rolled(row, LANES * (s - 1)), rotated)
    last[0] = direction.astype(jnp.bfloat16)
    last[1] = rotated.astype(jnp.bfloat16)
    for k, ref in enumerate((d_ref, r_ref)):
        copies.append(pltpu.make_async_copy(last.at[k], ref.at[ROWS - 1], last_sems.at[k]))
        copies[-1].start()
    for c in copies:
        c.wait()


def unpack(parts):
    whole = jax.ShapeDtypeStruct((ROWS, V, 128), jnp.bfloat16)
    return pl.pallas_call(
        unpack_kernel,
        out_shape=(whole, whole),
        in_specs=[ANY],
        out_specs=(ANY, ANY),
        scratch_shapes=[
            pltpu.VMEM((NB, V, 128), jnp.bfloat16),
            pltpu.VMEM((2, V, 128), jnp.bfloat16),
            pltpu.SemaphoreType.DMA((2 * NB,)),
            pltpu.SemaphoreType.DMA((NB,)),
            pltpu.SemaphoreType.DMA((2,)),
        ],
        compiler_params=pltpu.CompilerParams(vmem_limit_bytes=VMEM_LIMIT),
        name="unpack",
    )(parts)


NZ, NY = 3, 9
VB = 16


def curl_kernel(eps_ref, mat_ref, w_ref, above_ref, below_ref, out_ref, tensor, electric):
    @pl.when(pl.program_id(0) == 0)
    def _():
        marks = mat_ref[...]
        for c in range(3):
            for d in range(3):
                value = jnp.full(marks.shape, eps_ref[0, c * 3 + d], jnp.float32)
                for m in range(1, NMAT):
                    value = jnp.where(marks == m, eps_ref[m, c * 3 + d], value)
                tensor[c * 3 + d] = 0.25 * value

    def field(c, z, y):
        y %= NY
        if z < 0:
            tile = below_ref[c * NY + y]
        elif z < NZ:
            tile = w_ref[(c * NZ + z) * NY + y]
        else:
            tile = above_ref[c * NY + y]
        return tile.astype(jnp.float32)

    for z in range(-1, NZ):
        for y in range(NY):
            hx, hy, hz = (field(c, z, y) for c in range(3))
            curl = (
                (field(2, z, y + 1) - hz) - (field(1, z + 1, y) - hy),
                (field(0, z + 1, y) - hx) - (rolled(hz, -1) - hz),
                (rolled(hy, -1) - hy) - (field(0, z, y + 1) - hx),
            )
            for c in range(3 if z >= 0 else 2):
                total = None
                for d in range(3):
                    weight = tensor[c * 3 + d, pl.ds((z + 1) * NY + y, 1)]
                    term = weight * curl[d]
                    total = term if total is None else total + term
                electric[c, (z + 1) * NY + y] = total
    for z in range(NZ):
        for y in range(NY):
            before = (y - 1) % NY
            here = (z + 1) * NY
            ex, ey, ez = (electric[c, here + y] for c in range(3))
            applied = (
                (ez - electric[2, here + before]) - (ey - electric[1, here + y - NY]),
                (ex - electric[0, here + y - NY]) - (ez - rolled(ez, 1)),
                (ey - rolled(ey, 1)) - (ex - electric[0, here + before]),
            )
            for c in range(3):
                out_ref[(c * NZ + z) * NY + y] = applied[c].astype(jnp.bfloat16)


def apply_curls(w, above, below, marks, eps):
    block = lambda rows: pl.BlockSpec((rows, VB, 128), lambda i: (0, i, 0))
    return pl.pallas_call(
        curl_kernel,
        out_shape=jax.ShapeDtypeStruct((ROWS, V, 128), jnp.bfloat16),
        grid=(V // VB,),
        in_specs=[
            pl.BlockSpec(memory_space=pltpu.SMEM),
            pl.BlockSpec(memory_space=pltpu.VMEM),
            block(ROWS),
            block(2 * NY),
            block(3 * NY),
        ],
        out_specs=block(ROWS),
        scratch_shapes=[
            pltpu.VMEM((9, (NZ + 1) * NY, 128), jnp.float32),
            pltpu.VMEM((3, (NZ + 1) * NY, VB, 128), jnp.float32),
        ],
        compiler_params=pltpu.CompilerParams(vmem_limit_bytes=VMEM_LIMIT),
        cost_estimate=pl.CostEstimate(
            flops=60_000_000, bytes_accessed=5_000_000, transcendentals=0
        ),
        name="curls",
    )(eps, marks, w, above, below)


def as_rows(x):
    return x.transpose(1, 2, 3, 0, 4).reshape(ROWS, V, 128)


def as_block(rows):
    return rows.reshape(3, NZ, NY, V, 128).transpose(3, 0, 1, 2, 4)


def per_device(current, search, previous, coefficients, material, inverse_permittivity):
    w, p, x = as_rows(search), as_rows(previous), as_rows(current)
    layers = w.reshape(3, NZ, NY, V, 128)
    above = ring_shift(layers[:2, 0].reshape(2 * NY, V, 128), "slab", -1)
    below = ring_shift(layers[:, NZ - 1].reshape(3 * NY, V, 128), "slab", 1)
    mark_below = ring_shift(material[NZ - 1 :], "slab", 1)
    marks = jnp.concatenate([mark_below, material]).reshape((NZ + 1) * NY, 128)
    packed = pack(w, p, x)
    cells = lax.all_to_all(packed, "blk", split_axis=0, concat_axis=0, tiled=True)
    coef = gather_coefficients(coefficients)
    parts = rotate(cells, coef)
    back = lax.all_to_all(parts, "blk", split_axis=0, concat_axis=0, tiled=True)
    applied = apply_curls(w, above, below, marks, inverse_permittivity.reshape(NMAT, 9))
    direction, rotated = unpack(back)
    return as_block(applied), as_block(rotated), as_block(direction)


def solution(mesh):
    block = P("blk", None, "slab", None, None)
    return jax.shard_map(
        per_device,
        mesh=mesh,
        in_specs=(block, block, block, P("slab", "blk"), P("slab", None, None), P()),
        out_specs=(block, block, block),
        check_vma=False,
    )
```

time: 884 us -> 495 us (0.56); the launches traced: 867 us -> 494 us
  waiting for transfers between devices: 706 us -> 87.7 us
  Pallas kernels: 0 us -> 318 us
  local copies, waits for them, and re-layouts: 68.8 us -> 43.2 us
  matrix products: 16.8 us -> 0 us
  other arithmetic: 21.2 us -> 6.21 us
  between operations: 14.4 us -> 1.16 us
    all_gather x1 -> x0, waiting for transfers between devices: 633 us -> none  [per_device(): lax.all_gather(coefficients[None], ('slab', 'blk'), axis=0, tiled=True)]
    pallas_call x0 -> x4, Pallas kernels: none -> 318 us  [the longest x1 180 us: pack(): pl.pallas_call(pack_kernel, out_shape=jax.ShapeDtypeStruct((NB, 3 * SHARE...]
    ppermute x2 -> x16, waiting for transfers between devices: 5.01 us -> 54.2 us  [the longest x13 35.2 us: move(): return lax.ppermute(x, axis, pairs)]
    all_to_all x5 -> x2, waiting for transfers between devices: 67.2 us -> 33.5 us  [the longest x1 29.8 us: per_device(): back = lax.all_to_all(parts, 'blk', split_axis=0, concat_axis=0, tiled=True)]
    all_to_all x5 -> x2, starting transfers between devices: 35.6 us -> 9.42 us  [the longest x1 4.73 us: per_device(): lax.all_to_all(packed, 'blk', split_axis=0, concat_axis=0, tiled=True)]
    ppermute x2 -> x16, starting transfers between devices: 4.52 us -> 28.5 us  [the longest x13 23 us: move(): return lax.ppermute(x, axis, pairs)]
    reshape x2 -> x4, local copies, waits for them, and re-layouts: 13.6 us -> 36.3 us  [the longest x2 35 us: gather_coefficients(): return t.transpose(3, 4, 6, 2, 1, 0, 5).reshape(M, 3 * M)]
    dot_general x4 -> x0, matrix products: 16.8 us -> none  [the longest x3 16.5 us: contract(): lax.dot_general(coef, block, (((0,), (0,)), ((), ())), preferred_element_...]
  transfers between devices with their start and end apart: 8 -> 18, of which waited for: 6 -> 12; matrix products, arithmetic and copies ran while one was open for 10% -> 9% of each run, Pallas kernels for 0% -> 38%
where the time goes in v1:
time: 495 us; the launch traced here: 494 us
  Pallas kernels  318 us (64%)
  waiting for transfers between devices  87.7 us (18%)
  local copies, waits for them, and re-layouts  43.2 us (9%)
  starting transfers between devices  38 us (8%)
  other arithmetic  6.21 us (1%)
    pallas_call x1, Pallas kernels, pack(): pl.pallas_call(pack_kernel, out_shape=jax.ShapeDtypeStruct((NB, 3 * SHARE...  180 us
    pallas_call x1, Pallas kernels, unpack(): pl.pallas_call(unpack_kernel, out_shape=(whole, whole), in_specs=[ANY], o...  120 us
    ppermute x13, waiting for transfers between devices, move(): return lax.ppermute(x, axis, pairs)  35.2 us
    reshape x2, local copies, waits for them, and re-layouts, gather_coefficients(): return t.transpose(3, 4, 6, 2, 1, 0, 5).reshape(M, 3 * M)  35 us
    all_to_all x1, waiting for transfers between devices, per_device(): back = lax.all_to_all(parts, 'blk', split_axis=0, concat_axis=0, tiled=True)  29.8 us
    ppermute x13, starting transfers between devices, move(): return lax.ppermute(x, axis, pairs)  23 us
    ppermute x3, waiting for transfers between devices, ring_shift(): return lax.ppermute(x, axis, [(i, (i + by) % count) for i in range(count)])  19.1 us
    pallas_call x1, Pallas kernels, rotate(): pl.pallas_call(rotate_kernel, out_shape=jax.ShapeDtypeStruct((NB, 2 * SHA...  11 us
  transfers between devices with their start and end apart: 18, of which 12 were waited for; matrix products, arithmetic and copies ran while one was open for 9% of the time, Pallas kernels for 38%

profile of v1, /device:TPU:16, one launch (start us, length us, event | category | flops | bytes accessed | tf_op | source)
XLA Modules:
  0.0 493.8 jit_solution(7337774830965742005)
XLA Ops:
  0.6 1.4 collective-permute-start.3
  2.0 2.7 collective-permute-done.3
  5.4 2.8 collective-permute-start.4
  8.3 0.9 collective-permute-start.5
  9.2 0.9 collective-permute-start.6
  10.1 3.8 collective-permute-done.5
  14.9 6.3 %collective-permute-done.7 = bf16[4,2,72,96]{3,2,1,0:T(8,128)(2,1)S(1)} collective-permute-done((bf16[4,2,72,96]{3,2,1,0:T(8,128)(2,1)S(1)}, bf16[4,2,72,96]{3,2,1,0:T(8,128)(2,1)S(1)}, u32[]{:S(2)}, u32[]{:S(2)}) %collective-permute-start.7) | collective-permute-done | bytes 110624 | tf_op jit(solution)/shard_map/ppermute | solution.py:32
  21.3 5.9 %collective-permute-start.8 = (bf16[2,4,2,72,96]{4,3,2,1,0:T(8,128)(2,1)S(1)}, bf16[2,4,2,72,96]{4,3,2,1,0:T(8,128)(2,1)S(1)}, u32[]{:S(2)}, u32[]{:S(2)}) collective-permute-start(bf16[2,4,2,72,96]{4,3,2,1,0:T(8,128)(2,1)S(1)} %pad_maximum_fusion), channel_id=1, source_target_pairs={{0,112},{8,120},{16,0},{24,8},{32,16},{40,24},{48,32},{56,40},{64,... | collective-permute-start | bytes 663560 | tf_op jit(solution)/shard_map/ppermute | solution.py:32
  27.2 180.1 %pack.1 = bf16[8,31,96,128]{3,2,1,0:T(8,128)(2,1)} custom-call(bf16[81,96,128]{2,1,0:T(8,128)(2,1)} %bitcast.70, bf16[81,96,128]{2,1,0:T(8,128)(2,1)} %bitcast.74, bf16[81,96,128]{2,1,0:T(8,128)(2,1)} %bitcast.75), custom_call_target="tpu_custom_call" | custom-call | tf_op jit(solution)/shard_map/pack/pallas_call | solution.py:113
  207.3 4.7 all-to-all-start
  212.2 3.3 collective-permute-start.9
  215.6 6.1 %collective-permute-done.9 = bf16[2,4,2,72,96]{4,3,2,1,0:T(8,128)(2,1)S(1)} collective-permute-done((bf16[2,4,2,72,96]{4,3,2,1,0:T(8,128)(2,1)S(1)}, bf16[2,4,2,72,96]{4,3,2,1,0:T(8,128)(2,1)S(1)}, u32[]{:S(2)}, u32[]{:S(2)}) %collective-permute-start.9) | collective-permute-done | bytes 221216 | tf_op jit(solution)/shard_map/ppermute | solution.py:32
  221.6 3.7 collective-permute-start.10
  225.7 6.6 %collective-permute-done.10 = bf16[2,4,2,72,96]{4,3,2,1,0:T(8,128)(2,1)S(1)} collective-permute-done((bf16[2,4,2,72,96]{4,3,2,1,0:T(8,128)(2,1)S(1)}, bf16[2,4,2,72,96]{4,3,2,1,0:T(8,128)(2,1)S(1)}, u32[]{:S(2)}, u32[]{:S(2)}) %collective-permute-start.10) | collective-permute-done | bytes 221216 | tf_op jit(solution)/shard_map/ppermute | solution.py:32
  232.3 3.7 collective-permute-start.11
  236.0 4.2 collective-permute-done.11
  240.9 2.1 copy-done.1
  243.0 1.6 constant_dynamic-slice_fusion
  244.6 4.7 collective-permute-done.15
  249.4 2.0 select_bitcast_fusion.1
  251.3 3.2 maximum_bitcast_fusion
  254.5 16.1 %copy.16 = bf16[4,2,96,2,8,2,72]{6,5,4,3,2,1,0:T(2,128)(2,1)} copy(bf16[4,2,96,2,8,2,72]{2,6,1,0,3,4,5:T(8,128)(2,1)} %maximum_bitcast_fusion) | data formatting | bytes 7077888 | tf_op jit(solution)/shard_map/reshape | solution.py:64
  270.6 18.9 %reshape.42.coef_ref = bf16[768,2304]{1,0:T(8,128)(2,1)} reshape(bf16[4,2,96,2,8,2,72]{6,5,4,3,2,1,0:T(2,128)(2,1)} %copy.16) | data formatting | bytes 7077888 | tf_op jit(solution)/shard_map/reshape | solution.py:64
  289.5 3.7 all-to-all-done.cells_ref
  293.2 11.0 %rotate.1 = bf16[8,21,96,128]{3,2,1,0:T(8,128)(2,1)} custom-call(bf16[8,31,96,128]{3,2,1,0:T(8,128)(2,1)} %all-to-all-done.cells_ref, bf16[768,2304]{1,0:T(8,128)(2,1)} %reshape.42.coef_ref), custom_call_target="tpu_custom_call" | custom-call | flops 4982833152 | bytes 14000000 | tf_op jit(solution)/shard_map/rotate/pallas_call | solution.py:205
  304.2 4.7 all-to-all-start.1
  309.9 5.3 %collective-permute-start.1 = (bf16[18,96,128]{2,1,0:T(8,128)(2,1)}, bf16[18,96,128]{2,1,0:T(8,128)(2,1)S(1)}, u32[]{:S(2)}, u32[]{:S(2)}) collective-permute-start(bf16[18,96,128]{2,1,0:T(8,128)(2,1)} %bitcast.2), channel_id=1, source_target_pairs={{0,248},{8,0},{16,8},{24,16},{32,24},{40,32},{48,40},{56,48},{64,5... | collective-permute-start | bytes 1327112 | tf_op jit(solution)/shard_map/ppermute | solution.py:37
  316.0 19.1 %collective-permute-done = s32[1,9,128]{2,0,1:T(1,128)S(1)} collective-permute-done((s32[1,9,128]{2,0,1:T(1,128)S(1)}, s32[1,9,128]{2,0,1:T(1,128)S(1)}, u32[]{:S(2)}, u32[]{:S(2)}) %collective-permute-start) | collective-permute-done | bytes 4640 | tf_op jit(solution)/shard_map/ppermute | solution.py:37
  336.5 0.8 copy-done.2
  337.3 6.1 %curls.1 = bf16[81,96,128]{2,1,0:T(8,128)(2,1)} custom-call(f32[4,9]{1,0:T(4,128)} %reshape.33.eps_ref, s32[36,128]{1,0:T(8,128)} %reshape.34.mat_ref, bf16[81,96,128]{2,1,0:T(8,128)(2,1)} %bitcast.71, bf16[18,96,128]{2,1,0:T(8,128)(2,1)} %copy-done.3, bf16[27,96,128]{2,1,0:T(8,128)(2,1)} %copy-done.2), custom_call_target="tpu_custom_call" | custom-call | flops 60000000 | bytes 5000000 | tf_op jit(solution)/shard_map/curls/pallas_call | solution.py:333
  343.4 29.8 %all-to-all-done.1.in_ref = bf16[8,21,96,128]{3,2,1,0:T(8,128)(2,1)} async-done(((bf16[8,21,96,128]{3,2,1,0:T(8,128)(2,1)}), bf16[8,21,96,128]{3,2,1,0:T(8,128)(2,1)}, u32[]{:S(2)}, u32[]{:S(2)}) %all-to-all-start.1) | async-done | bytes 4128800 | tf_op jit(solution)/shard_map/all_to_all | solution.py:376
  373.2 120.5 %unpack.1 = (bf16[81,96,128]{2,1,0:T(8,128)(2,1)}, bf16[81,96,128]{2,1,0:T(8,128)(2,1)}) custom-call(bf16[8,21,96,128]{3,2,1,0:T(8,128)(2,1)} %all-to-all-done.1.in_ref), custom_call_target="tpu_custom_call" | custom-call | tf_op jit(solution)/shard_map/unpack/pallas_call | solution.py:260
  (62 shorter events, 6.1 us)
Async XLA Ops:
  0.6 4.1 collective-permute-start.3
  5.4 4.6 collective-permute-start.4
  8.3 5.5 %collective-permute-start.5 = (bf16[2,72,96]{2,1,0:T(8,128)(2,1)S(1)}, bf16[2,72,96]{2,1,0:T(8,128)(2,1)S(1)}, u32[]{:S(2)}, u32[]{:S(2)}) collective-permute-start(bf16[2,72,96]{2,1,0:T(8,128)(2,1)S(1)} %pad_maximum_fusion.1), channel_id=1, source_target_pairs={{0,4},{1,5},{2,6},{3,7},{4,0},{5,1},{6,2},{7,3},{8,12},{9,13},{10,... | collective-permute-start | bytes 82952 | tf_op jit(solution)/shard_map/ppermute | solution.py:32
  9.2 5.2 %collective-permute-start.6 = (bf16[2,72,96]{2,1,0:T(8,128)(2,1)S(1)}, bf16[2,72,96]{2,1,0:T(8,128)(2,1)S(1)}, u32[]{:S(2)}, u32[]{:S(2)}) collective-permute-start(bf16[2,72,96]{2,1,0:T(8,128)(2,1)S(1)} %pad_maximum_fusion.1), channel_id=1, source_target_pairs={{0,2},{1,3},{2,4},{3,5},{4,6},{5,7},{6,0},{7,1},{8,10},{9,11},{10,... | collective-permute-start | bytes 82952 | tf_op jit(solution)/shard_map/ppermute | solution.py:32
  14.5 6.7 %collective-permute-start.7 = (bf16[4,2,72,96]{3,2,1,0:T(8,128)(2,1)S(1)}, bf16[4,2,72,96]{3,2,1,0:T(8,128)(2,1)S(1)}, u32[]{:S(2)}, u32[]{:S(2)}) collective-permute-start(bf16[4,2,72,96]{3,2,1,0:T(8,128)(2,1)S(1)} %constant_dynamic-slice_fusion.1), channel_id=1, source_target_pairs={{0,128},{8,136},{16,144},{24,152},{32,160},{40,168},{48,176},{56,1... | collective-permute-start | bytes 331784 | tf_op jit(solution)/shard_map/ppermute | solution.py:32
  21.3 190.9 %collective-permute-start.8 = (bf16[2,4,2,72,96]{4,3,2,1,0:T(8,128)(2,1)S(1)}, bf16[2,4,2,72,96]{4,3,2,1,0:T(8,128)(2,1)S(1)}, u32[]{:S(2)}, u32[]{:S(2)}) collective-permute-start(bf16[2,4,2,72,96]{4,3,2,1,0:T(8,128)(2,1)S(1)} %pad_maximum_fusion), channel_id=1, source_target_pairs={{0,112},{8,120},{16,0},{24,8},{32,16},{40,24},{48,32},{56,40},{64,... | collective-permute-start | bytes 663560 | tf_op jit(solution)/shard_map/ppermute | solution.py:32
  27.2 188.3 %collective-permute-start.12 = (bf16[2,4,2,72,96]{4,3,2,1,0:T(8,128)(2,1)S(1)}, bf16[2,4,2,72,96]{4,3,2,1,0:T(8,128)(2,1)S(1)}, u32[]{:S(2)}, u32[]{:S(2)}) collective-permute-start(bf16[2,4,2,72,96]{4,3,2,1,0:T(8,128)(2,1)S(1)} %pad_maximum_fusion), channel_id=1, source_target_pairs={{0,16},{8,24},{16,32},{24,40},{32,48},{40,56},{48,64},{56,72},{64,... | collective-permute-start | bytes 663560 | tf_op jit(solution)/shard_map/ppermute | solution.py:32
  207.3 85.9 %all-to-all-start = ((bf16[8,31,96,128]{3,2,1,0:T(8,128)(2,1)}), bf16[8,31,96,128]{3,2,1,0:T(8,128)(2,1)}, u32[]{:S(2)}, u32[]{:S(2)}) async-start(bf16[8,31,96,128]{3,2,1,0:T(8,128)(2,1)} %pack.1), calls=%async_computation | async-start | bytes 12189696 | tf_op jit(solution)/shard_map/all_to_all | solution.py:373
  212.2 9.4 %collective-permute-start.9 = (bf16[2,4,2,72,96]{4,3,2,1,0:T(8,128)(2,1)S(1)}, bf16[2,4,2,72,96]{4,3,2,1,0:T(8,128)(2,1)S(1)}, u32[]{:S(2)}, u32[]{:S(2)}) collective-permute-start(bf16[2,4,2,72,96]{4,3,2,1,0:T(8,128)(2,1)S(1)} %collective-permute-done.8), channel_id=1, source_target_pairs={{0,112},{8,120},{16,0},{24,8},{32,16},{40,24},{48,32},{56,40},{64,... | collective-permute-start | bytes 663560 | tf_op jit(solution)/shard_map/ppermute | solution.py:32
  215.5 10.1 %collective-permute-start.13 = (bf16[2,4,2,72,96]{4,3,2,1,0:T(8,128)(2,1)S(1)}, bf16[2,4,2,72,96]{4,3,2,1,0:T(8,128)(2,1)S(1)}, u32[]{:S(2)}, u32[]{:S(2)}) collective-permute-start(bf16[2,4,2,72,96]{4,3,2,1,0:T(8,128)(2,1)S(1)} %collective-permute-done.12), channel_id=1, source_target_pairs={{0,16},{8,24},{16,32},{24,40},{32,48},{40,56},{48,64},{56,72},{64,... | collective-permute-start | bytes 663560 | tf_op jit(solution)/shard_map/ppermute | solution.py:32
  221.6 10.6 %collective-permute-start.10 = (bf16[2,4,2,72,96]{4,3,2,1,0:T(8,128)(2,1)S(1)}, bf16[2,4,2,72,96]{4,3,2,1,0:T(8,128)(2,1)S(1)}, u32[]{:S(2)}, u32[]{:S(2)}) collective-permute-start(bf16[2,4,2,72,96]{4,3,2,1,0:T(8,128)(2,1)S(1)} %collective-permute-done.9), channel_id=1, source_target_pairs={{0,112},{8,120},{16,0},{24,8},{32,16},{40,24},{48,32},{56,40},{64,... | collective-permute-start | bytes 663560 | tf_op jit(solution)/shard_map/ppermute | solution.py:32
  225.6 14.6 %collective-permute-start.14 = (bf16[2,4,2,72,96]{4,3,2,1,0:T(8,128)(2,1)S(1)}, bf16[2,4,2,72,96]{4,3,2,1,0:T(8,128)(2,1)S(1)}, u32[]{:S(2)}, u32[]{:S(2)}) collective-permute-start(bf16[2,4,2,72,96]{4,3,2,1,0:T(8,128)(2,1)S(1)} %collective-permute-done.13), channel_id=1, source_target_pairs={{0,16},{8,24},{16,32},{24,40},{32,48},{40,56},{48,64},{56,72},{64,... | collective-permute-start | bytes 663560 | tf_op jit(solution)/shard_map/ppermute | solution.py:32
  232.3 7.9 %collective-permute-start.11 = (bf16[2,4,2,72,96]{4,3,2,1,0:T(8,128)(2,1)S(1)}, bf16[2,4,2,72,96]{4,3,2,1,0:T(8,128)(2,1)S(1)}, u32[]{:S(2)}, u32[]{:S(2)}) collective-permute-start(bf16[2,4,2,72,96]{4,3,2,1,0:T(8,128)(2,1)S(1)} %collective-permute-done.10), channel_id=1, source_target_pairs={{0,112},{8,120},{16,0},{24,8},{32,16},{40,24},{48,32},{56,40},{64,... | collective-permute-start | bytes 663560 | tf_op jit(solution)/shard_map/ppermute | solution.py:32
  240.8 2.1 copy-start.1
  244.6 4.7 collective-permute-start.15
  304.2 4.7 copy-start
  304.2 11.0 %copy-start.4 = (s32[3,9,128]{2,0,1:T(4,128)S(1)}, s32[3,9,128]{2,0,1:T(4,128)}, u32[]{:S(2)}) copy-start(s32[3,9,128]{2,0,1:T(4,128)} %param.10) | copy-start | bytes 41476
  304.2 11.1 %copy-start.5 = (f32[4,3,3]{2,0,1:T(4,128)S(1)}, f32[4,3,3]{2,0,1:T(4,128)}, u32[]{:S(2)}) copy-start(f32[4,3,3]{2,0,1:T(4,128)} %param.11) | copy-start | bytes 436
  304.2 68.9 %all-to-all-start.1 = ((bf16[8,21,96,128]{3,2,1,0:T(8,128)(2,1)}), bf16[8,21,96,128]{3,2,1,0:T(8,128)(2,1)}, u32[]{:S(2)}, u32[]{:S(2)}) async-start(bf16[8,21,96,128]{3,2,1,0:T(8,128)(2,1)} %rotate.1), calls=%async_computation.1 | async-start | bytes 8257536 | tf_op jit(solution)/shard_map/all_to_all | solution.py:376
  309.0 26.7 %collective-permute-start.2 = (bf16[27,96,128]{2,1,0:T(8,128)(2,1)S(1)}, bf16[27,96,128]{2,1,0:T(8,128)(2,1)S(1)}, u32[]{:S(2)}, u32[]{:S(2)}) collective-permute-start(bf16[27,96,128]{2,1,0:T(8,128)(2,1)S(1)} %bitcast.77), channel_id=1, source_target_pairs={{0,8},{8,16},{16,24},{24,32},{32,40},{40,48},{48,56},{56,64},{64,7... | collective-permute-start | bytes 1990664 | tf_op jit(solution)/shard_map/ppermute | solution.py:37
  309.9 25.8 %collective-permute-start.1 = (bf16[18,96,128]{2,1,0:T(8,128)(2,1)}, bf16[18,96,128]{2,1,0:T(8,128)(2,1)S(1)}, u32[]{:S(2)}, u32[]{:S(2)}) collective-permute-start(bf16[18,96,128]{2,1,0:T(8,128)(2,1)} %bitcast.2), channel_id=1, source_target_pairs={{0,248},{8,0},{16,8},{24,16},{32,24},{40,32},{48,40},{56,48},{64,5... | collective-permute-start | bytes 1327112 | tf_op jit(solution)/shard_map/ppermute | solution.py:37
  315.2 19.8 %collective-permute-start = (s32[1,9,128]{2,0,1:T(1,128)S(1)}, s32[1,9,128]{2,0,1:T(1,128)S(1)}, u32[]{:S(2)}, u32[]{:S(2)}) collective-permute-start(s32[1,9,128]{2,0,1:T(1,128)S(1)} %slice.9), channel_id=1, source_target_pairs={{0,8},{8,16},{16,24},{24,32},{32,40},{40,48},{48,56},{56,64},{64,7... | collective-permute-start | bytes 13832 | tf_op jit(solution)/shard_map/ppermute | solution.py:37
  335.7 0.8 copy-start.3
  336.5 0.8 copy-start.2

commit v2 on v1

--- a/solution.py
+++ b/solution.py
@@ -37,31 +37,68 @@
     return lax.ppermute(x, axis, [(i, (i + by) % count) for i in range(count)])
 
 
-def in_order(parts, me):
-    count = len(parts)
-    if count == 2:
-        first = jnp.where(me == 0, parts[0], parts[1])
-        second = jnp.where(me == 0, parts[1], parts[0])
-        return jnp.stack([first, second])
-    twice = jnp.stack(parts + parts)
-    return lax.dynamic_slice_in_dim(twice, (count - me) % count, count, 0)
-
-
-def gather_coefficients(tile):
+def gather_plane(tile):
+    pieces = [tile]
+    pieces.append(move(tile, "blk", BLK, (0, 1)))
+    pieces.append(move(tile, "slab", SLAB, (1, 0, 0)))
+    pieces.append(
+        lax.ppermute(
+            tile,
+            ("slab", "blk"),
+            [
+                (s * NB + b, (s + 16) % 32 * NB + (b ^ 1))
+                for s in range(32)
+                for b in range(NB)
+            ],
+        )
+    )
+    t = jnp.stack(pieces)
+    return jnp.stack([t] + [move(t, "blk", BLK, (-k, 0)) for k in (1, 2, 3)])
+
+
+def gather_coefficients(plane):
     slab, blk = lax.axis_index("slab"), lax.axis_index("blk")
-    y_hi, z, core = slab // 16, (slab // 2) % 8, slab % 2
-    x, y_lo = blk // 2, blk % 2
-    t = in_order([tile, move(tile, "blk", BLK, (0, 1))], y_lo)
-    t = in_order([t] + [move(t, "blk", BLK, (-k, 0)) for k in (1, 2, 3)], x)
-    t = in_order([t, move(t, "slab", SLAB, (1, 0, 0))], y_hi)
-    got = {0: t}
-    for k in (1, 2, 3, 4):
-        got[k] = move(got[k - 1], "slab", SLAB, (0, -1, 0))
-        if k < 4:
-            got[-k] = move(got[1 - k], "slab", SLAB, (0, 1, 0))
-    t = in_order([got[k if k <= 4 else k - 8] for k in range(8)], z)
-    t = in_order([t, move(t, "slab", SLAB, (0, 0, 1))], core)
-    return t.transpose(3, 4, 6, 2, 1, 0, 5).reshape(M, 3 * M)
+    place = jnp.stack([slab // 16, (slab // 2) % 8, slab % 2, blk // 2, blk % 2])
+    groups = [[h * 16 + z * 2 + c for z in range(8)] for h in range(2) for c in range(2)]
+    mine = lax.all_gather(plane, "slab", axis_index_groups=groups)
+    other = move(mine, "slab", SLAB, (0, 0, 1))
+    return assemble(place, mine, other)
+
+
+def assemble_kernel(place_ref, mine_ref, other_ref, out_ref):
+    here, core = place_ref[0], place_ref[2]
+    tiles = []
+    for y_hi in range(2):
+        k = (y_hi - here + 2) % 2
+        for z in range(8):
+            own = mine_ref[z, 0, k, 0].astype(jnp.float32)
+            far = other_ref[z, 0, k, 0].astype(jnp.float32)
+            tiles.append(jnp.where(core == 0, own, far))
+            tiles.append(jnp.where(core == 0, far, own))
+    out_ref[...] = jnp.concatenate(tiles, axis=0).T.astype(jnp.bfloat16)
+
+
+def assemble(place, mine, other):
+    def piece(b, at):
+        return 0, (b // 2 - at[3] + 4) % 4, 0, (b % 2 - at[4] + 2) % 2, 0, 0
+
+    mine, other = (t.reshape(8, 4, 2, 2, 72, 96) for t in (mine, other))
+    pieces = pl.BlockSpec((8, 1, 2, 1, 72, 96), piece)
+    return pl.pallas_call(
+        assemble_kernel,
+        out_shape=jax.ShapeDtypeStruct((M, 3 * M), jnp.bfloat16),
+        grid_spec=pltpu.PrefetchScalarGridSpec(
+            num_scalar_prefetch=1,
+            grid=(NB,),
+            in_specs=[pieces, pieces],
+            out_specs=pl.BlockSpec((M // NB, 3 * M), lambda b, at: (b, 0)),
+        ),
+        compiler_params=pltpu.CompilerParams(vmem_limit_bytes=VMEM_LIMIT),
+        cost_estimate=pl.CostEstimate(
+            flops=10_000_000, bytes_accessed=8_000_000, transcendentals=0
+        ),
+        name="assemble",
+    )(place, mine, other)
 
 
 def lane_index(shape):
@@ -73,56 +110,66 @@
     return x if by == 0 else pltpu.roll(x, by, x.ndim - 1)
 
 
-def pack_kernel(w_ref, p_ref, x_ref, out_ref, tail, mixed, sems, tail_sems, out_sems):
+def pack_kernel(w_ref, p_ref, x_ref, out_ref, stage, tail, in_sems, tail_sems, out_sems):
     fields = (w_ref, p_ref, x_ref)
-    copies = []
-    for d in range(NB):
-        for k, ref in enumerate(fields):
-            copies.append(
-                pltpu.make_async_copy(
-                    ref.at[pl.ds(SHARE * d, SHARE)],
-                    out_ref.at[d, pl.ds(SHARE * k, SHARE)],
-                    sems.at[3 * d + k],
-                )
-            )
     last = [
         pltpu.make_async_copy(ref.at[ROWS - 1], tail.at[k], tail_sems.at[k])
         for k, ref in enumerate(fields)
     ]
-    for c in last + copies:
+    fetches = [
+        [
+            pltpu.make_async_copy(
+                ref.at[pl.ds(SHARE * d, SHARE)],
+                stage.at[d, pl.ds(SHARE * k, SHARE)],
+                in_sems.at[d, k],
+            )
+            for k, ref in enumerate(fields)
+        ]
+        for d in range(NB)
+    ]
+    sends = [
+        pltpu.make_async_copy(stage.at[d], out_ref.at[d], out_sems.at[d])
+        for d in range(NB)
+    ]
+    for c in last:
         c.start()
+    for group in fetches:
+        for c in group:
+            c.start()
     for c in last:
         c.wait()
     lane = lane_index((V, 128))
     w, p, x = (tail[k].astype(jnp.float32) for k in range(3))
-    sends = []
     for d in range(NB):
         row = jnp.where(lane < 3 * LANES, rolled(x, LANES * (2 - d)), 0.0)
         row = jnp.where(lane < 2 * LANES, rolled(p, LANES * (1 - d)), row)
         row = jnp.where(lane < LANES, rolled(w, LANES * (0 - d)), row)
-        mixed[d] = row.astype(jnp.bfloat16)
-        sends.append(
-            pltpu.make_async_copy(mixed.at[d], out_ref.at[d, 3 * SHARE], out_sems.at[d])
-        )
-        sends[-1].start()
-    for c in copies + sends:
+        stage[d, 3 * SHARE] = row.astype(jnp.bfloat16)
+        for c in fetches[d]:
+            c.wait()
+        sends[d].start()
+    for c in sends:
         c.wait()
 
 
 def pack(w, p, x):
+    shape = (NB, 3 * SHARE + 1, V, 128)
     return pl.pallas_call(
         pack_kernel,
-        out_shape=jax.ShapeDtypeStruct((NB, 3 * SHARE + 1, V, 128), jnp.bfloat16),
+        out_shape=jax.ShapeDtypeStruct(shape, jnp.bfloat16),
         in_specs=[ANY] * 3,
         out_specs=ANY,
         scratch_shapes=[
+            pltpu.VMEM(shape, jnp.bfloat16),
             pltpu.VMEM((3, V, 128), jnp.bfloat16),
-            pltpu.VMEM((NB, V, 128), jnp.bfloat16),
-            pltpu.SemaphoreType.DMA((3 * NB,)),
+            pltpu.SemaphoreType.DMA((NB, 3)),
             pltpu.SemaphoreType.DMA((3,)),
             pltpu.SemaphoreType.DMA((NB,)),
         ],
         compiler_params=pltpu.CompilerParams(vmem_limit_bytes=VMEM_LIMIT),
+        cost_estimate=pl.CostEstimate(
+            flops=2_000_000, bytes_accessed=12_000_000, transcendentals=0
+        ),
         name="pack",
     )(w, p, x)
 
@@ -221,31 +268,42 @@
     )(cells, coef)
 
 
-def unpack_kernel(in_ref, d_ref, r_ref, tail, last, sems, tail_sems, last_sems):
-    copies = []
-    for s in range(NB):
-        for k, ref in enumerate((d_ref, r_ref)):
-            copies.append(
-                pltpu.make_async_copy(
-                    in_ref.at[s, pl.ds(SHARE * k, SHARE)],
-                    ref.at[pl.ds(SHARE * s, SHARE)],
-                    sems.at[2 * s + k],
-                )
-            )
+def unpack_kernel(in_ref, d_ref, r_ref, stage, last, in_sems, tail_sems, out_sems, last_sems):
     tails = [
-        pltpu.make_async_copy(in_ref.at[s, 2 * SHARE], tail.at[s], tail_sems.at[s])
+        pltpu.make_async_copy(
+            in_ref.at[s, 2 * SHARE], stage.at[s, 2 * SHARE], tail_sems.at[s]
+        )
         for s in range(NB)
     ]
-    for c in tails + copies:
+    fetches = [
+        pltpu.make_async_copy(
+            in_ref.at[s, pl.ds(0, 2 * SHARE)],
+            stage.at[s, pl.ds(0, 2 * SHARE)],
+            in_sems.at[s],
+        )
+        for s in range(NB)
+    ]
+    for c in tails + fetches:
         c.start()
     for c in tails:
         c.wait()
     which = lane_index((V, 128)) // LANES
     direction = rotated = jnp.zeros((V, 128), jnp.float32)
+    copies = []
     for s in range(NB):
-        row = tail[s].astype(jnp.float32)
+        row = stage[s, 2 * SHARE].astype(jnp.float32)
         direction = jnp.where(which == s, rolled(row, LANES * s), direction)
         rotated = jnp.where(which == s, rolled(row, LANES * (s - 1)), rotated)
+        fetches[s].wait()
+        for k, ref in enumerate((d_ref, r_ref)):
+            copies.append(
+                pltpu.make_async_copy(
+                    stage.at[s, pl.ds(SHARE * k, SHARE)],
+                    ref.at[pl.ds(SHARE * s, SHARE)],
+                    out_sems.at[s, k],
+                )
+            )
+            copies[-1].start()
     last[0] = direction.astype(jnp.bfloat16)
     last[1] = rotated.astype(jnp.bfloat16)
     for k, ref in enumerate((d_ref, r_ref)):
@@ -263,10 +321,11 @@
         in_specs=[ANY],
         out_specs=(ANY, ANY),
         scratch_shapes=[
-            pltpu.VMEM((NB, V, 128), jnp.bfloat16),
+            pltpu.VMEM((NB, 2 * SHARE + 1, V, 128), jnp.bfloat16),
             pltpu.VMEM((2, V, 128), jnp.bfloat16),
-            pltpu.SemaphoreType.DMA((2 * NB,)),
             pltpu.SemaphoreType.DMA((NB,)),
+            pltpu.SemaphoreType.DMA((NB,)),
+            pltpu.SemaphoreType.DMA((NB, 2)),
             pltpu.SemaphoreType.DMA((2,)),
         ],
         compiler_params=pltpu.CompilerParams(vmem_limit_bytes=VMEM_LIMIT),
@@ -364,14 +423,18 @@
 
 def per_device(current, search, previous, coefficients, material, inverse_permittivity):
     w, p, x = as_rows(search), as_rows(previous), as_rows(current)
+    packed = pack(w, p, x)
+    plane = gather_plane(coefficients)
+    packed, plane = lax.optimization_barrier((packed, plane))
+    cells = lax.all_to_all(packed, "blk", split_axis=0, concat_axis=0, tiled=True)
     layers = w.reshape(3, NZ, NY, V, 128)
     above = ring_shift(layers[:2, 0].reshape(2 * NY, V, 128), "slab", -1)
     below = ring_shift(layers[:, NZ - 1].reshape(3 * NY, V, 128), "slab", 1)
     mark_below = ring_shift(material[NZ - 1 :], "slab", 1)
+    plane, below, mark_below = lax.optimization_barrier((plane, below, mark_below))
     marks = jnp.concatenate([mark_below, material]).reshape((NZ + 1) * NY, 128)
-    packed = pack(w, p, x)
-    cells = lax.all_to_all(packed, "blk", split_axis=0, concat_axis=0, tiled=True)
-    coef = gather_coefficients(coefficients)
+    coef = gather_coefficients(plane)
+    coef, above = lax.optimization_barrier((coef, above))
     parts = rotate(cells, coef)
     back = lax.all_to_all(parts, "blk", split_axis=0, concat_axis=0, tiled=True)
     applied = apply_curls(w, above, below, marks, inverse_permittivity.reshape(NMAT, 9))

time: 495 us -> 205 us (0.41)
  the two profiles are of different devices: /device:TPU:16 before, /device:TPU:224 now
where the time goes in v2:
time: 205 us; the launch traced here: 204 us
  waiting for transfers between devices  129 us (63%)
  Pallas kernels  34.1 us (17%)
  starting transfers between devices  20.1 us (10%)
  between operations  14.2 us (7%)
  local copies, waits for them, and re-layouts  5.47 us (3%)
    all_to_all x1, waiting for transfers between devices, per_device(): back = lax.all_to_all(parts, 'blk', split_axis=0, concat_axis=0, tiled=True)  49.6 us
    all_gather x1, waiting for transfers between devices, gather_coefficients(): mine = lax.all_gather(plane, 'slab', axis_index_groups=groups)  41 us
    all_to_all x1, waiting for transfers between devices, per_device(): lax.all_to_all(packed, 'blk', split_axis=0, concat_axis=0, tiled=True)  29.1 us
    pallas_call x1, Pallas kernels, rotate(): pl.pallas_call(rotate_kernel, out_shape=jax.ShapeDtypeStruct((NB, 2 * SHA...  11 us
    pallas_call x1, Pallas kernels, assemble(): pl.pallas_call(assemble_kernel, out_shape=jax.ShapeDtypeStruct((M, 3 * M)...  7.93 us
    ppermute x6, starting transfers between devices, move(): return lax.ppermute(x, axis, pairs)  7.52 us
    pallas_call x1, Pallas kernels, apply_curls(): pl.pallas_call(curl_kernel, out_shape=jax.ShapeDtypeStruct((ROWS, V, 128)...  6.05 us
    pallas_call x1, Pallas kernels, pack(): pl.pallas_call(pack_kernel, out_shape=jax.ShapeDtypeStruct(shape, jnp.bfl...  5.56 us
  transfers between devices with their start and end apart: 13, of which 7 were waited for; matrix products, arithmetic and copies ran while one was open for 3% of the time, Pallas kernels for 10%

profile of v2, /device:TPU:224, one launch (start us, length us, event | category | flops | bytes accessed | tf_op | source)
XLA Modules:
  0.0 204.0 jit_solution(1909086244748770815)
XLA Ops:
  7.2 1.7 collective-permute-start
  8.8 2.2 %collective-permute-start.2 = (bf16[72,96]{1,0:T(8,128)(2,1)}, bf16[72,96]{1,0:T(8,128)(2,1)S(1)}, u32[]{:S(2)}, u32[]{:S(2)}) collective-permute-start(bf16[72,96]{1,0:T(8,128)(2,1)} %param.9), channel_id=1, source_target_pairs={{0,129},{1,128},{2,131},{3,130},{4,133},{5,132},{6,135},{7,134},{8... | collective-permute-start | bytes 41480 | tf_op jit(solution)/shard_map/ppermute | solution.py:45
  11.0 0.7 collective-permute-start.1
  11.7 1.1 slice.12
  12.9 0.1 collective-permute-start.6
  13.0 1.0 collective-permute-done.2
  14.0 2.5 %collective-permute-done.1 = bf16[72,96]{1,0:T(8,128)(2,1)S(1)} collective-permute-done((bf16[72,96]{1,0:T(8,128)(2,1)}, bf16[72,96]{1,0:T(8,128)(2,1)S(1)}, u32[]{:S(2)}, u32[]{:S(2)}) %collective-permute-start.1) | collective-permute-done | bytes 13856 | tf_op jit(solution)/shard_map/ppermute | solution.py:32
  16.5 0.7 fusion
  17.2 3.1 %collective-permute-start.4 = (bf16[4,72,96]{2,1,0:T(8,128)(2,1)S(1)}, bf16[4,72,96]{2,1,0:T(8,128)(2,1)S(1)}, u32[]{:S(2)}, u32[]{:S(2)}) collective-permute-start(bf16[4,72,96]{2,1,0:T(8,128)(2,1)S(1)} %get-tuple-element.22), channel_id=1, source_target_pairs={{0,4},{1,5},{2,6},{3,7},{4,0},{5,1},{6,2},{7,3},{8,12},{9,13},{10,... | collective-permute-start | bytes 165896 | tf_op jit(solution)/shard_map/ppermute | solution.py:32
  20.3 1.1 collective-permute-start.3
  21.5 0.9 collective-permute-start.5
  22.4 5.6 %pack.1 = bf16[8,31,96,128]{3,2,1,0:T(8,128)(2,1)} custom-call(bf16[81,96,128]{2,1,0:T(8,128)(2,1)} %bitcast.38, bf16[81,96,128]{2,1,0:T(8,128)(2,1)} %bitcast.44, bf16[81,96,128]{2,1,0:T(8,128)(2,1)} %bitcast.45), custom_call_target="tpu_custom_call" | custom-call | flops 2000000 | bytes 12000000 | tf_op jit(solution)/shard_map/pack/pallas_call | solution.py:157
  28.0 0.8 pad_maximum_fusion
  28.8 4.9 %all-to-all-start = ((bf16[8,31,96,128]{3,2,1,0:T(8,128)(2,1)}), bf16[8,31,96,128]{3,2,1,0:T(8,128)(2,1)}, u32[]{:S(2)}, u32[]{:S(2)}) async-start(bf16[8,31,96,128]{3,2,1,0:T(8,128)(2,1)} %pack.1), calls=%async_computation | async-start | bytes 12189696 | tf_op jit(solution)/shard_map/all_to_all | solution.py:429
  33.6 0.0 all-gather.3.cloned.1.call-start
  33.7 0.1 collective-permute-start.7
  33.8 3.0 %collective-permute-done.7 = s32[1,9,128]{2,0,1:T(1,128)S(1)} collective-permute-done((s32[1,9,128]{2,0,1:T(1,128)S(1)}, s32[1,9,128]{2,0,1:T(1,128)S(1)}, u32[]{:S(2)}, u32[]{:S(2)}) %collective-permute-start.7) | collective-permute-done | bytes 4640 | tf_op jit(solution)/shard_map/ppermute | solution.py:37
  36.8 41.0 %all-gather.3.cloned.1.call-done = bf16[32,4,72,96]{3,2,1,0:T(8,128)(2,1)} async-done(((bf16[4,4,72,96]{3,2,1,0:T(8,128)(2,1)}), bf16[32,4,72,96]{3,2,1,0:T(8,128)(2,1)}) %all-gather.3.cloned.1.call-update) | async-done | bytes 1769488 | tf_op jit(solution)/shard_map/all_gather | solution.py:63
  77.9 1.0 slice.13
  78.9 0.8 collective-permute-start.9
  79.7 0.6 stack.63.place_ref
  80.3 2.3 %collective-permute-done.8 = bf16[8,4,4,72,96]{4,3,2,1,0:T(8,128)(2,1)S(1)} collective-permute-done((bf16[8,4,4,72,96]{4,3,2,1,0:T(8,128)(2,1)}, bf16[8,4,4,72,96]{4,3,2,1,0:T(8,128)(2,1)S(1)}, u32[]{:S(2)}, u32[]{:S(2)}) %collective-permute-start.8) | collective-permute-done | bytes 1769504 | tf_op jit(solution)/shard_map/ppermute | solution.py:32
  82.6 1.4 copy-done
  84.0 7.9 %assemble.1.coef_ref = bf16[768,2304]{1,0:T(8,128)(2,1)} custom-call(s32[5]{0:T(128)} %stack.63.place_ref, bf16[8,4,2,2,72,96]{5,4,3,2,1,0:T(8,128)(2,1)} %bitcast.42, bf16[8,4,2,2,72,96]{5,4,3,2,1,0:T(8,128)(2,1)} %bitcast.43), custom_call_target="tpu_custom_call" | custom-call | flops 10000000 | bytes 8000000 | tf_op jit(solution)/shard_map/assemble/pallas_call | solution.py:87
  91.9 29.1 %all-to-all-done.cells_ref = bf16[8,31,96,128]{3,2,1,0:T(8,128)(2,1)} async-done(((bf16[8,31,96,128]{3,2,1,0:T(8,128)(2,1)}), bf16[8,31,96,128]{3,2,1,0:T(8,128)(2,1)}, u32[]{:S(2)}, u32[]{:S(2)}) %all-to-all-start) | async-done | bytes 6094880 | tf_op jit(solution)/shard_map/all_to_all | solution.py:429
  121.0 11.0 %rotate.1 = bf16[8,21,96,128]{3,2,1,0:T(8,128)(2,1)} custom-call(bf16[8,31,96,128]{3,2,1,0:T(8,128)(2,1)} %all-to-all-done.cells_ref, bf16[768,2304]{1,0:T(8,128)(2,1)} %assemble.1.coef_ref), custom_call_target="tpu_custom_call" | custom-call | flops 4982833152 | bytes 14000000 | tf_op jit(solution)/shard_map/rotate/pallas_call | solution.py:252
  132.0 4.6 %all-to-all-start.1 = ((bf16[8,21,96,128]{3,2,1,0:T(8,128)(2,1)}), bf16[8,21,96,128]{3,2,1,0:T(8,128)(2,1)}, u32[]{:S(2)}, u32[]{:S(2)}) async-start(bf16[8,21,96,128]{3,2,1,0:T(8,128)(2,1)} %rotate.1), calls=%async_computation.1 | async-start | bytes 8257536 | tf_op jit(solution)/shard_map/all_to_all | solution.py:439
  136.6 0.7 reshape.36.eps_ref
  137.3 0.6 reshape.40.mat_ref
  137.9 6.1 %curls.1 = bf16[81,96,128]{2,1,0:T(8,128)(2,1)} custom-call(f32[4,9]{1,0:T(4,128)} %reshape.36.eps_ref, s32[36,128]{1,0:T(8,128)} %reshape.40.mat_ref, bf16[81,96,128]{2,1,0:T(8,128)(2,1)} %bitcast.40, bf16[18,96,128]{2,1,0:T(8,128)(2,1)} %collective-permute-done.9.above_ref, bf16[27,96,128]{2,1,0:T(8,128)(2,1)} %copy-done.1), custom_call_target="tpu_custom_call" | custom-call | flops 60000000 | bytes 5000000 | tf_op jit(solution)/shard_map/curls/pallas_call | solution.py:392
  143.9 49.6 %all-to-all-done.1.in_ref = bf16[8,21,96,128]{3,2,1,0:T(8,128)(2,1)} async-done(((bf16[8,21,96,128]{3,2,1,0:T(8,128)(2,1)}), bf16[8,21,96,128]{3,2,1,0:T(8,128)(2,1)}, u32[]{:S(2)}, u32[]{:S(2)}) %all-to-all-start.1) | async-done | bytes 4128800 | tf_op jit(solution)/shard_map/all_to_all | solution.py:439
  193.5 3.6 %unpack.1 = (bf16[81,96,128]{2,1,0:T(8,128)(2,1)}, bf16[81,96,128]{2,1,0:T(8,128)(2,1)}) custom-call(bf16[8,21,96,128]{3,2,1,0:T(8,128)(2,1)} %all-to-all-done.1.in_ref), custom_call_target="tpu_custom_call" | custom-call | tf_op jit(solution)/shard_map/unpack/pallas_call | solution.py:318
  (19 shorter events, 0.1 us)
Async XLA Ops:
  7.2 5.8 %collective-permute-start = (bf16[72,96]{1,0:T(8,128)(2,1)}, bf16[72,96]{1,0:T(8,128)(2,1)S(1)}, u32[]{:S(2)}, u32[]{:S(2)}) collective-permute-start(bf16[72,96]{1,0:T(8,128)(2,1)} %param.9), channel_id=1, source_target_pairs={{0,1},{1,0},{2,3},{3,2},{4,5},{5,4},{6,7},{7,6},{8,9},{9,8},{10,11... | collective-permute-start | bytes 41480 | tf_op jit(solution)/shard_map/ppermute | solution.py:32
  8.8 5.2 %collective-permute-start.2 = (bf16[72,96]{1,0:T(8,128)(2,1)}, bf16[72,96]{1,0:T(8,128)(2,1)S(1)}, u32[]{:S(2)}, u32[]{:S(2)}) collective-permute-start(bf16[72,96]{1,0:T(8,128)(2,1)} %param.9), channel_id=1, source_target_pairs={{0,129},{1,128},{2,131},{3,130},{4,133},{5,132},{6,135},{7,134},{8... | collective-permute-start | bytes 41480 | tf_op jit(solution)/shard_map/ppermute | solution.py:45
  11.0 5.5 %collective-permute-start.1 = (bf16[72,96]{1,0:T(8,128)(2,1)}, bf16[72,96]{1,0:T(8,128)(2,1)S(1)}, u32[]{:S(2)}, u32[]{:S(2)}) collective-permute-start(bf16[72,96]{1,0:T(8,128)(2,1)} %param.9), channel_id=1, source_target_pairs={{0,128},{8,136},{16,144},{24,152},{32,160},{40,168},{48,176},{56,1... | collective-permute-start | bytes 41480 | tf_op jit(solution)/shard_map/ppermute | solution.py:32
  12.9 24.0 %collective-permute-start.6 = (bf16[27,96,128]{2,1,0:T(8,128)(2,1)S(1)}, bf16[27,96,128]{2,1,0:T(8,128)(2,1)S(1)}, u32[]{:S(2)}, u32[]{:S(2)}) collective-permute-start(bf16[27,96,128]{2,1,0:T(8,128)(2,1)S(1)} %bitcast.47), channel_id=1, source_target_pairs={{0,8},{8,16},{16,24},{24,32},{32,40},{40,48},{48,56},{56,64},{64,7... | collective-permute-start | bytes 1990664 | tf_op jit(solution)/shard_map/ppermute | solution.py:37
  17.2 10.7 %collective-permute-start.4 = (bf16[4,72,96]{2,1,0:T(8,128)(2,1)S(1)}, bf16[4,72,96]{2,1,0:T(8,128)(2,1)S(1)}, u32[]{:S(2)}, u32[]{:S(2)}) collective-permute-start(bf16[4,72,96]{2,1,0:T(8,128)(2,1)S(1)} %get-tuple-element.22), channel_id=1, source_target_pairs={{0,4},{1,5},{2,6},{3,7},{4,0},{5,1},{6,2},{7,3},{8,12},{9,13},{10,... | collective-permute-start | bytes 165896 | tf_op jit(solution)/shard_map/ppermute | solution.py:32
  20.3 7.6 %collective-permute-start.3 = (bf16[4,72,96]{2,1,0:T(8,128)(2,1)S(1)}, bf16[4,72,96]{2,1,0:T(8,128)(2,1)S(1)}, u32[]{:S(2)}, u32[]{:S(2)}) collective-permute-start(bf16[4,72,96]{2,1,0:T(8,128)(2,1)S(1)} %get-tuple-element.22), channel_id=1, source_target_pairs={{0,6},{1,7},{2,0},{3,1},{4,2},{5,3},{6,4},{7,5},{8,14},{9,15},{10,... | collective-permute-start | bytes 165896 | tf_op jit(solution)/shard_map/ppermute | solution.py:32
  21.5 6.5 %collective-permute-start.5 = (bf16[4,72,96]{2,1,0:T(8,128)(2,1)S(1)}, bf16[4,72,96]{2,1,0:T(8,128)(2,1)S(1)}, u32[]{:S(2)}, u32[]{:S(2)}) collective-permute-start(bf16[4,72,96]{2,1,0:T(8,128)(2,1)S(1)} %get-tuple-element.22), channel_id=1, source_target_pairs={{0,2},{1,3},{2,4},{3,5},{4,6},{5,7},{6,0},{7,1},{8,10},{9,11},{10,... | collective-permute-start | bytes 165896 | tf_op jit(solution)/shard_map/ppermute | solution.py:32
  28.8 4.9 %copy-start.2 = (s32[3,9,128]{2,0,1:T(4,128)S(1)}, s32[3,9,128]{2,0,1:T(4,128)}, u32[]{:S(2)}) copy-start(s32[3,9,128]{2,0,1:T(4,128)} %param.10) | copy-start | bytes 41476
  28.8 92.3 %all-to-all-start = ((bf16[8,31,96,128]{3,2,1,0:T(8,128)(2,1)}), bf16[8,31,96,128]{3,2,1,0:T(8,128)(2,1)}, u32[]{:S(2)}, u32[]{:S(2)}) async-start(bf16[8,31,96,128]{3,2,1,0:T(8,128)(2,1)} %pack.1), calls=%async_computation | async-start | bytes 12189696 | tf_op jit(solution)/shard_map/all_to_all | solution.py:429
  33.6 44.2 %all-gather.3.cloned.1.call-start = ((), (), s32[]{:S(2)}) async-start(), calls=%async_computation.2 | async-start | bytes 2654208 | tf_op jit(solution)/shard_map/all_gather | solution.py:63
  33.7 3.1 %collective-permute-start.7 = (s32[1,9,128]{2,0,1:T(1,128)S(1)}, s32[1,9,128]{2,0,1:T(1,128)S(1)}, u32[]{:S(2)}, u32[]{:S(2)}) collective-permute-start(s32[1,9,128]{2,0,1:T(1,128)S(1)} %slice.10), channel_id=1, source_target_pairs={{0,8},{8,16},{16,24},{24,32},{32,40},{40,48},{48,56},{56,64},{64,7... | collective-permute-start | bytes 13832 | tf_op jit(solution)/shard_map/ppermute | solution.py:37
  36.8 55.1 %copy-start.1 = (bf16[27,96,128]{2,1,0:T(8,128)(2,1)}, bf16[27,96,128]{2,1,0:T(8,128)(2,1)S(1)}, u32[]{:S(2)}) copy-start(bf16[27,96,128]{2,1,0:T(8,128)(2,1)S(1)} %collective-permute-done.6.below_ref) | copy-start | bytes 1990660
  77.9 4.7 %collective-permute-start.8 = (bf16[8,4,4,72,96]{4,3,2,1,0:T(8,128)(2,1)}, bf16[8,4,4,72,96]{4,3,2,1,0:T(8,128)(2,1)S(1)}, u32[]{:S(2)}, u32[]{:S(2)}) collective-permute-start(bf16[8,4,4,72,96]{4,3,2,1,0:T(8,128)(2,1)} %bitcast.41), channel_id=1, source_target_pairs={{0,8},{8,0},{16,24},{24,16},{32,40},{40,32},{48,56},{56,48},{64,72... | collective-permute-start | bytes 5308424 | tf_op jit(solution)/shard_map/ppermute | solution.py:32
  78.9 13.0 %collective-permute-start.9 = (bf16[18,96,128]{2,1,0:T(8,128)(2,1)S(1)}, bf16[18,96,128]{2,1,0:T(8,128)(2,1)}, u32[]{:S(2)}, u32[]{:S(2)}) collective-permute-start(bf16[18,96,128]{2,1,0:T(8,128)(2,1)S(1)} %bitcast.48), channel_id=1, source_target_pairs={{0,248},{8,0},{16,8},{24,16},{32,24},{40,32},{48,40},{56,48},{64,5... | collective-permute-start | bytes 1327112 | tf_op jit(solution)/shard_map/ppermute | solution.py:37
  82.6 1.4 copy-start
  132.0 4.6 %copy-start.3 = (f32[4,3,3]{2,0,1:T(4,128)S(1)}, f32[4,3,3]{2,0,1:T(4,128)}, u32[]{:S(2)}) copy-start(f32[4,3,3]{2,0,1:T(4,128)} %param.11) | copy-start | bytes 436
  132.0 61.5 %all-to-all-start.1 = ((bf16[8,21,96,128]{3,2,1,0:T(8,128)(2,1)}), bf16[8,21,96,128]{3,2,1,0:T(8,128)(2,1)}, u32[]{:S(2)}, u32[]{:S(2)}) async-start(bf16[8,21,96,128]{3,2,1,0:T(8,128)(2,1)} %rotate.1), calls=%async_computation.1 | async-start | bytes 8257536 | tf_op jit(solution)/shard_map/all_to_all | solution.py:439
Sparse Core Ops, SparseCore 0:
  37.0 40.8 all-gather.2

commit v3 on v2

--- a/solution.py
+++ b/solution.py
@@ -54,15 +54,6 @@
     )
     t = jnp.stack(pieces)
     return jnp.stack([t] + [move(t, "blk", BLK, (-k, 0)) for k in (1, 2, 3)])
-
-
-def gather_coefficients(plane):
-    slab, blk = lax.axis_index("slab"), lax.axis_index("blk")
-    place = jnp.stack([slab // 16, (slab // 2) % 8, slab % 2, blk // 2, blk % 2])
-    groups = [[h * 16 + z * 2 + c for z in range(8)] for h in range(2) for c in range(2)]
-    mine = lax.all_gather(plane, "slab", axis_index_groups=groups)
-    other = move(mine, "slab", SLAB, (0, 0, 1))
-    return assemble(place, mine, other)
 
 
 def assemble_kernel(place_ref, mine_ref, other_ref, out_ref):
@@ -174,7 +165,9 @@
     )(w, p, x)
 
 
-def rotate_kernel(cells_ref, coef_ref, out_ref, cells, out, in_sems, out_sems):
+def rotate_kernel(cells_ref, coef_ref, after_ref, out_ref, cells, out, in_sems, out_sems):
+    del after_ref
+
     def fetch(k, i):
         rows = pl.ds(SHARE * k + 2 * i, 2)
         return pltpu.make_async_copy(
@@ -248,11 +241,11 @@
     put_tail.wait()
 
 
-def rotate(cells, coef):
+def rotate(cells, coef, after):
     return pl.pallas_call(
         rotate_kernel,
         out_shape=jax.ShapeDtypeStruct((NB, 2 * SHARE + 1, V, 128), jnp.bfloat16),
-        in_specs=[ANY, pl.BlockSpec(memory_space=pltpu.VMEM)],
+        in_specs=[ANY, pl.BlockSpec(memory_space=pltpu.VMEM), ANY],
         out_specs=ANY,
         scratch_shapes=[
             pltpu.VMEM((NB, 3 * SHARE + 1, V, 128), jnp.bfloat16),
@@ -265,7 +258,7 @@
             flops=6 * M * M * 128 * (SHARE + 1), bytes_accessed=14_000_000, transcendentals=0
         ),
         name="rotate",
-    )(cells, coef)
+    )(cells, coef, after)
 
 
 def unpack_kernel(in_ref, d_ref, r_ref, stage, last, in_sems, tail_sems, out_sems, last_sems):
@@ -333,6 +326,22 @@
     )(parts)
 
 
+def hold(arrays, until):
+    count = len(arrays)
+
+    def kernel(*refs):
+        del refs
+
+    return pl.pallas_call(
+        kernel,
+        out_shape=[jax.ShapeDtypeStruct(x.shape, x.dtype) for x in arrays],
+        in_specs=[ANY] * (count + len(until)),
+        out_specs=[ANY] * count,
+        input_output_aliases={i: i for i in range(count)},
+        name="hold",
+    )(*arrays, *until)
+
+
 NZ, NY = 3, 9
 VB = 16
 
@@ -423,21 +432,27 @@
 
 def per_device(current, search, previous, coefficients, material, inverse_permittivity):
     w, p, x = as_rows(search), as_rows(previous), as_rows(current)
+    slab, blk = lax.axis_index("slab"), lax.axis_index("blk")
+    place = jnp.stack([slab // 16, (slab // 2) % 8, slab % 2, blk // 2, blk % 2])
+    mark_below = ring_shift(material[NZ - 1 :], "slab", 1)
+    marks = jnp.concatenate([mark_below, material]).reshape((NZ + 1) * NY, 128)
     packed = pack(w, p, x)
     plane = gather_plane(coefficients)
     packed, plane = lax.optimization_barrier((packed, plane))
     cells = lax.all_to_all(packed, "blk", split_axis=0, concat_axis=0, tiled=True)
+    groups = [[h * 16 + z * 2 + c for z in range(8)] for h in range(2) for c in range(2)]
+    mine = lax.all_gather(plane, "slab", axis_index_groups=groups)
+    other = move(mine, "slab", SLAB, (0, 0, 1))
+    coef = assemble(place, mine, other)
     layers = w.reshape(3, NZ, NY, V, 128)
-    above = ring_shift(layers[:2, 0].reshape(2 * NY, V, 128), "slab", -1)
-    below = ring_shift(layers[:, NZ - 1].reshape(3 * NY, V, 128), "slab", 1)
-    mark_below = ring_shift(material[NZ - 1 :], "slab", 1)
-    plane, below, mark_below = lax.optimization_barrier((plane, below, mark_below))
-    marks = jnp.concatenate([mark_below, material]).reshape((NZ + 1) * NY, 128)
-    coef = gather_coefficients(plane)
-    coef, above = lax.optimization_barrier((coef, above))
-    parts = rotate(cells, coef)
+    low = layers[:2, 0].reshape(2 * NY, V, 128)
+    high = layers[:, NZ - 1].reshape(3 * NY, V, 128)
+    low, high = hold([low, high], [mine])
+    above = ring_shift(low, "slab", -1)
+    below = ring_shift(high, "slab", 1)
+    applied = apply_curls(w, above, below, marks, inverse_permittivity.reshape(NMAT, 9))
+    parts = rotate(cells, coef, applied)
     back = lax.all_to_all(parts, "blk", split_axis=0, concat_axis=0, tiled=True)
-    applied = apply_curls(w, above, below, marks, inverse_permittivity.reshape(NMAT, 9))
     direction, rotated = unpack(back)
     return as_block(applied), as_block(rotated), as_block(direction)
 

time: 205 us -> 196 us (0.956)
  the two profiles are of different devices: /device:TPU:224 before, /device:TPU:16 now
where the time goes in v3:
time: 196 us; the launch traced here: 194 us
  waiting for transfers between devices  69.1 us (35%)
  blocking collectives  51.3 us (26%)
  Pallas kernels  34.1 us (17%)
  starting transfers between devices  18.4 us (9%)
  between operations  14.2 us (7%)
  local copies, waits for them, and re-layouts  5.23 us (3%)
    all_to_all x1, blocking collectives, per_device(): back = lax.all_to_all(parts, 'blk', split_axis=0, concat_axis=0, tiled=True)  51.3 us
    all_gather x1, waiting for transfers between devices, per_device(): mine = lax.all_gather(plane, 'slab', axis_index_groups=groups)  47.7 us
    ppermute x3, waiting for transfers between devices, ring_shift(): return lax.ppermute(x, axis, [(i, (i + by) % count) for i in range(count)])  14.9 us
    pallas_call x1, Pallas kernels, rotate(): pl.pallas_call(rotate_kernel, out_shape=jax.ShapeDtypeStruct((NB, 2 * SHA...  11 us
    pallas_call x1, Pallas kernels, assemble(): pl.pallas_call(assemble_kernel, out_shape=jax.ShapeDtypeStruct((M, 3 * M)...  7.93 us
    ppermute x6, starting transfers between devices, move(): return lax.ppermute(x, axis, pairs)  6.62 us
    pallas_call x1, Pallas kernels, apply_curls(): pl.pallas_call(curl_kernel, out_shape=jax.ShapeDtypeStruct((ROWS, V, 128)...  6.05 us
    pallas_call x1, Pallas kernels, pack(): pl.pallas_call(pack_kernel, out_shape=jax.ShapeDtypeStruct(shape, jnp.bfl...  5.56 us
  transfers between devices with their start and end apart: 12, of which 5 were waited for; matrix products, arithmetic and copies ran while one was open for 2% of the time, Pallas kernels for 10%

profile of v3, /device:TPU:16, one launch (start us, length us, event | category | flops | bytes accessed | tf_op | source)
XLA Modules:
  0.0 193.8 jit_solution(4868124479794192580)
XLA Ops:
  7.2 1.4 collective-permute-start.1
  8.5 1.4 collective-permute-start.3
  9.9 1.5 collective-permute-start.2
  11.3 1.3 collective-permute-done.3
  12.7 2.7 %collective-permute-done.2 = bf16[72,96]{1,0:T(8,128)(2,1)S(1)} collective-permute-done((bf16[72,96]{1,0:T(8,128)(2,1)}, bf16[72,96]{1,0:T(8,128)(2,1)S(1)}, u32[]{:S(2)}, u32[]{:S(2)}) %collective-permute-start.2) | collective-permute-done | bytes 13856 | tf_op jit(solution)/shard_map/ppermute | solution.py:32
  15.4 0.7 fusion
  16.1 1.8 collective-permute-start.5
  17.9 1.1 collective-permute-start.4
  19.0 0.9 collective-permute-start.6
  19.9 5.6 %pack.1 = bf16[8,31,96,128]{3,2,1,0:T(8,128)(2,1)} custom-call(bf16[81,96,128]{2,1,0:T(8,128)(2,1)} %bitcast.37, bf16[81,96,128]{2,1,0:T(8,128)(2,1)} %bitcast.45, bf16[81,96,128]{2,1,0:T(8,128)(2,1)} %bitcast.46), custom_call_target="tpu_custom_call" | custom-call | flops 2000000 | bytes 12000000 | tf_op jit(solution)/shard_map/pack/pallas_call | solution.py:148
  25.5 0.8 pad_maximum_fusion
  26.3 5.0 %all-to-all-start = ((bf16[8,31,96,128]{3,2,1,0:T(8,128)(2,1)}), bf16[8,31,96,128]{3,2,1,0:T(8,128)(2,1)}, u32[]{:S(2)}, u32[]{:S(2)}) async-start(bf16[8,31,96,128]{3,2,1,0:T(8,128)(2,1)} %pack.1), calls=%async_computation | async-start | bytes 12189696 | tf_op jit(solution)/shard_map/all_to_all | solution.py:442
  31.3 0.0 all-gather.3.cloned.1.call-start
  31.3 0.7 all-gather.3.cloned.1.call-update
  32.0 47.7 %all-gather.3.cloned.1.call-done = bf16[32,4,72,96]{3,2,1,0:T(8,128)(2,1)} async-done(((bf16[4,4,72,96]{3,2,1,0:T(8,128)(2,1)}), bf16[32,4,72,96]{3,2,1,0:T(8,128)(2,1)}) %all-gather.3.cloned.1.call-update) | async-done | bytes 1769488 | tf_op jit(solution)/shard_map/all_gather | solution.py:444
  79.8 0.8 slice.12
  80.6 0.9 slice.13
  81.5 0.5 collective-permute-start.8
  82.0 4.9 %collective-permute-start.7 = (bf16[18,96,128]{2,1,0:T(8,128)(2,1)}, bf16[18,96,128]{2,1,0:T(8,128)(2,1)S(1)}, u32[]{:S(2)}, u32[]{:S(2)}) collective-permute-start(bf16[18,96,128]{2,1,0:T(8,128)(2,1)} %get-tuple-element.10), channel_id=1, source_target_pairs={{0,248},{8,0},{16,8},{24,16},{32,24},{40,32},{48,40},{56,48},{64,5... | collective-permute-start | bytes 1327112 | tf_op jit(solution)/shard_map/ppermute | solution.py:37
  86.8 0.1 collective-permute-start
  87.0 0.7 reshape.36.eps_ref
  87.7 0.7 stack.63.place_ref
  88.3 14.9 %collective-permute-done = s32[1,9,128]{2,0,1:T(1,128)S(1)} collective-permute-done((s32[1,9,128]{2,0,1:T(1,128)S(1)}, s32[1,9,128]{2,0,1:T(1,128)S(1)}, u32[]{:S(2)}, u32[]{:S(2)}) %collective-permute-start) | collective-permute-done | bytes 4640 | tf_op jit(solution)/shard_map/ppermute | solution.py:37
  103.3 0.6 reshape.37.mat_ref
  103.9 0.8 copy-done.2
  104.6 0.8 copy-done.1
  105.5 6.1 %curls.1.after_ref = bf16[81,96,128]{2,1,0:T(8,128)(2,1)} custom-call(f32[4,9]{1,0:T(4,128)} %reshape.36.eps_ref, s32[36,128]{1,0:T(8,128)} %reshape.37.mat_ref, bf16[81,96,128]{2,1,0:T(8,128)(2,1)} %bitcast.38, bf16[18,96,128]{2,1,0:T(8,128)(2,1)} %copy-done.2, bf16[27,96,128]{2,1,0:T(8,128)(2,1)} %copy-done.1), custom_call_target="tpu_custom_call" | custom-call | flops 60000000 | bytes 5000000 | tf_op jit(solution)/shard_map/curls/pallas_call | solution.py:401
  111.5 7.9 %assemble.1.coef_ref = bf16[768,2304]{1,0:T(8,128)(2,1)} custom-call(s32[5]{0:T(128)} %stack.63.place_ref, bf16[8,4,2,2,72,96]{5,4,3,2,1,0:T(8,128)(2,1)} %bitcast.43, bf16[8,4,2,2,72,96]{5,4,3,2,1,0:T(8,128)(2,1)} %bitcast.26.other_ref), custom_call_target="tpu_custom_call" | custom-call | flops 10000000 | bytes 8000000 | tf_op jit(solution)/shard_map/assemble/pallas_call | solution.py:78
  119.5 1.7 all-to-all-done.cells_ref
  121.2 11.0 %rotate.1 = bf16[8,21,96,128]{3,2,1,0:T(8,128)(2,1)} custom-call(bf16[8,31,96,128]{3,2,1,0:T(8,128)(2,1)} %all-to-all-done.cells_ref, bf16[768,2304]{1,0:T(8,128)(2,1)} %assemble.1.coef_ref, bf16[81,96,128]{2,1,0:T(8,128)(2,1)} %curls.1.after_ref), custom_call_target="tpu_custom_call" | custom-call | flops 4982833152 | bytes 14000000 | tf_op jit(solution)/shard_map/rotate/pallas_call | solution.py:245
  132.1 51.3 %all_to_all.10.in_ref = bf16[8,21,96,128]{3,2,1,0:T(8,128)(2,1)} all-to-all(bf16[8,21,96,128]{3,2,1,0:T(8,128)(2,1)} %rotate.1), channel_id=1, replica_groups=mesh['slab'=32,'blk'=8] {'blk'}, dimensions={0} | all-to-all | bytes 8257536 | tf_op jit(solution)/shard_map/all_to_all | solution.py:455
  183.4 3.6 %unpack.1 = (bf16[81,96,128]{2,1,0:T(8,128)(2,1)}, bf16[81,96,128]{2,1,0:T(8,128)(2,1)}) custom-call(bf16[8,21,96,128]{3,2,1,0:T(8,128)(2,1)} %all_to_all.10.in_ref), custom_call_target="tpu_custom_call" | custom-call | tf_op jit(solution)/shard_map/unpack/pallas_call | solution.py:311
  (21 shorter events, 0.1 us)
Async XLA Ops:
  7.2 4.2 %collective-permute-start.1 = (bf16[72,96]{1,0:T(8,128)(2,1)}, bf16[72,96]{1,0:T(8,128)(2,1)S(1)}, u32[]{:S(2)}, u32[]{:S(2)}) collective-permute-start(bf16[72,96]{1,0:T(8,128)(2,1)} %param.9), channel_id=1, source_target_pairs={{0,1},{1,0},{2,3},{3,2},{4,5},{5,4},{6,7},{7,6},{8,9},{9,8},{10,11... | collective-permute-start | bytes 41480 | tf_op jit(solution)/shard_map/ppermute | solution.py:32
  8.5 4.2 %collective-permute-start.3 = (bf16[72,96]{1,0:T(8,128)(2,1)}, bf16[72,96]{1,0:T(8,128)(2,1)S(1)}, u32[]{:S(2)}, u32[]{:S(2)}) collective-permute-start(bf16[72,96]{1,0:T(8,128)(2,1)} %param.9), channel_id=1, source_target_pairs={{0,129},{1,128},{2,131},{3,130},{4,133},{5,132},{6,135},{7,134},{8... | collective-permute-start | bytes 41480 | tf_op jit(solution)/shard_map/ppermute | solution.py:45
  9.9 5.5 %collective-permute-start.2 = (bf16[72,96]{1,0:T(8,128)(2,1)}, bf16[72,96]{1,0:T(8,128)(2,1)S(1)}, u32[]{:S(2)}, u32[]{:S(2)}) collective-permute-start(bf16[72,96]{1,0:T(8,128)(2,1)} %param.9), channel_id=1, source_target_pairs={{0,128},{8,136},{16,144},{24,152},{32,160},{40,168},{48,176},{56,1... | collective-permute-start | bytes 41480 | tf_op jit(solution)/shard_map/ppermute | solution.py:32
  16.1 9.4 %collective-permute-start.5 = (bf16[4,72,96]{2,1,0:T(8,128)(2,1)S(1)}, bf16[4,72,96]{2,1,0:T(8,128)(2,1)S(1)}, u32[]{:S(2)}, u32[]{:S(2)}) collective-permute-start(bf16[4,72,96]{2,1,0:T(8,128)(2,1)S(1)} %get-tuple-element.16), channel_id=1, source_target_pairs={{0,4},{1,5},{2,6},{3,7},{4,0},{5,1},{6,2},{7,3},{8,12},{9,13},{10,... | collective-permute-start | bytes 165896 | tf_op jit(solution)/shard_map/ppermute | solution.py:32
  17.9 7.6 %collective-permute-start.4 = (bf16[4,72,96]{2,1,0:T(8,128)(2,1)S(1)}, bf16[4,72,96]{2,1,0:T(8,128)(2,1)S(1)}, u32[]{:S(2)}, u32[]{:S(2)}) collective-permute-start(bf16[4,72,96]{2,1,0:T(8,128)(2,1)S(1)} %get-tuple-element.16), channel_id=1, source_target_pairs={{0,6},{1,7},{2,0},{3,1},{4,2},{5,3},{6,4},{7,5},{8,14},{9,15},{10,... | collective-permute-start | bytes 165896 | tf_op jit(solution)/shard_map/ppermute | solution.py:32
  19.0 6.5 %collective-permute-start.6 = (bf16[4,72,96]{2,1,0:T(8,128)(2,1)S(1)}, bf16[4,72,96]{2,1,0:T(8,128)(2,1)S(1)}, u32[]{:S(2)}, u32[]{:S(2)}) collective-permute-start(bf16[4,72,96]{2,1,0:T(8,128)(2,1)S(1)} %get-tuple-element.16), channel_id=1, source_target_pairs={{0,2},{1,3},{2,4},{3,5},{4,6},{5,7},{6,0},{7,1},{8,10},{9,11},{10,... | collective-permute-start | bytes 165896 | tf_op jit(solution)/shard_map/ppermute | solution.py:32
  26.3 53.5 %copy-start = (bf16[96,3,3,9,128]{4,0,3,2,1:T(8,128)(2,1)S(1)}, bf16[96,3,3,9,128]{4,0,3,2,1:T(8,128)(2,1)}, u32[]{:S(2)}) copy-start(bf16[96,3,3,9,128]{4,0,3,2,1:T(8,128)(2,1)} %param.7) | copy-start | bytes 5971972
  26.3 94.9 %all-to-all-start = ((bf16[8,31,96,128]{3,2,1,0:T(8,128)(2,1)}), bf16[8,31,96,128]{3,2,1,0:T(8,128)(2,1)}, u32[]{:S(2)}, u32[]{:S(2)}) async-start(bf16[8,31,96,128]{3,2,1,0:T(8,128)(2,1)} %pack.1), calls=%async_computation | async-start | bytes 12189696 | tf_op jit(solution)/shard_map/all_to_all | solution.py:442
  31.3 48.5 %all-gather.3.cloned.1.call-start = ((), (), s32[]{:S(2)}) async-start(), calls=%async_computation.2 | async-start | bytes 2654208 | tf_op jit(solution)/shard_map/all_gather | solution.py:444
  79.8 31.8 %collective-permute-start.9 = (bf16[8,4,4,72,96]{4,3,2,1,0:T(8,128)(2,1)}, bf16[8,4,4,72,96]{4,3,2,1,0:T(8,128)(2,1)}, u32[]{:S(2)}, u32[]{:S(2)}) collective-permute-start(bf16[8,4,4,72,96]{4,3,2,1,0:T(8,128)(2,1)} %bitcast.41), channel_id=1, source_target_pairs={{0,8},{8,0},{16,24},{24,16},{32,40},{40,32},{48,56},{56,48},{64,72... | collective-permute-start | bytes 5308424 | tf_op jit(solution)/shard_map/ppermute | solution.py:32
  80.6 6.2 %copy-start.3 = (s32[3,9,128]{2,0,1:T(4,128)S(1)}, s32[3,9,128]{2,0,1:T(4,128)}, u32[]{:S(2)}) copy-start(s32[3,9,128]{2,0,1:T(4,128)} %param.10) | copy-start | bytes 41476
  80.6 6.4 %copy-start.4 = (f32[4,3,3]{2,0,1:T(4,128)S(1)}, f32[4,3,3]{2,0,1:T(4,128)}, u32[]{:S(2)}) copy-start(f32[4,3,3]{2,0,1:T(4,128)} %param.11) | copy-start | bytes 436
  81.5 22.4 %collective-permute-start.8 = (bf16[27,96,128]{2,1,0:T(8,128)(2,1)}, bf16[27,96,128]{2,1,0:T(8,128)(2,1)S(1)}, u32[]{:S(2)}, u32[]{:S(2)}) collective-permute-start(bf16[27,96,128]{2,1,0:T(8,128)(2,1)} %get-tuple-element.11), channel_id=1, source_target_pairs={{0,8},{8,16},{16,24},{24,32},{32,40},{40,48},{48,56},{56,64},{64,7... | collective-permute-start | bytes 1990664 | tf_op jit(solution)/shard_map/ppermute | solution.py:37
  82.0 21.9 %collective-permute-start.7 = (bf16[18,96,128]{2,1,0:T(8,128)(2,1)}, bf16[18,96,128]{2,1,0:T(8,128)(2,1)S(1)}, u32[]{:S(2)}, u32[]{:S(2)}) collective-permute-start(bf16[18,96,128]{2,1,0:T(8,128)(2,1)} %get-tuple-element.10), channel_id=1, source_target_pairs={{0,248},{8,0},{16,8},{24,16},{32,24},{40,32},{48,40},{56,48},{64,5... | collective-permute-start | bytes 1327112 | tf_op jit(solution)/shard_map/ppermute | solution.py:37
  86.8 16.4 %collective-permute-start = (s32[1,9,128]{2,0,1:T(1,128)S(1)}, s32[1,9,128]{2,0,1:T(1,128)S(1)}, u32[]{:S(2)}, u32[]{:S(2)}) collective-permute-start(s32[1,9,128]{2,0,1:T(1,128)S(1)} %slice.9), channel_id=1, source_target_pairs={{0,8},{8,16},{16,24},{24,32},{32,40},{40,48},{48,56},{56,64},{64,7... | collective-permute-start | bytes 13832 | tf_op jit(solution)/shard_map/ppermute | solution.py:37
  103.9 0.8 copy-start.2
  104.6 0.8 copy-start.1
Sparse Core Ops, SparseCore 0:
  34.5 45.2 all-gather.2

commit v4 on v3

--- a/solution.py
+++ b/solution.py
@@ -18,7 +18,7 @@
 SLAB = (2, 8, 2)
 BLK = (4, 2)
 ANY = pl.BlockSpec(memory_space=pl.ANY)
-VMEM_LIMIT = 56 * 1024 * 1024
+MIB = 1024 * 1024
 
 
 def move(x, axis, sizes, steps):
@@ -84,7 +84,7 @@
             in_specs=[pieces, pieces],
             out_specs=pl.BlockSpec((M // NB, 3 * M), lambda b, at: (b, 0)),
         ),
-        compiler_params=pltpu.CompilerParams(vmem_limit_bytes=VMEM_LIMIT),
+        compiler_params=pltpu.CompilerParams(vmem_limit_bytes=56 * MIB),
         cost_estimate=pl.CostEstimate(
             flops=10_000_000, bytes_accessed=8_000_000, transcendentals=0
         ),
@@ -157,7 +157,7 @@
             pltpu.SemaphoreType.DMA((3,)),
             pltpu.SemaphoreType.DMA((NB,)),
         ],
-        compiler_params=pltpu.CompilerParams(vmem_limit_bytes=VMEM_LIMIT),
+        compiler_params=pltpu.CompilerParams(vmem_limit_bytes=56 * MIB),
         cost_estimate=pl.CostEstimate(
             flops=2_000_000, bytes_accessed=12_000_000, transcendentals=0
         ),
@@ -253,7 +253,7 @@
             pltpu.SemaphoreType.DMA((3, SHARE // 2 + 1)),
             pltpu.SemaphoreType.DMA((2, SHARE // 2 + 1)),
         ],
-        compiler_params=pltpu.CompilerParams(vmem_limit_bytes=VMEM_LIMIT),
+        compiler_params=pltpu.CompilerParams(vmem_limit_bytes=24 * MIB),
         cost_estimate=pl.CostEstimate(
             flops=6 * M * M * 128 * (SHARE + 1), bytes_accessed=14_000_000, transcendentals=0
         ),
@@ -321,7 +321,7 @@
             pltpu.SemaphoreType.DMA((NB, 2)),
             pltpu.SemaphoreType.DMA((2,)),
         ],
-        compiler_params=pltpu.CompilerParams(vmem_limit_bytes=VMEM_LIMIT),
+        compiler_params=pltpu.CompilerParams(vmem_limit_bytes=8 * MIB),
         name="unpack",
     )(parts)
 
@@ -346,7 +346,11 @@
 VB = 16
 
 
-def curl_kernel(eps_ref, mat_ref, w_ref, above_ref, below_ref, out_ref, tensor, electric):
+def curl_kernel(
+    eps_ref, mat_ref, w_ref, above_ref, below_ref, out_ref, token_ref, tensor, electric
+):
+    token_ref[...] = jnp.zeros_like(token_ref)
+
     @pl.when(pl.program_id(0) == 0)
     def _():
         marks = mat_ref[...]
@@ -400,7 +404,10 @@
     block = lambda rows: pl.BlockSpec((rows, VB, 128), lambda i: (0, i, 0))
     return pl.pallas_call(
         curl_kernel,
-        out_shape=jax.ShapeDtypeStruct((ROWS, V, 128), jnp.bfloat16),
+        out_shape=(
+            jax.ShapeDtypeStruct((ROWS, V, 128), jnp.bfloat16),
+            jax.ShapeDtypeStruct((8, 128), jnp.float32),
+        ),
         grid=(V // VB,),
         in_specs=[
             pl.BlockSpec(memory_space=pltpu.SMEM),
@@ -409,12 +416,12 @@
             block(2 * NY),
             block(3 * NY),
         ],
-        out_specs=block(ROWS),
+        out_specs=(block(ROWS), pl.BlockSpec((8, 128), lambda i: (0, 0))),
         scratch_shapes=[
             pltpu.VMEM((9, (NZ + 1) * NY, 128), jnp.float32),
             pltpu.VMEM((3, (NZ + 1) * NY, VB, 128), jnp.float32),
         ],
-        compiler_params=pltpu.CompilerParams(vmem_limit_bytes=VMEM_LIMIT),
+        compiler_params=pltpu.CompilerParams(vmem_limit_bytes=56 * MIB),
         cost_estimate=pl.CostEstimate(
             flops=60_000_000, bytes_accessed=5_000_000, transcendentals=0
         ),
@@ -450,8 +457,8 @@
     low, high = hold([low, high], [mine])
     above = ring_shift(low, "slab", -1)
     below = ring_shift(high, "slab", 1)
-    applied = apply_curls(w, above, below, marks, inverse_permittivity.reshape(NMAT, 9))
-    parts = rotate(cells, coef, applied)
+    applied, token = apply_curls(w, above, below, marks, inverse_permittivity.reshape(NMAT, 9))
+    parts = rotate(cells, coef, token)
     back = lax.all_to_all(parts, "blk", split_axis=0, concat_axis=0, tiled=True)
     direction, rotated = unpack(back)
     return as_block(applied), as_block(rotated), as_block(direction)

time: 196 us -> 195 us (level)
  blocking collectives: 51.3 us -> 49.2 us
    pallas_call x1, Pallas kernels: 11 us -> 8.74 us  [rotate(): pl.pallas_call(rotate_kernel, out_shape=jax.ShapeDtypeStruct((NB, 2 * SHA...]
    all_to_all x1, blocking collectives: 51.3 us -> 49.2 us  [per_device(): back = lax.all_to_all(parts, 'blk', split_axis=0, concat_axis=0, tiled=True)]
    unnamed x11 -> x15, local copies, waits for them, and re-layouts: 1.61 us -> 3.61 us
where the time goes in v4:
time: 195 us; the launch traced here: 193 us
  waiting for transfers between devices  69.2 us (35%)
  blocking collectives  49.2 us (25%)
  Pallas kernels  33.3 us (17%)
  starting transfers between devices  18.4 us (9%)
  between operations  14.2 us (7%)
  local copies, waits for them, and re-layouts  7.1 us (4%)
    all_to_all x1, blocking collectives, per_device(): back = lax.all_to_all(parts, 'blk', split_axis=0, concat_axis=0, tiled=True)  49.2 us
    all_gather x1, waiting for transfers between devices, per_device(): mine = lax.all_gather(plane, 'slab', axis_index_groups=groups)  47.8 us
    ppermute x3, waiting for transfers between devices, ring_shift(): return lax.ppermute(x, axis, [(i, (i + by) % count) for i in range(count)])  15 us
    pallas_call x1, Pallas kernels, rotate(): pl.pallas_call(rotate_kernel, out_shape=jax.ShapeDtypeStruct((NB, 2 * SHA...  8.74 us
    pallas_call x1, Pallas kernels, assemble(): pl.pallas_call(assemble_kernel, out_shape=jax.ShapeDtypeStruct((M, 3 * M)...  7.94 us
    ppermute x6, starting transfers between devices, move(): return lax.ppermute(x, axis, pairs)  6.62 us
    pallas_call x1, Pallas kernels, apply_curls(): pl.pallas_call(curl_kernel, out_shape=(jax.ShapeDtypeStruct((ROWS, V, 128...  6.05 us
    pallas_call x1, Pallas kernels, pack(): pl.pallas_call(pack_kernel, out_shape=jax.ShapeDtypeStruct(shape, jnp.bfl...  5.58 us
  transfers between devices with their start and end apart: 12, of which 5 were waited for; matrix products, arithmetic and copies ran while one was open for 2% of the time, Pallas kernels for 10%

profile of v4, /device:TPU:16, one launch (start us, length us, event | category | flops | bytes accessed | tf_op | source)
XLA Modules:
  0.0 193.1 jit_solution(1761578155725883850)
XLA Ops:
  7.2 1.4 collective-permute-start.1
  8.5 1.4 collective-permute-start.3
  9.9 1.5 collective-permute-start.2
  11.3 1.3 collective-permute-done.3
  12.7 2.7 %collective-permute-done.2 = bf16[72,96]{1,0:T(8,128)(2,1)S(1)} collective-permute-done((bf16[72,96]{1,0:T(8,128)(2,1)}, bf16[72,96]{1,0:T(8,128)(2,1)S(1)}, u32[]{:S(2)}, u32[]{:S(2)}) %collective-permute-start.2) | collective-permute-done | bytes 13856 | tf_op jit(solution)/shard_map/ppermute | solution.py:32
  15.4 0.7 fusion
  16.1 1.8 collective-permute-start.5
  17.9 1.1 collective-permute-start.4
  19.0 0.9 collective-permute-start.6
  19.9 5.6 %pack.1 = bf16[8,31,96,128]{3,2,1,0:T(8,128)(2,1)} custom-call(bf16[81,96,128]{2,1,0:T(8,128)(2,1)} %bitcast.37, bf16[81,96,128]{2,1,0:T(8,128)(2,1)} %bitcast.45, bf16[81,96,128]{2,1,0:T(8,128)(2,1)} %bitcast.46), custom_call_target="tpu_custom_call" | custom-call | flops 2000000 | bytes 12000000 | tf_op jit(solution)/shard_map/pack/pallas_call | solution.py:148
  25.5 0.8 pad_maximum_fusion
  26.3 5.0 %all-to-all-start = ((bf16[8,31,96,128]{3,2,1,0:T(8,128)(2,1)}), bf16[8,31,96,128]{3,2,1,0:T(8,128)(2,1)}, u32[]{:S(2)}, u32[]{:S(2)}) async-start(bf16[8,31,96,128]{3,2,1,0:T(8,128)(2,1)} %pack.1), calls=%async_computation | async-start | bytes 12189696 | tf_op jit(solution)/shard_map/all_to_all | solution.py:449
  31.3 0.7 all-gather.3.cloned.1.call-update
  32.0 47.8 %all-gather.3.cloned.1.call-done = bf16[32,4,72,96]{3,2,1,0:T(8,128)(2,1)} async-done(((bf16[4,4,72,96]{3,2,1,0:T(8,128)(2,1)}), bf16[32,4,72,96]{3,2,1,0:T(8,128)(2,1)}) %all-gather.3.cloned.1.call-update) | async-done | bytes 1769488 | tf_op jit(solution)/shard_map/all_gather | solution.py:451
  79.8 0.8 slice.12
  80.6 0.9 slice.13
  81.5 0.5 collective-permute-start.8
  82.0 4.9 %collective-permute-start.7 = (bf16[18,96,128]{2,1,0:T(8,128)(2,1)}, bf16[18,96,128]{2,1,0:T(8,128)(2,1)S(1)}, u32[]{:S(2)}, u32[]{:S(2)}) collective-permute-start(bf16[18,96,128]{2,1,0:T(8,128)(2,1)} %get-tuple-element.12), channel_id=1, source_target_pairs={{0,248},{8,0},{16,8},{24,16},{32,24},{40,32},{48,40},{56,48},{64,5... | collective-permute-start | bytes 1327112 | tf_op jit(solution)/shard_map/ppermute | solution.py:37
  86.8 0.1 collective-permute-start
  87.0 0.6 reshape.36.eps_ref
  87.7 0.6 stack.63.place_ref
  88.2 15.0 %collective-permute-done = s32[1,9,128]{2,0,1:T(1,128)S(1)} collective-permute-done((s32[1,9,128]{2,0,1:T(1,128)S(1)}, s32[1,9,128]{2,0,1:T(1,128)S(1)}, u32[]{:S(2)}, u32[]{:S(2)}) %collective-permute-start) | collective-permute-done | bytes 4640 | tf_op jit(solution)/shard_map/ppermute | solution.py:37
  103.3 0.6 reshape.37.mat_ref
  103.9 0.8 copy-done.4
  104.7 0.8 copy-done.3
  105.5 6.1 %curls.1 = (bf16[81,96,128]{2,1,0:T(8,128)(2,1)}, f32[8,128]{1,0:T(8,128)}) custom-call(f32[4,9]{1,0:T(4,128)} %reshape.36.eps_ref, s32[36,128]{1,0:T(8,128)} %reshape.37.mat_ref, bf16[81,96,128]{2,1,0:T(8,128)(2,1)} %bitcast.38, bf16[18,96,128]{2,1,0:T(8,128)(2,1)} %copy-done.4, bf16[27,96,128]{2,1,0:T(8,128)(2,1)} %copy-done.3), custom_call_target="tpu_custom_call" | custom-call | flops 60000000 | bytes 5000000 | tf_op jit(solution)/shard_map/curls/pallas_call | solution.py:405
  111.5 7.9 %assemble.1.coef_ref = bf16[768,2304]{1,0:T(8,128)(2,1)} custom-call(s32[5]{0:T(128)} %stack.63.place_ref, bf16[8,4,2,2,72,96]{5,4,3,2,1,0:T(8,128)(2,1)} %bitcast.43, bf16[8,4,2,2,72,96]{5,4,3,2,1,0:T(8,128)(2,1)} %bitcast.26.other_ref), custom_call_target="tpu_custom_call" | custom-call | flops 10000000 | bytes 8000000 | tf_op jit(solution)/shard_map/assemble/pallas_call | solution.py:78
  119.5 1.7 all-to-all-done.cells_ref
  121.2 2.0 %copy-done = bf16[768,2304]{1,0:T(8,128)(2,1)S(1)} copy-done((bf16[768,2304]{1,0:T(8,128)(2,1)S(1)}, bf16[768,2304]{1,0:T(8,128)(2,1)}, u32[]{:S(2)}) %copy-start) | copy-done | bytes 3538968
  123.2 8.7 %rotate.1 = bf16[8,21,96,128]{3,2,1,0:T(8,128)(2,1)S(1)} custom-call(bf16[8,31,96,128]{3,2,1,0:T(8,128)(2,1)} %all-to-all-done.cells_ref, bf16[768,2304]{1,0:T(8,128)(2,1)S(1)} %copy-done, f32[8,128]{1,0:T(8,128)S(1)} %copy-done.1), custom_call_target="tpu_custom_call" | custom-call | flops 4982833152 | bytes 14000000 | tf_op jit(solution)/shard_map/rotate/pallas_call | solution.py:245
  131.9 49.2 %all_to_all.10.in_ref = bf16[8,21,96,128]{3,2,1,0:T(8,128)(2,1)S(1)} all-to-all(bf16[8,21,96,128]{3,2,1,0:T(8,128)(2,1)S(1)} %rotate.1), channel_id=1, replica_groups=mesh['slab'=32,'blk'=8] {'blk'}, dimensions={0} | all-to-all | bytes 8257536 | tf_op jit(solution)/shard_map/all_to_all | solution.py:462
  181.2 5.0 %unpack.1 = (bf16[81,96,128]{2,1,0:T(8,128)(2,1)}, bf16[81,96,128]{2,1,0:T(8,128)(2,1)}) custom-call(bf16[8,21,96,128]{3,2,1,0:T(8,128)(2,1)S(1)} %all_to_all.10.in_ref), custom_call_target="tpu_custom_call" | custom-call | tf_op jit(solution)/shard_map/unpack/pallas_call | solution.py:311
  (25 shorter events, 0.1 us)
Async XLA Ops:
  7.2 4.2 %collective-permute-start.1 = (bf16[72,96]{1,0:T(8,128)(2,1)}, bf16[72,96]{1,0:T(8,128)(2,1)S(1)}, u32[]{:S(2)}, u32[]{:S(2)}) collective-permute-start(bf16[72,96]{1,0:T(8,128)(2,1)} %param.9), channel_id=1, source_target_pairs={{0,1},{1,0},{2,3},{3,2},{4,5},{5,4},{6,7},{7,6},{8,9},{9,8},{10,11... | collective-permute-start | bytes 41480 | tf_op jit(solution)/shard_map/ppermute | solution.py:32
  8.5 4.2 %collective-permute-start.3 = (bf16[72,96]{1,0:T(8,128)(2,1)}, bf16[72,96]{1,0:T(8,128)(2,1)S(1)}, u32[]{:S(2)}, u32[]{:S(2)}) collective-permute-start(bf16[72,96]{1,0:T(8,128)(2,1)} %param.9), channel_id=1, source_target_pairs={{0,129},{1,128},{2,131},{3,130},{4,133},{5,132},{6,135},{7,134},{8... | collective-permute-start | bytes 41480 | tf_op jit(solution)/shard_map/ppermute | solution.py:45
  9.9 5.5 %collective-permute-start.2 = (bf16[72,96]{1,0:T(8,128)(2,1)}, bf16[72,96]{1,0:T(8,128)(2,1)S(1)}, u32[]{:S(2)}, u32[]{:S(2)}) collective-permute-start(bf16[72,96]{1,0:T(8,128)(2,1)} %param.9), channel_id=1, source_target_pairs={{0,128},{8,136},{16,144},{24,152},{32,160},{40,168},{48,176},{56,1... | collective-permute-start | bytes 41480 | tf_op jit(solution)/shard_map/ppermute | solution.py:32
  16.1 9.4 %collective-permute-start.5 = (bf16[4,72,96]{2,1,0:T(8,128)(2,1)S(1)}, bf16[4,72,96]{2,1,0:T(8,128)(2,1)S(1)}, u32[]{:S(2)}, u32[]{:S(2)}) collective-permute-start(bf16[4,72,96]{2,1,0:T(8,128)(2,1)S(1)} %get-tuple-element.20), channel_id=1, source_target_pairs={{0,4},{1,5},{2,6},{3,7},{4,0},{5,1},{6,2},{7,3},{8,12},{9,13},{10,... | collective-permute-start | bytes 165896 | tf_op jit(solution)/shard_map/ppermute | solution.py:32
  17.9 7.6 %collective-permute-start.4 = (bf16[4,72,96]{2,1,0:T(8,128)(2,1)S(1)}, bf16[4,72,96]{2,1,0:T(8,128)(2,1)S(1)}, u32[]{:S(2)}, u32[]{:S(2)}) collective-permute-start(bf16[4,72,96]{2,1,0:T(8,128)(2,1)S(1)} %get-tuple-element.20), channel_id=1, source_target_pairs={{0,6},{1,7},{2,0},{3,1},{4,2},{5,3},{6,4},{7,5},{8,14},{9,15},{10,... | collective-permute-start | bytes 165896 | tf_op jit(solution)/shard_map/ppermute | solution.py:32
  19.0 6.5 %collective-permute-start.6 = (bf16[4,72,96]{2,1,0:T(8,128)(2,1)S(1)}, bf16[4,72,96]{2,1,0:T(8,128)(2,1)S(1)}, u32[]{:S(2)}, u32[]{:S(2)}) collective-permute-start(bf16[4,72,96]{2,1,0:T(8,128)(2,1)S(1)} %get-tuple-element.20), channel_id=1, source_target_pairs={{0,2},{1,3},{2,4},{3,5},{4,6},{5,7},{6,0},{7,1},{8,10},{9,11},{10,... | collective-permute-start | bytes 165896 | tf_op jit(solution)/shard_map/ppermute | solution.py:32
  26.3 53.5 %copy-start.2 = (bf16[96,3,3,9,128]{4,0,3,2,1:T(8,128)(2,1)S(1)}, bf16[96,3,3,9,128]{4,0,3,2,1:T(8,128)(2,1)}, u32[]{:S(2)}) copy-start(bf16[96,3,3,9,128]{4,0,3,2,1:T(8,128)(2,1)} %param.7) | copy-start | bytes 5971972
  26.3 94.9 %all-to-all-start = ((bf16[8,31,96,128]{3,2,1,0:T(8,128)(2,1)}), bf16[8,31,96,128]{3,2,1,0:T(8,128)(2,1)}, u32[]{:S(2)}, u32[]{:S(2)}) async-start(bf16[8,31,96,128]{3,2,1,0:T(8,128)(2,1)} %pack.1), calls=%async_computation | async-start | bytes 12189696 | tf_op jit(solution)/shard_map/all_to_all | solution.py:449
  31.3 48.5 %all-gather.3.cloned.1.call-start = ((), (), s32[]{:S(2)}) async-start(), calls=%async_computation.2 | async-start | bytes 2654208 | tf_op jit(solution)/shard_map/all_gather | solution.py:451
  79.8 31.8 %collective-permute-start.9 = (bf16[8,4,4,72,96]{4,3,2,1,0:T(8,128)(2,1)}, bf16[8,4,4,72,96]{4,3,2,1,0:T(8,128)(2,1)}, u32[]{:S(2)}, u32[]{:S(2)}) collective-permute-start(bf16[8,4,4,72,96]{4,3,2,1,0:T(8,128)(2,1)} %bitcast.41), channel_id=1, source_target_pairs={{0,8},{8,0},{16,24},{24,16},{32,40},{40,32},{48,56},{56,48},{64,72... | collective-permute-start | bytes 5308424 | tf_op jit(solution)/shard_map/ppermute | solution.py:32
  80.6 6.2 %copy-start.5 = (s32[3,9,128]{2,0,1:T(4,128)S(1)}, s32[3,9,128]{2,0,1:T(4,128)}, u32[]{:S(2)}) copy-start(s32[3,9,128]{2,0,1:T(4,128)} %param.10) | copy-start | bytes 41476
  80.6 6.4 %copy-start.6 = (f32[4,3,3]{2,0,1:T(4,128)S(1)}, f32[4,3,3]{2,0,1:T(4,128)}, u32[]{:S(2)}) copy-start(f32[4,3,3]{2,0,1:T(4,128)} %param.11) | copy-start | bytes 436
  81.5 22.4 %collective-permute-start.8 = (bf16[27,96,128]{2,1,0:T(8,128)(2,1)}, bf16[27,96,128]{2,1,0:T(8,128)(2,1)S(1)}, u32[]{:S(2)}, u32[]{:S(2)}) collective-permute-start(bf16[27,96,128]{2,1,0:T(8,128)(2,1)} %get-tuple-element.13), channel_id=1, source_target_pairs={{0,8},{8,16},{16,24},{24,32},{32,40},{40,48},{48,56},{56,64},{64,7... | collective-permute-start | bytes 1990664 | tf_op jit(solution)/shard_map/ppermute | solution.py:37
  82.0 21.9 %collective-permute-start.7 = (bf16[18,96,128]{2,1,0:T(8,128)(2,1)}, bf16[18,96,128]{2,1,0:T(8,128)(2,1)S(1)}, u32[]{:S(2)}, u32[]{:S(2)}) collective-permute-start(bf16[18,96,128]{2,1,0:T(8,128)(2,1)} %get-tuple-element.12), channel_id=1, source_target_pairs={{0,248},{8,0},{16,8},{24,16},{32,24},{40,32},{48,40},{56,48},{64,5... | collective-permute-start | bytes 1327112 | tf_op jit(solution)/shard_map/ppermute | solution.py:37
  86.8 16.4 %collective-permute-start = (s32[1,9,128]{2,0,1:T(1,128)S(1)}, s32[1,9,128]{2,0,1:T(1,128)S(1)}, u32[]{:S(2)}, u32[]{:S(2)}) collective-permute-start(s32[1,9,128]{2,0,1:T(1,128)S(1)} %slice.9), channel_id=1, source_target_pairs={{0,8},{8,16},{16,24},{24,32},{32,40},{40,48},{48,56},{56,64},{64,7... | collective-permute-start | bytes 13832 | tf_op jit(solution)/shard_map/ppermute | solution.py:37
  103.9 0.8 copy-start.4
  104.6 0.8 copy-start.3
  111.5 9.6 %copy-start.1 = (f32[8,128]{1,0:T(8,128)S(1)}, f32[8,128]{1,0:T(8,128)}, u32[]{:S(2)}) copy-start(f32[8,128]{1,0:T(8,128)} %get-tuple-element.16.after_ref) | copy-start | bytes 12292
  121.2 2.0 %copy-start = (bf16[768,2304]{1,0:T(8,128)(2,1)S(1)}, bf16[768,2304]{1,0:T(8,128)(2,1)}, u32[]{:S(2)}) copy-start(bf16[768,2304]{1,0:T(8,128)(2,1)} %assemble.1.coef_ref) | copy-start | bytes 10616836
Sparse Core Ops, SparseCore 0:
  34.5 45.2 all-gather.2

commit v5 on v4

--- a/solution.py
+++ b/solution.py
@@ -53,7 +53,8 @@
         )
     )
     t = jnp.stack(pieces)
-    return jnp.stack([t] + [move(t, "blk", BLK, (-k, 0)) for k in (1, 2, 3)])
+    plane = jnp.stack([t] + [move(t, "blk", BLK, (-k, 0)) for k in (1, 2, 3)])
+    return plane, pieces[1:]
 
 
 def assemble_kernel(place_ref, mine_ref, other_ref, out_ref):
@@ -261,42 +262,24 @@
     )(cells, coef, after)
 
 
-def unpack_kernel(in_ref, d_ref, r_ref, stage, last, in_sems, tail_sems, out_sems, last_sems):
-    tails = [
-        pltpu.make_async_copy(
-            in_ref.at[s, 2 * SHARE], stage.at[s, 2 * SHARE], tail_sems.at[s]
-        )
-        for s in range(NB)
-    ]
-    fetches = [
-        pltpu.make_async_copy(
-            in_ref.at[s, pl.ds(0, 2 * SHARE)],
-            stage.at[s, pl.ds(0, 2 * SHARE)],
-            in_sems.at[s],
-        )
-        for s in range(NB)
-    ]
-    for c in tails + fetches:
-        c.start()
-    for c in tails:
-        c.wait()
-    which = lane_index((V, 128)) // LANES
-    direction = rotated = jnp.zeros((V, 128), jnp.float32)
+def unpack_kernel(parts, d_ref, r_ref, last, out_sems, last_sems):
     copies = []
     for s in range(NB):
-        row = stage[s, 2 * SHARE].astype(jnp.float32)
-        direction = jnp.where(which == s, rolled(row, LANES * s), direction)
-        rotated = jnp.where(which == s, rolled(row, LANES * (s - 1)), rotated)
-        fetches[s].wait()
         for k, ref in enumerate((d_ref, r_ref)):
             copies.append(
                 pltpu.make_async_copy(
-                    stage.at[s, pl.ds(SHARE * k, SHARE)],
+                    parts.at[s, pl.ds(SHARE * k, SHARE)],
                     ref.at[pl.ds(SHARE * s, SHARE)],
                     out_sems.at[s, k],
                 )
             )
             copies[-1].start()
+    which = lane_index((V, 128)) // LANES
+    direction = rotated = jnp.zeros((V, 128), jnp.float32)
+    for s in range(NB):
+        row = parts[s, 2 * SHARE].astype(jnp.float32)
+        direction = jnp.where(which == s, rolled(row, LANES * s), direction)
+        rotated = jnp.where(which == s, rolled(row, LANES * (s - 1)), rotated)
     last[0] = direction.astype(jnp.bfloat16)
     last[1] = rotated.astype(jnp.bfloat16)
     for k, ref in enumerate((d_ref, r_ref)):
@@ -311,17 +294,14 @@
     return pl.pallas_call(
         unpack_kernel,
         out_shape=(whole, whole),
-        in_specs=[ANY],
+        in_specs=[pl.BlockSpec(memory_space=pltpu.VMEM)],
         out_specs=(ANY, ANY),
         scratch_shapes=[
-            pltpu.VMEM((NB, 2 * SHARE + 1, V, 128), jnp.bfloat16),
             pltpu.VMEM((2, V, 128), jnp.bfloat16),
-            pltpu.SemaphoreType.DMA((NB,)),
-            pltpu.SemaphoreType.DMA((NB,)),
             pltpu.SemaphoreType.DMA((NB, 2)),
             pltpu.SemaphoreType.DMA((2,)),
         ],
-        compiler_params=pltpu.CompilerParams(vmem_limit_bytes=8 * MIB),
+        compiler_params=pltpu.CompilerParams(vmem_limit_bytes=12 * MIB),
         name="unpack",
     )(parts)
 
@@ -441,22 +421,23 @@
     w, p, x = as_rows(search), as_rows(previous), as_rows(current)
     slab, blk = lax.axis_index("slab"), lax.axis_index("blk")
     place = jnp.stack([slab // 16, (slab // 2) % 8, slab % 2, blk // 2, blk % 2])
-    mark_below = ring_shift(material[NZ - 1 :], "slab", 1)
-    marks = jnp.concatenate([mark_below, material]).reshape((NZ + 1) * NY, 128)
+    plane, first = gather_plane(coefficients)
+    layers = w.reshape(3, NZ, NY, V, 128)
+    low = layers[:2, 0].reshape(2 * NY, V, 128)
+    high = layers[:, NZ - 1].reshape(3 * NY, V, 128)
+    low, high = hold([low, high], first)
+    below = ring_shift(high, "slab", 1)
+    above = ring_shift(low, "slab", -1)
     packed = pack(w, p, x)
-    plane = gather_plane(coefficients)
     packed, plane = lax.optimization_barrier((packed, plane))
+    (packed,) = hold([packed], [below, above])
     cells = lax.all_to_all(packed, "blk", split_axis=0, concat_axis=0, tiled=True)
     groups = [[h * 16 + z * 2 + c for z in range(8)] for h in range(2) for c in range(2)]
     mine = lax.all_gather(plane, "slab", axis_index_groups=groups)
     other = move(mine, "slab", SLAB, (0, 0, 1))
     coef = assemble(place, mine, other)
-    layers = w.reshape(3, NZ, NY, V, 128)
-    low = layers[:2, 0].reshape(2 * NY, V, 128)
-    high = layers[:, NZ - 1].reshape(3 * NY, V, 128)
-    low, high = hold([low, high], [mine])
-    above = ring_shift(low, "slab", -1)
-    below = ring_shift(high, "slab", 1)
+    mark_below = ring_shift(material[NZ - 1 :], "slab", 1)
+    marks = jnp.concatenate([mark_below, material]).reshape((NZ + 1) * NY, 128)
     applied, token = apply_curls(w, above, below, marks, inverse_permittivity.reshape(NMAT, 9))
     parts = rotate(cells, coef, token)
     back = lax.all_to_all(parts, "blk", split_axis=0, concat_axis=0, tiled=True)

time: 195 us -> 198 us (1.015)
  the two profiles are of different devices: /device:TPU:16 before, /device:TPU:96 now
where the time goes in v5:
time: 198 us; the launch traced here: 197 us
  waiting for transfers between devices  69.2 us (35%)
  blocking collectives  52.4 us (26%)
  Pallas kernels  30.5 us (15%)
  starting transfers between devices  17.8 us (9%)
  between operations  14.2 us (7%)
  local copies, waits for them, and re-layouts  11.3 us (6%)
    all_to_all x1, blocking collectives, per_device(): back = lax.all_to_all(parts, 'blk', split_axis=0, concat_axis=0, tiled=True)  52.4 us
    all_gather x1, waiting for transfers between devices, per_device(): mine = lax.all_gather(plane, 'slab', axis_index_groups=groups)  44.9 us
    all_to_all x1, waiting for transfers between devices, per_device(): lax.all_to_all(packed, 'blk', split_axis=0, concat_axis=0, tiled=True)  20.1 us
    ppermute x6, starting transfers between devices, move(): return lax.ppermute(x, axis, pairs)  10.3 us
    pallas_call x1, Pallas kernels, rotate(): pl.pallas_call(rotate_kernel, out_shape=jax.ShapeDtypeStruct((NB, 2 * SHA...  8.74 us
    pallas_call x1, Pallas kernels, assemble(): pl.pallas_call(assemble_kernel, out_shape=jax.ShapeDtypeStruct((M, 3 * M)...  8.05 us
    pallas_call x1, Pallas kernels, apply_curls(): pl.pallas_call(curl_kernel, out_shape=(jax.ShapeDtypeStruct((ROWS, V, 128...  6.05 us
    unnamed x23, local copies, waits for them, and re-layouts  5.59 us
  transfers between devices with their start and end apart: 12, of which 4 were waited for; matrix products, arithmetic and copies ran while one was open for 4% of the time, Pallas kernels for 10%

profile of v5, /device:TPU:96, one launch (start us, length us, event | category | flops | bytes accessed | tf_op | source)
XLA Modules:
  0.0 196.9 jit_solution(10480419682579641222)
XLA Ops:
  7.2 1.7 collective-permute-start.1
  8.8 2.9 %collective-permute-start.2 = (bf16[72,96]{1,0:T(8,128)(2,1)}, bf16[72,96]{1,0:T(8,128)(2,1)S(1)}, u32[]{:S(2)}, u32[]{:S(2)}) collective-permute-start(bf16[72,96]{1,0:T(8,128)(2,1)} %param.9), channel_id=1, source_target_pairs={{0,128},{8,136},{16,144},{24,152},{32,160},{40,168},{48,176},{56,1... | collective-permute-start | bytes 41480 | tf_op jit(solution)/shard_map/ppermute | solution.py:32
  11.7 0.2 collective-permute-start.3
  12.0 1.8 slice.12
  13.8 2.0 %slice.13 = bf16[3,1,9,96,128]{4,3,2,1,0:T(8,128)(2,1)} slice(bf16[3,3,9,96,128]{4,3,2,1,0:T(8,128)(2,1)} %bitcast.38), slice={[0:3], [2:3], [0:9], [0:96], [0:128]} | slice | bytes 1327104 | tf_op jit(solution)/shard_map/slice | solution.py:427
  15.8 1.2 collective-permute-done.3.refs_4_
  16.9 0.6 copy-done.7
  17.5 1.7 collective-permute-start.4
  19.3 0.8 fusion
  20.1 1.6 collective-permute-start.8
  21.6 2.7 %collective-permute-start.7 = (bf16[4,72,96]{2,1,0:T(8,128)(2,1)S(1)}, bf16[4,72,96]{2,1,0:T(8,128)(2,1)S(1)}, u32[]{:S(2)}, u32[]{:S(2)}) collective-permute-start(bf16[4,72,96]{2,1,0:T(8,128)(2,1)S(1)} %get-tuple-element.20), channel_id=1, source_target_pairs={{0,4},{1,5},{2,6},{3,7},{4,0},{5,1},{6,2},{7,3},{8,12},{9,13},{10,... | collective-permute-start | bytes 165896 | tf_op jit(solution)/shard_map/ppermute | solution.py:32
  24.4 1.4 collective-permute-start.6
  25.8 5.6 %pack.1.refs_0_ = bf16[8,31,96,128]{3,2,1,0:T(8,128)(2,1)} custom-call(bf16[81,96,128]{2,1,0:T(8,128)(2,1)} %bitcast.39, bf16[81,96,128]{2,1,0:T(8,128)(2,1)} %bitcast.45, bf16[81,96,128]{2,1,0:T(8,128)(2,1)} %bitcast.46), custom_call_target="tpu_custom_call" | custom-call | flops 2000000 | bytes 12000000 | tf_op jit(solution)/shard_map/pack/pallas_call | solution.py:149
  31.4 0.8 pad_maximum_fusion
  32.2 0.8 copy-done.4
  32.9 0.8 copy-done.2
  33.8 4.9 %all-to-all-start = ((bf16[8,31,96,128]{3,2,1,0:T(8,128)(2,1)}), bf16[8,31,96,128]{3,2,1,0:T(8,128)(2,1)}, u32[]{:S(2)}, u32[]{:S(2)}) async-start(bf16[8,31,96,128]{3,2,1,0:T(8,128)(2,1)} %hold.3), calls=%async_computation | async-start | bytes 12189696 | tf_op jit(solution)/shard_map/all_to_all | solution.py:434
  38.7 0.7 all-gather.3.cloned.1.call-update
  39.4 44.9 %all-gather.3.cloned.1.call-done = bf16[32,4,72,96]{3,2,1,0:T(8,128)(2,1)} async-done(((bf16[4,4,72,96]{3,2,1,0:T(8,128)(2,1)}), bf16[32,4,72,96]{3,2,1,0:T(8,128)(2,1)}) %all-gather.3.cloned.1.call-update) | async-done | bytes 1769488 | tf_op jit(solution)/shard_map/all_gather | solution.py:436
  84.4 0.6 collective-permute-start
  84.9 0.7 reshape.36.eps_ref
  85.6 0.6 stack.63.place_ref
  86.2 2.3 %collective-permute-done = s32[1,9,128]{2,0,1:T(1,128)S(1)} collective-permute-done((s32[1,9,128]{2,0,1:T(1,128)S(1)}, s32[1,9,128]{2,0,1:T(1,128)S(1)}, u32[]{:S(2)}, u32[]{:S(2)}) %collective-permute-start) | collective-permute-done | bytes 4640 | tf_op jit(solution)/shard_map/ppermute | solution.py:37
  88.5 0.6 reshape.37.mat_ref
  89.1 6.1 %curls.1 = (bf16[81,96,128]{2,1,0:T(8,128)(2,1)}, f32[8,128]{1,0:T(8,128)}) custom-call(f32[4,9]{1,0:T(4,128)} %reshape.36.eps_ref, s32[36,128]{1,0:T(8,128)} %reshape.37.mat_ref, bf16[81,96,128]{2,1,0:T(8,128)(2,1)} %bitcast.40, bf16[18,96,128]{2,1,0:T(8,128)(2,1)} %copy-done.4, bf16[27,96,128]{2,1,0:T(8,128)(2,1)} %copy-done.2), custom_call_target="tpu_custom_call" | custom-call | flops 60000000 | bytes 5000000 | tf_op jit(solution)/shard_map/curls/pallas_call | solution.py:385
  95.2 1.4 copy-done.3
  96.6 8.1 %assemble.1.coef_ref = bf16[768,2304]{1,0:T(8,128)(2,1)} custom-call(s32[5]{0:T(128)} %stack.63.place_ref, bf16[8,4,2,2,72,96]{5,4,3,2,1,0:T(8,128)(2,1)} %bitcast.43, bf16[8,4,2,2,72,96]{5,4,3,2,1,0:T(8,128)(2,1)} %bitcast.44), custom_call_target="tpu_custom_call" | custom-call | flops 10000000 | bytes 8000000 | tf_op jit(solution)/shard_map/assemble/pallas_call | solution.py:79
  104.6 20.1 %all-to-all-done.cells_ref = bf16[8,31,96,128]{3,2,1,0:T(8,128)(2,1)} async-done(((bf16[8,31,96,128]{3,2,1,0:T(8,128)(2,1)}), bf16[8,31,96,128]{3,2,1,0:T(8,128)(2,1)}, u32[]{:S(2)}, u32[]{:S(2)}) %all-to-all-start) | async-done | bytes 6094880 | tf_op jit(solution)/shard_map/all_to_all | solution.py:434
  124.8 2.0 %copy-done = bf16[768,2304]{1,0:T(8,128)(2,1)S(1)} copy-done((bf16[768,2304]{1,0:T(8,128)(2,1)S(1)}, bf16[768,2304]{1,0:T(8,128)(2,1)}, u32[]{:S(2)}) %copy-start) | copy-done | bytes 3538968
  126.8 8.7 %rotate.1 = bf16[8,21,96,128]{3,2,1,0:T(8,128)(2,1)S(1)} custom-call(bf16[8,31,96,128]{3,2,1,0:T(8,128)(2,1)} %all-to-all-done.cells_ref, bf16[768,2304]{1,0:T(8,128)(2,1)S(1)} %copy-done, f32[8,128]{1,0:T(8,128)S(1)} %copy-done.1), custom_call_target="tpu_custom_call" | custom-call | flops 4982833152 | bytes 14000000 | tf_op jit(solution)/shard_map/rotate/pallas_call | solution.py:246
  135.5 52.4 %all_to_all.10.parts = bf16[8,21,96,128]{3,2,1,0:T(8,128)(2,1)S(1)} all-to-all(bf16[8,21,96,128]{3,2,1,0:T(8,128)(2,1)S(1)} %rotate.1), channel_id=1, replica_groups=mesh['slab'=32,'blk'=8] {'blk'}, dimensions={0} | all-to-all | bytes 8257536 | tf_op jit(solution)/shard_map/all_to_all | solution.py:443
  187.9 2.1 %unpack.1 = (bf16[81,96,128]{2,1,0:T(8,128)(2,1)}, bf16[81,96,128]{2,1,0:T(8,128)(2,1)}) custom-call(bf16[8,21,96,128]{3,2,1,0:T(8,128)(2,1)S(1)} %all_to_all.10.parts), custom_call_target="tpu_custom_call" | custom-call | tf_op jit(solution)/shard_map/unpack/pallas_call | solution.py:294
  (34 shorter events, 0.1 us)
Async XLA Ops:
  7.2 12.1 %copy-start.9 = (bf16[72,96]{1,0:T(8,128)(2,1)S(1)}, bf16[72,96]{1,0:T(8,128)(2,1)}, u32[]{:S(2)}) copy-start(bf16[72,96]{1,0:T(8,128)(2,1)} %param.9) | copy-start | bytes 41476
  7.2 8.6 %collective-permute-start.1 = (bf16[72,96]{1,0:T(8,128)(2,1)}, bf16[72,96]{1,0:T(8,128)(2,1)S(1)}, u32[]{:S(2)}, u32[]{:S(2)}) collective-permute-start(bf16[72,96]{1,0:T(8,128)(2,1)} %param.9), channel_id=1, source_target_pairs={{0,1},{1,0},{2,3},{3,2},{4,5},{5,4},{6,7},{7,6},{8,9},{9,8},{10,11... | collective-permute-start | bytes 41480 | tf_op jit(solution)/shard_map/ppermute | solution.py:32
  8.8 6.9 %collective-permute-start.2 = (bf16[72,96]{1,0:T(8,128)(2,1)}, bf16[72,96]{1,0:T(8,128)(2,1)S(1)}, u32[]{:S(2)}, u32[]{:S(2)}) collective-permute-start(bf16[72,96]{1,0:T(8,128)(2,1)} %param.9), channel_id=1, source_target_pairs={{0,128},{8,136},{16,144},{24,152},{32,160},{40,168},{48,176},{56,1... | collective-permute-start | bytes 41480 | tf_op jit(solution)/shard_map/ppermute | solution.py:32
  11.7 5.2 %collective-permute-start.3 = (bf16[72,96]{1,0:T(8,128)(2,1)}, bf16[72,96]{1,0:T(8,128)(2,1)S(1)}, u32[]{:S(2)}, u32[]{:S(2)}) collective-permute-start(bf16[72,96]{1,0:T(8,128)(2,1)} %param.9), channel_id=1, source_target_pairs={{0,129},{1,128},{2,131},{3,130},{4,133},{5,132},{6,135},{7,134},{8... | collective-permute-start | bytes 41480 | tf_op jit(solution)/shard_map/ppermute | solution.py:45
  15.7 1.2 copy-start.5
  15.7 1.2 copy-start.6
  16.9 0.6 copy-start.7
  17.5 14.7 %collective-permute-start.5 = (bf16[27,96,128]{2,1,0:T(8,128)(2,1)}, bf16[27,96,128]{2,1,0:T(8,128)(2,1)S(1)}, u32[]{:S(2)}, u32[]{:S(2)}) collective-permute-start(bf16[27,96,128]{2,1,0:T(8,128)(2,1)} %get-tuple-element.12), channel_id=1, source_target_pairs={{0,8},{8,16},{16,24},{24,32},{32,40},{40,48},{48,56},{56,64},{64,7... | collective-permute-start | bytes 1990664 | tf_op jit(solution)/shard_map/ppermute | solution.py:37
  17.5 14.7 %collective-permute-start.4 = (bf16[18,96,128]{2,1,0:T(8,128)(2,1)}, bf16[18,96,128]{2,1,0:T(8,128)(2,1)S(1)}, u32[]{:S(2)}, u32[]{:S(2)}) collective-permute-start(bf16[18,96,128]{2,1,0:T(8,128)(2,1)} %get-tuple-element.11), channel_id=1, source_target_pairs={{0,248},{8,0},{16,8},{24,16},{32,24},{40,32},{48,40},{56,48},{64,5... | collective-permute-start | bytes 1327112 | tf_op jit(solution)/shard_map/ppermute | solution.py:37
  20.1 11.3 %collective-permute-start.8 = (bf16[4,72,96]{2,1,0:T(8,128)(2,1)S(1)}, bf16[4,72,96]{2,1,0:T(8,128)(2,1)S(1)}, u32[]{:S(2)}, u32[]{:S(2)}) collective-permute-start(bf16[4,72,96]{2,1,0:T(8,128)(2,1)S(1)} %get-tuple-element.20), channel_id=1, source_target_pairs={{0,2},{1,3},{2,4},{3,5},{4,6},{5,7},{6,0},{7,1},{8,10},{9,11},{10,... | collective-permute-start | bytes 165896 | tf_op jit(solution)/shard_map/ppermute | solution.py:32
  21.6 9.7 %collective-permute-start.7 = (bf16[4,72,96]{2,1,0:T(8,128)(2,1)S(1)}, bf16[4,72,96]{2,1,0:T(8,128)(2,1)S(1)}, u32[]{:S(2)}, u32[]{:S(2)}) collective-permute-start(bf16[4,72,96]{2,1,0:T(8,128)(2,1)S(1)} %get-tuple-element.20), channel_id=1, source_target_pairs={{0,4},{1,5},{2,6},{3,7},{4,0},{5,1},{6,2},{7,3},{8,12},{9,13},{10,... | collective-permute-start | bytes 165896 | tf_op jit(solution)/shard_map/ppermute | solution.py:32
  24.4 7.0 %collective-permute-start.6 = (bf16[4,72,96]{2,1,0:T(8,128)(2,1)S(1)}, bf16[4,72,96]{2,1,0:T(8,128)(2,1)S(1)}, u32[]{:S(2)}, u32[]{:S(2)}) collective-permute-start(bf16[4,72,96]{2,1,0:T(8,128)(2,1)S(1)} %get-tuple-element.20), channel_id=1, source_target_pairs={{0,6},{1,7},{2,0},{3,1},{4,2},{5,3},{6,4},{7,5},{8,14},{9,15},{10,... | collective-permute-start | bytes 165896 | tf_op jit(solution)/shard_map/ppermute | solution.py:32
  32.2 0.8 copy-start.4
  32.9 0.8 copy-start.2
  33.8 50.6 %copy-start.8 = (s32[3,9,128]{2,0,1:T(4,128)S(1)}, s32[3,9,128]{2,0,1:T(4,128)}, u32[]{:S(2)}) copy-start(s32[3,9,128]{2,0,1:T(4,128)} %param.10) | copy-start | bytes 41476
  33.8 51.2 %copy-start.10 = (f32[4,3,3]{2,0,1:T(4,128)S(1)}, f32[4,3,3]{2,0,1:T(4,128)}, u32[]{:S(2)}) copy-start(f32[4,3,3]{2,0,1:T(4,128)} %param.11) | copy-start | bytes 436
  33.8 91.0 %all-to-all-start = ((bf16[8,31,96,128]{3,2,1,0:T(8,128)(2,1)}), bf16[8,31,96,128]{3,2,1,0:T(8,128)(2,1)}, u32[]{:S(2)}, u32[]{:S(2)}) async-start(bf16[8,31,96,128]{3,2,1,0:T(8,128)(2,1)} %hold.3), calls=%async_computation | async-start | bytes 12189696 | tf_op jit(solution)/shard_map/all_to_all | solution.py:434
  38.7 45.7 %all-gather.3.cloned.1.call-start = ((), (), s32[]{:S(2)}) async-start(), calls=%async_computation.2 | async-start | bytes 2654208 | tf_op jit(solution)/shard_map/all_gather | solution.py:436
  84.3 10.9 %collective-permute-start.9 = (bf16[8,4,4,72,96]{4,3,2,1,0:T(8,128)(2,1)}, bf16[8,4,4,72,96]{4,3,2,1,0:T(8,128)(2,1)S(1)}, u32[]{:S(2)}, u32[]{:S(2)}) collective-permute-start(bf16[8,4,4,72,96]{4,3,2,1,0:T(8,128)(2,1)} %bitcast.42), channel_id=1, source_target_pairs={{0,8},{8,0},{16,24},{24,16},{32,40},{40,32},{48,56},{56,48},{64,72... | collective-permute-start | bytes 5308424 | tf_op jit(solution)/shard_map/ppermute | solution.py:32
  84.4 4.2 %collective-permute-start = (s32[1,9,128]{2,0,1:T(1,128)S(1)}, s32[1,9,128]{2,0,1:T(1,128)S(1)}, u32[]{:S(2)}, u32[]{:S(2)}) collective-permute-start(s32[1,9,128]{2,0,1:T(1,128)S(1)} %slice.9), channel_id=1, source_target_pairs={{0,8},{8,16},{16,24},{24,32},{32,40},{40,48},{48,56},{56,64},{64,7... | collective-permute-start | bytes 13832 | tf_op jit(solution)/shard_map/ppermute | solution.py:37
  95.2 1.4 copy-start.3
  96.6 28.2 %copy-start.1 = (f32[8,128]{1,0:T(8,128)S(1)}, f32[8,128]{1,0:T(8,128)}, u32[]{:S(2)}) copy-start(f32[8,128]{1,0:T(8,128)} %get-tuple-element.16.after_ref) | copy-start | bytes 12292
  124.8 2.0 %copy-start = (bf16[768,2304]{1,0:T(8,128)(2,1)S(1)}, bf16[768,2304]{1,0:T(8,128)(2,1)}, u32[]{:S(2)}) copy-start(bf16[768,2304]{1,0:T(8,128)(2,1)} %assemble.1.coef_ref) | copy-start | bytes 10616836
Sparse Core Ops, SparseCore 0:
  41.9 42.4 all-gather.2

commit v6 on v5

--- a/solution.py
+++ b/solution.py
@@ -53,8 +53,7 @@
         )
     )
     t = jnp.stack(pieces)
-    plane = jnp.stack([t] + [move(t, "blk", BLK, (-k, 0)) for k in (1, 2, 3)])
-    return plane, pieces[1:]
+    return jnp.stack([t] + [move(t, "blk", BLK, (-k, 0)) for k in (1, 2, 3)])
 
 
 def assemble_kernel(place_ref, mine_ref, other_ref, out_ref):
@@ -421,23 +420,22 @@
     w, p, x = as_rows(search), as_rows(previous), as_rows(current)
     slab, blk = lax.axis_index("slab"), lax.axis_index("blk")
     place = jnp.stack([slab // 16, (slab // 2) % 8, slab % 2, blk // 2, blk % 2])
-    plane, first = gather_plane(coefficients)
-    layers = w.reshape(3, NZ, NY, V, 128)
-    low = layers[:2, 0].reshape(2 * NY, V, 128)
-    high = layers[:, NZ - 1].reshape(3 * NY, V, 128)
-    low, high = hold([low, high], first)
-    below = ring_shift(high, "slab", 1)
-    above = ring_shift(low, "slab", -1)
+    mark_below = ring_shift(material[NZ - 1 :], "slab", 1)
+    marks = jnp.concatenate([mark_below, material]).reshape((NZ + 1) * NY, 128)
     packed = pack(w, p, x)
+    plane = gather_plane(coefficients)
     packed, plane = lax.optimization_barrier((packed, plane))
-    (packed,) = hold([packed], [below, above])
     cells = lax.all_to_all(packed, "blk", split_axis=0, concat_axis=0, tiled=True)
     groups = [[h * 16 + z * 2 + c for z in range(8)] for h in range(2) for c in range(2)]
     mine = lax.all_gather(plane, "slab", axis_index_groups=groups)
     other = move(mine, "slab", SLAB, (0, 0, 1))
     coef = assemble(place, mine, other)
-    mark_below = ring_shift(material[NZ - 1 :], "slab", 1)
-    marks = jnp.concatenate([mark_below, material]).reshape((NZ + 1) * NY, 128)
+    layers = w.reshape(3, NZ, NY, V, 128)
+    low = layers[:2, 0].reshape(2 * NY, V, 128)
+    high = layers[:, NZ - 1].reshape(3 * NY, V, 128)
+    low, high = hold([low, high], [mine])
+    above = ring_shift(low, "slab", -1)
+    below = ring_shift(high, "slab", 1)
     applied, token = apply_curls(w, above, below, marks, inverse_permittivity.reshape(NMAT, 9))
     parts = rotate(cells, coef, token)
     back = lax.all_to_all(parts, "blk", split_axis=0, concat_axis=0, tiled=True)

time: 198 us -> 192 us (0.970)
  the two profiles are of different devices: /device:TPU:96 before, /device:TPU:16 now
where the time goes in v6:
time: 192 us; the launch traced here: 190 us
  waiting for transfers between devices  69.2 us (36%)
  blocking collectives  49.2 us (26%)
  Pallas kernels  30.4 us (16%)
  starting transfers between devices  18.4 us (10%)
  between operations  14.2 us (7%)
  local copies, waits for them, and re-layouts  7.1 us (4%)
    all_to_all x1, blocking collectives, per_device(): back = lax.all_to_all(parts, 'blk', split_axis=0, concat_axis=0, tiled=True)  49.2 us
    all_gather x1, waiting for transfers between devices, per_device(): mine = lax.all_gather(plane, 'slab', axis_index_groups=groups)  47.8 us
    ppermute x3, waiting for transfers between devices, ring_shift(): return lax.ppermute(x, axis, [(i, (i + by) % count) for i in range(count)])  15 us
    pallas_call x1, Pallas kernels, rotate(): pl.pallas_call(rotate_kernel, out_shape=jax.ShapeDtypeStruct((NB, 2 * SHA...  8.74 us
    pallas_call x1, Pallas kernels, assemble(): pl.pallas_call(assemble_kernel, out_shape=jax.ShapeDtypeStruct((M, 3 * M)...  7.94 us
    ppermute x6, starting transfers between devices, move(): return lax.ppermute(x, axis, pairs)  6.62 us
    pallas_call x1, Pallas kernels, apply_curls(): pl.pallas_call(curl_kernel, out_shape=(jax.ShapeDtypeStruct((ROWS, V, 128...  6.05 us
    pallas_call x1, Pallas kernels, pack(): pl.pallas_call(pack_kernel, out_shape=jax.ShapeDtypeStruct(shape, jnp.bfl...  5.58 us
  transfers between devices with their start and end apart: 12, of which 5 were waited for; matrix products, arithmetic and copies ran while one was open for 2% of the time, Pallas kernels for 10%

profile of v6, /device:TPU:16, one launch (start us, length us, event | category | flops | bytes accessed | tf_op | source)
XLA Modules:
  0.0 190.2 jit_solution(8051153464590645115)
XLA Ops:
  7.2 1.4 collective-permute-start.1
  8.5 1.4 collective-permute-start.3
  9.9 1.5 collective-permute-start.2
  11.3 1.3 collective-permute-done.3
  12.7 2.7 %collective-permute-done.2 = bf16[72,96]{1,0:T(8,128)(2,1)S(1)} collective-permute-done((bf16[72,96]{1,0:T(8,128)(2,1)}, bf16[72,96]{1,0:T(8,128)(2,1)S(1)}, u32[]{:S(2)}, u32[]{:S(2)}) %collective-permute-start.2) | collective-permute-done | bytes 13856 | tf_op jit(solution)/shard_map/ppermute | solution.py:32
  15.4 0.7 fusion
  16.1 1.8 collective-permute-start.5
  17.9 1.1 collective-permute-start.4
  19.0 0.9 collective-permute-start.6
  19.9 5.6 %pack.1 = bf16[8,31,96,128]{3,2,1,0:T(8,128)(2,1)} custom-call(bf16[81,96,128]{2,1,0:T(8,128)(2,1)} %bitcast.37, bf16[81,96,128]{2,1,0:T(8,128)(2,1)} %bitcast.45, bf16[81,96,128]{2,1,0:T(8,128)(2,1)} %bitcast.46), custom_call_target="tpu_custom_call" | custom-call | flops 2000000 | bytes 12000000 | tf_op jit(solution)/shard_map/pack/pallas_call | solution.py:148
  25.5 0.8 pad_maximum_fusion
  26.3 5.0 %all-to-all-start = ((bf16[8,31,96,128]{3,2,1,0:T(8,128)(2,1)}), bf16[8,31,96,128]{3,2,1,0:T(8,128)(2,1)}, u32[]{:S(2)}, u32[]{:S(2)}) async-start(bf16[8,31,96,128]{3,2,1,0:T(8,128)(2,1)} %pack.1), calls=%async_computation | async-start | bytes 12189696 | tf_op jit(solution)/shard_map/all_to_all | solution.py:428
  31.3 0.7 all-gather.3.cloned.1.call-update
  32.0 47.8 %all-gather.3.cloned.1.call-done = bf16[32,4,72,96]{3,2,1,0:T(8,128)(2,1)} async-done(((bf16[4,4,72,96]{3,2,1,0:T(8,128)(2,1)}), bf16[32,4,72,96]{3,2,1,0:T(8,128)(2,1)}) %all-gather.3.cloned.1.call-update) | async-done | bytes 1769488 | tf_op jit(solution)/shard_map/all_gather | solution.py:430
  79.8 0.8 slice.12
  80.6 0.9 slice.13
  81.5 0.5 collective-permute-start.8
  82.0 4.9 %collective-permute-start.7 = (bf16[18,96,128]{2,1,0:T(8,128)(2,1)}, bf16[18,96,128]{2,1,0:T(8,128)(2,1)S(1)}, u32[]{:S(2)}, u32[]{:S(2)}) collective-permute-start(bf16[18,96,128]{2,1,0:T(8,128)(2,1)} %get-tuple-element.12), channel_id=1, source_target_pairs={{0,248},{8,0},{16,8},{24,16},{32,24},{40,32},{48,40},{56,48},{64,5... | collective-permute-start | bytes 1327112 | tf_op jit(solution)/shard_map/ppermute | solution.py:37
  86.8 0.1 collective-permute-start
  87.0 0.6 reshape.36.eps_ref
  87.7 0.6 stack.63.place_ref
  88.2 15.0 %collective-permute-done = s32[1,9,128]{2,0,1:T(1,128)S(1)} collective-permute-done((s32[1,9,128]{2,0,1:T(1,128)S(1)}, s32[1,9,128]{2,0,1:T(1,128)S(1)}, u32[]{:S(2)}, u32[]{:S(2)}) %collective-permute-start) | collective-permute-done | bytes 4640 | tf_op jit(solution)/shard_map/ppermute | solution.py:37
  103.3 0.6 reshape.37.mat_ref
  103.9 0.8 copy-done.4
  104.7 0.8 copy-done.3
  105.5 6.1 %curls.1 = (bf16[81,96,128]{2,1,0:T(8,128)(2,1)}, f32[8,128]{1,0:T(8,128)}) custom-call(f32[4,9]{1,0:T(4,128)} %reshape.36.eps_ref, s32[36,128]{1,0:T(8,128)} %reshape.37.mat_ref, bf16[81,96,128]{2,1,0:T(8,128)(2,1)} %bitcast.38, bf16[18,96,128]{2,1,0:T(8,128)(2,1)} %copy-done.4, bf16[27,96,128]{2,1,0:T(8,128)(2,1)} %copy-done.3), custom_call_target="tpu_custom_call" | custom-call | flops 60000000 | bytes 5000000 | tf_op jit(solution)/shard_map/curls/pallas_call | solution.py:384
  111.5 7.9 %assemble.1.coef_ref = bf16[768,2304]{1,0:T(8,128)(2,1)} custom-call(s32[5]{0:T(128)} %stack.63.place_ref, bf16[8,4,2,2,72,96]{5,4,3,2,1,0:T(8,128)(2,1)} %bitcast.43, bf16[8,4,2,2,72,96]{5,4,3,2,1,0:T(8,128)(2,1)} %bitcast.26.other_ref), custom_call_target="tpu_custom_call" | custom-call | flops 10000000 | bytes 8000000 | tf_op jit(solution)/shard_map/assemble/pallas_call | solution.py:78
  119.5 1.7 all-to-all-done.cells_ref
  121.2 2.0 %copy-done = bf16[768,2304]{1,0:T(8,128)(2,1)S(1)} copy-done((bf16[768,2304]{1,0:T(8,128)(2,1)S(1)}, bf16[768,2304]{1,0:T(8,128)(2,1)}, u32[]{:S(2)}) %copy-start) | copy-done | bytes 3538968
  123.2 8.7 %rotate.1 = bf16[8,21,96,128]{3,2,1,0:T(8,128)(2,1)S(1)} custom-call(bf16[8,31,96,128]{3,2,1,0:T(8,128)(2,1)} %all-to-all-done.cells_ref, bf16[768,2304]{1,0:T(8,128)(2,1)S(1)} %copy-done, f32[8,128]{1,0:T(8,128)S(1)} %copy-done.1), custom_call_target="tpu_custom_call" | custom-call | flops 4982833152 | bytes 14000000 | tf_op jit(solution)/shard_map/rotate/pallas_call | solution.py:245
  131.9 49.2 %all_to_all.10.parts = bf16[8,21,96,128]{3,2,1,0:T(8,128)(2,1)S(1)} all-to-all(bf16[8,21,96,128]{3,2,1,0:T(8,128)(2,1)S(1)} %rotate.1), channel_id=1, replica_groups=mesh['slab'=32,'blk'=8] {'blk'}, dimensions={0} | all-to-all | bytes 8257536 | tf_op jit(solution)/shard_map/all_to_all | solution.py:441
  181.2 2.1 %unpack.1 = (bf16[81,96,128]{2,1,0:T(8,128)(2,1)}, bf16[81,96,128]{2,1,0:T(8,128)(2,1)}) custom-call(bf16[8,21,96,128]{3,2,1,0:T(8,128)(2,1)S(1)} %all_to_all.10.parts), custom_call_target="tpu_custom_call" | custom-call | tf_op jit(solution)/shard_map/unpack/pallas_call | solution.py:293
  (25 shorter events, 0.1 us)
Async XLA Ops:
  7.2 4.2 %collective-permute-start.1 = (bf16[72,96]{1,0:T(8,128)(2,1)}, bf16[72,96]{1,0:T(8,128)(2,1)S(1)}, u32[]{:S(2)}, u32[]{:S(2)}) collective-permute-start(bf16[72,96]{1,0:T(8,128)(2,1)} %param.9), channel_id=1, source_target_pairs={{0,1},{1,0},{2,3},{3,2},{4,5},{5,4},{6,7},{7,6},{8,9},{9,8},{10,11... | collective-permute-start | bytes 41480 | tf_op jit(solution)/shard_map/ppermute | solution.py:32
  8.5 4.2 %collective-permute-start.3 = (bf16[72,96]{1,0:T(8,128)(2,1)}, bf16[72,96]{1,0:T(8,128)(2,1)S(1)}, u32[]{:S(2)}, u32[]{:S(2)}) collective-permute-start(bf16[72,96]{1,0:T(8,128)(2,1)} %param.9), channel_id=1, source_target_pairs={{0,129},{1,128},{2,131},{3,130},{4,133},{5,132},{6,135},{7,134},{8... | collective-permute-start | bytes 41480 | tf_op jit(solution)/shard_map/ppermute | solution.py:45
  9.9 5.5 %collective-permute-start.2 = (bf16[72,96]{1,0:T(8,128)(2,1)}, bf16[72,96]{1,0:T(8,128)(2,1)S(1)}, u32[]{:S(2)}, u32[]{:S(2)}) collective-permute-start(bf16[72,96]{1,0:T(8,128)(2,1)} %param.9), channel_id=1, source_target_pairs={{0,128},{8,136},{16,144},{24,152},{32,160},{40,168},{48,176},{56,1... | collective-permute-start | bytes 41480 | tf_op jit(solution)/shard_map/ppermute | solution.py:32
  16.1 9.4 %collective-permute-start.5 = (bf16[4,72,96]{2,1,0:T(8,128)(2,1)S(1)}, bf16[4,72,96]{2,1,0:T(8,128)(2,1)S(1)}, u32[]{:S(2)}, u32[]{:S(2)}) collective-permute-start(bf16[4,72,96]{2,1,0:T(8,128)(2,1)S(1)} %get-tuple-element.20), channel_id=1, source_target_pairs={{0,4},{1,5},{2,6},{3,7},{4,0},{5,1},{6,2},{7,3},{8,12},{9,13},{10,... | collective-permute-start | bytes 165896 | tf_op jit(solution)/shard_map/ppermute | solution.py:32
  17.9 7.6 %collective-permute-start.4 = (bf16[4,72,96]{2,1,0:T(8,128)(2,1)S(1)}, bf16[4,72,96]{2,1,0:T(8,128)(2,1)S(1)}, u32[]{:S(2)}, u32[]{:S(2)}) collective-permute-start(bf16[4,72,96]{2,1,0:T(8,128)(2,1)S(1)} %get-tuple-element.20), channel_id=1, source_target_pairs={{0,6},{1,7},{2,0},{3,1},{4,2},{5,3},{6,4},{7,5},{8,14},{9,15},{10,... | collective-permute-start | bytes 165896 | tf_op jit(solution)/shard_map/ppermute | solution.py:32
  19.0 6.5 %collective-permute-start.6 = (bf16[4,72,96]{2,1,0:T(8,128)(2,1)S(1)}, bf16[4,72,96]{2,1,0:T(8,128)(2,1)S(1)}, u32[]{:S(2)}, u32[]{:S(2)}) collective-permute-start(bf16[4,72,96]{2,1,0:T(8,128)(2,1)S(1)} %get-tuple-element.20), channel_id=1, source_target_pairs={{0,2},{1,3},{2,4},{3,5},{4,6},{5,7},{6,0},{7,1},{8,10},{9,11},{10,... | collective-permute-start | bytes 165896 | tf_op jit(solution)/shard_map/ppermute | solution.py:32
  26.3 53.5 %copy-start.2 = (bf16[96,3,3,9,128]{4,0,3,2,1:T(8,128)(2,1)S(1)}, bf16[96,3,3,9,128]{4,0,3,2,1:T(8,128)(2,1)}, u32[]{:S(2)}) copy-start(bf16[96,3,3,9,128]{4,0,3,2,1:T(8,128)(2,1)} %param.7) | copy-start | bytes 5971972
  26.3 94.9 %all-to-all-start = ((bf16[8,31,96,128]{3,2,1,0:T(8,128)(2,1)}), bf16[8,31,96,128]{3,2,1,0:T(8,128)(2,1)}, u32[]{:S(2)}, u32[]{:S(2)}) async-start(bf16[8,31,96,128]{3,2,1,0:T(8,128)(2,1)} %pack.1), calls=%async_computation | async-start | bytes 12189696 | tf_op jit(solution)/shard_map/all_to_all | solution.py:428
  31.3 48.5 %all-gather.3.cloned.1.call-start = ((), (), s32[]{:S(2)}) async-start(), calls=%async_computation.2 | async-start | bytes 2654208 | tf_op jit(solution)/shard_map/all_gather | solution.py:430
  79.8 31.8 %collective-permute-start.9 = (bf16[8,4,4,72,96]{4,3,2,1,0:T(8,128)(2,1)}, bf16[8,4,4,72,96]{4,3,2,1,0:T(8,128)(2,1)}, u32[]{:S(2)}, u32[]{:S(2)}) collective-permute-start(bf16[8,4,4,72,96]{4,3,2,1,0:T(8,128)(2,1)} %bitcast.41), channel_id=1, source_target_pairs={{0,8},{8,0},{16,24},{24,16},{32,40},{40,32},{48,56},{56,48},{64,72... | collective-permute-start | bytes 5308424 | tf_op jit(solution)/shard_map/ppermute | solution.py:32
  80.6 6.2 %copy-start.5 = (s32[3,9,128]{2,0,1:T(4,128)S(1)}, s32[3,9,128]{2,0,1:T(4,128)}, u32[]{:S(2)}) copy-start(s32[3,9,128]{2,0,1:T(4,128)} %param.10) | copy-start | bytes 41476
  80.6 6.4 %copy-start.6 = (f32[4,3,3]{2,0,1:T(4,128)S(1)}, f32[4,3,3]{2,0,1:T(4,128)}, u32[]{:S(2)}) copy-start(f32[4,3,3]{2,0,1:T(4,128)} %param.11) | copy-start | bytes 436
  81.5 22.4 %collective-permute-start.8 = (bf16[27,96,128]{2,1,0:T(8,128)(2,1)}, bf16[27,96,128]{2,1,0:T(8,128)(2,1)S(1)}, u32[]{:S(2)}, u32[]{:S(2)}) collective-permute-start(bf16[27,96,128]{2,1,0:T(8,128)(2,1)} %get-tuple-element.13), channel_id=1, source_target_pairs={{0,8},{8,16},{16,24},{24,32},{32,40},{40,48},{48,56},{56,64},{64,7... | collective-permute-start | bytes 1990664 | tf_op jit(solution)/shard_map/ppermute | solution.py:37
  82.0 21.9 %collective-permute-start.7 = (bf16[18,96,128]{2,1,0:T(8,128)(2,1)}, bf16[18,96,128]{2,1,0:T(8,128)(2,1)S(1)}, u32[]{:S(2)}, u32[]{:S(2)}) collective-permute-start(bf16[18,96,128]{2,1,0:T(8,128)(2,1)} %get-tuple-element.12), channel_id=1, source_target_pairs={{0,248},{8,0},{16,8},{24,16},{32,24},{40,32},{48,40},{56,48},{64,5... | collective-permute-start | bytes 1327112 | tf_op jit(solution)/shard_map/ppermute | solution.py:37
  86.8 16.4 %collective-permute-start = (s32[1,9,128]{2,0,1:T(1,128)S(1)}, s32[1,9,128]{2,0,1:T(1,128)S(1)}, u32[]{:S(2)}, u32[]{:S(2)}) collective-permute-start(s32[1,9,128]{2,0,1:T(1,128)S(1)} %slice.9), channel_id=1, source_target_pairs={{0,8},{8,16},{16,24},{24,32},{32,40},{40,48},{48,56},{56,64},{64,7... | collective-permute-start | bytes 13832 | tf_op jit(solution)/shard_map/ppermute | solution.py:37
  103.9 0.8 copy-start.4
  104.6 0.8 copy-start.3
  111.5 9.6 %copy-start.1 = (f32[8,128]{1,0:T(8,128)S(1)}, f32[8,128]{1,0:T(8,128)}, u32[]{:S(2)}) copy-start(f32[8,128]{1,0:T(8,128)} %get-tuple-element.16.after_ref) | copy-start | bytes 12292
  121.2 2.0 %copy-start = (bf16[768,2304]{1,0:T(8,128)(2,1)S(1)}, bf16[768,2304]{1,0:T(8,128)(2,1)}, u32[]{:S(2)}) copy-start(bf16[768,2304]{1,0:T(8,128)(2,1)} %assemble.1.coef_ref) | copy-start | bytes 10616836
Sparse Core Ops, SparseCore 0:
  34.5 45.2 all-gather.2

commit v7 on v6

--- a/solution.py
+++ b/solution.py
@@ -15,6 +15,8 @@
 ROWS = 81
 SHARE = 10
 LANES = 128 // NB
+PART = SHARE * V
+HALF = V // 2
 SLAB = (2, 8, 2)
 BLK = (4, 2)
 ANY = pl.BlockSpec(memory_space=pl.ANY)
@@ -101,17 +103,28 @@
     return x if by == 0 else pltpu.roll(x, by, x.ndim - 1)
 
 
+def folded(row):
+    lower = row[..., HALF:, :]
+    shifted = rolled(lower.reshape(-1, 128), 64).reshape(lower.shape)
+    return jnp.where(lane_index(lower.shape) < 64, row[..., :HALF, :], shifted)
+
+
+def unfolded(half):
+    shifted = rolled(half.reshape(-1, 128), 64).reshape(half.shape)
+    return jnp.concatenate([half, shifted], axis=-2)
+
+
 def pack_kernel(w_ref, p_ref, x_ref, out_ref, stage, tail, in_sems, tail_sems, out_sems):
     fields = (w_ref, p_ref, x_ref)
     last = [
-        pltpu.make_async_copy(ref.at[ROWS - 1], tail.at[k], tail_sems.at[k])
+        pltpu.make_async_copy(ref.at[pl.ds((ROWS - 1) * V, V)], tail.at[k], tail_sems.at[k])
         for k, ref in enumerate(fields)
     ]
     fetches = [
         [
             pltpu.make_async_copy(
-                ref.at[pl.ds(SHARE * d, SHARE)],
-                stage.at[d, pl.ds(SHARE * k, SHARE)],
+                ref.at[pl.ds(PART * d, PART)],
+                stage.at[d, pl.ds(PART * k, PART)],
                 in_sems.at[d, k],
             )
             for k, ref in enumerate(fields)
@@ -135,7 +148,7 @@
         row = jnp.where(lane < 3 * LANES, rolled(x, LANES * (2 - d)), 0.0)
         row = jnp.where(lane < 2 * LANES, rolled(p, LANES * (1 - d)), row)
         row = jnp.where(lane < LANES, rolled(w, LANES * (0 - d)), row)
-        stage[d, 3 * SHARE] = row.astype(jnp.bfloat16)
+        stage[d, 3 * PART :] = folded(row).astype(jnp.bfloat16)
         for c in fetches[d]:
             c.wait()
         sends[d].start()
@@ -144,7 +157,7 @@
 
 
 def pack(w, p, x):
-    shape = (NB, 3 * SHARE + 1, V, 128)
+    shape = (NB, 3 * PART + HALF, 128)
     return pl.pallas_call(
         pack_kernel,
         out_shape=jax.ShapeDtypeStruct(shape, jnp.bfloat16),
@@ -162,33 +175,33 @@
             flops=2_000_000, bytes_accessed=12_000_000, transcendentals=0
         ),
         name="pack",
-    )(w, p, x)
+    )(*(t.reshape(ROWS * V, 128) for t in (w, p, x)))
 
 
 def rotate_kernel(cells_ref, coef_ref, after_ref, out_ref, cells, out, in_sems, out_sems):
     del after_ref
 
     def fetch(k, i):
-        rows = pl.ds(SHARE * k + 2 * i, 2)
+        rows = pl.ds(pl.multiple_of(PART * k + 2 * V * i, 2 * V), 2 * V)
         return pltpu.make_async_copy(
             cells_ref.at[:, rows], cells.at[:, rows], in_sems.at[k, i]
         )
 
     def put(k, i):
-        rows = pl.ds(SHARE * k + 2 * i, 2)
+        rows = pl.ds(pl.multiple_of(PART * k + 2 * V * i, 2 * V), 2 * V)
         return pltpu.make_async_copy(
             out.at[:, rows], out_ref.at[:, rows], out_sems.at[k, i]
         )
 
     steps = SHARE // 2
     fetch_tail = pltpu.make_async_copy(
-        cells_ref.at[:, pl.ds(3 * SHARE, 1)],
-        cells.at[:, pl.ds(3 * SHARE, 1)],
+        cells_ref.at[:, pl.ds(3 * PART, HALF)],
+        cells.at[:, pl.ds(3 * PART, HALF)],
         in_sems.at[0, steps],
     )
     put_tail = pltpu.make_async_copy(
-        out.at[:, pl.ds(2 * SHARE, 1)],
-        out_ref.at[:, pl.ds(2 * SHARE, 1)],
+        out.at[:, pl.ds(2 * PART, HALF)],
+        out_ref.at[:, pl.ds(2 * PART, HALF)],
         out_sems.at[0, steps],
     )
     for i in range(steps):
@@ -206,34 +219,36 @@
         )
         return direction, rotated
 
+    def row(k, i, j):
+        return pl.ds(pl.multiple_of(PART * k + 2 * V * i + V * j, V), V)
+
     def step(i, carry):
         for k in range(3):
             fetch(k, i).wait()
 
         def row_pair(k):
-            first = cells[:, SHARE * k + 2 * i].reshape(M, 128)
-            second = cells[:, SHARE * k + 2 * i + 1].reshape(M, 128)
-            return jnp.concatenate([first, second], axis=1)
+            pair = [cells[:, row(k, i, j)].reshape(M, 128) for j in range(2)]
+            return jnp.concatenate(pair, axis=1)
 
         results = product(row_pair(0), row_pair(1), row_pair(2))
         for k, result in enumerate(results):
             result = result.astype(jnp.bfloat16)
             for j in range(2):
                 part = result[:, 128 * j : 128 * (j + 1)]
-                out[:, SHARE * k + 2 * i + j] = part.reshape(NB, V, 128)
+                out[:, row(k, i, j)] = part.reshape(NB, V, 128)
             put(k, i).start()
         return carry
 
     lax.fori_loop(0, steps, step, 0)
     fetch_tail.wait()
-    tail = cells[:, 3 * SHARE].reshape(M, 128)
-    wide = tail.astype(jnp.float32)
+    wide = unfolded(cells[:, 3 * PART :].astype(jnp.float32)).reshape(M, 128)
+    tail = wide.astype(jnp.bfloat16)
     shifted = [rolled(wide, -LANES * k).astype(jnp.bfloat16) for k in (1, 2)]
     direction, rotated = product(tail, *shifted)
     mixed = jnp.where(
         lane_index((M, 128)) < LANES, direction, rolled(rotated, LANES)
     )
-    out[:, 2 * SHARE] = mixed.astype(jnp.bfloat16).reshape(NB, V, 128)
+    out[:, 2 * PART :] = folded(mixed.reshape(NB, V, 128)).astype(jnp.bfloat16)
     put_tail.start()
     for k in range(2):
         for i in range(steps):
@@ -244,12 +259,12 @@
 def rotate(cells, coef, after):
     return pl.pallas_call(
         rotate_kernel,
-        out_shape=jax.ShapeDtypeStruct((NB, 2 * SHARE + 1, V, 128), jnp.bfloat16),
+        out_shape=jax.ShapeDtypeStruct((NB, 2 * PART + HALF, 128), jnp.bfloat16),
         in_specs=[ANY, pl.BlockSpec(memory_space=pltpu.VMEM), ANY],
         out_specs=ANY,
         scratch_shapes=[
-            pltpu.VMEM((NB, 3 * SHARE + 1, V, 128), jnp.bfloat16),
-            pltpu.VMEM((NB, 2 * SHARE + 1, V, 128), jnp.bfloat16),
+            pltpu.VMEM((NB, 3 * PART + HALF, 128), jnp.bfloat16),
+            pltpu.VMEM((NB, 2 * PART + HALF, 128), jnp.bfloat16),
             pltpu.SemaphoreType.DMA((3, SHARE // 2 + 1)),
             pltpu.SemaphoreType.DMA((2, SHARE // 2 + 1)),
         ],
@@ -267,8 +282,8 @@
         for k, ref in enumerate((d_ref, r_ref)):
             copies.append(
                 pltpu.make_async_copy(
-                    parts.at[s, pl.ds(SHARE * k, SHARE)],
-                    ref.at[pl.ds(SHARE * s, SHARE)],
+                    parts.at[s, pl.ds(PART * k, PART)],
+                    ref.at[pl.ds(PART * s, PART)],
                     out_sems.at[s, k],
                 )
             )
@@ -276,20 +291,20 @@
     which = lane_index((V, 128)) // LANES
     direction = rotated = jnp.zeros((V, 128), jnp.float32)
     for s in range(NB):
-        row = parts[s, 2 * SHARE].astype(jnp.float32)
+        row = unfolded(parts[s, 2 * PART :].astype(jnp.float32))
         direction = jnp.where(which == s, rolled(row, LANES * s), direction)
         rotated = jnp.where(which == s, rolled(row, LANES * (s - 1)), rotated)
     last[0] = direction.astype(jnp.bfloat16)
     last[1] = rotated.astype(jnp.bfloat16)
     for k, ref in enumerate((d_ref, r_ref)):
-        copies.append(pltpu.make_async_copy(last.at[k], ref.at[ROWS - 1], last_sems.at[k]))
+        copies.append(pltpu.make_async_copy(last.at[k], ref.at[pl.ds((ROWS - 1) * V, V)], last_sems.at[k]))
         copies[-1].start()
     for c in copies:
         c.wait()
 
 
 def unpack(parts):
-    whole = jax.ShapeDtypeStruct((ROWS, V, 128), jnp.bfloat16)
+    whole = jax.ShapeDtypeStruct((ROWS * V, 128), jnp.bfloat16)
     return pl.pallas_call(
         unpack_kernel,
         out_shape=(whole, whole),

time: 192 us -> 189 us (0.984)
  transfers between devices with their start and end apart: 12 -> 12, of which waited for: 5 -> 4; matrix products, arithmetic and copies ran while one was open for 2% -> 2% of each run, Pallas kernels for 10% -> 10%
where the time goes in v7:
time: 189 us; the launch traced here: 187 us
  waiting for transfers between devices  67.5 us (36%)
  blocking collectives  48.3 us (26%)
  Pallas kernels  30.6 us (16%)
  starting transfers between devices  18.4 us (10%)
  between operations  14.2 us (8%)
  local copies, waits for them, and re-layouts  6.54 us (3%)
    all_to_all x1, blocking collectives, per_device(): back = lax.all_to_all(parts, 'blk', split_axis=0, concat_axis=0, tiled=True)  48.3 us
    all_gather x1, waiting for transfers between devices, per_device(): mine = lax.all_gather(plane, 'slab', axis_index_groups=groups)  47.7 us
    ppermute x3, waiting for transfers between devices, ring_shift(): return lax.ppermute(x, axis, [(i, (i + by) % count) for i in range(count)])  15 us
    pallas_call x1, Pallas kernels, rotate(): pl.pallas_call(rotate_kernel, out_shape=jax.ShapeDtypeStruct((NB, 2 * PAR...  8.99 us
    pallas_call x1, Pallas kernels, assemble(): pl.pallas_call(assemble_kernel, out_shape=jax.ShapeDtypeStruct((M, 3 * M)...  7.93 us
    ppermute x6, starting transfers between devices, move(): return lax.ppermute(x, axis, pairs)  6.62 us
    pallas_call x1, Pallas kernels, apply_curls(): pl.pallas_call(curl_kernel, out_shape=(jax.ShapeDtypeStruct((ROWS, V, 128...  6.05 us
    pallas_call x1, Pallas kernels, pack(): pl.pallas_call(pack_kernel, out_shape=jax.ShapeDtypeStruct(shape, jnp.bfl...  5.6 us
  transfers between devices with their start and end apart: 12, of which 4 were waited for; matrix products, arithmetic and copies ran while one was open for 2% of the time, Pallas kernels for 10%

profile of v7, /device:TPU:16, one launch (start us, length us, event | category | flops | bytes accessed | tf_op | source)
XLA Modules:
  0.0 187.2 jit_solution(16057635036805026987)
XLA Ops:
  7.2 1.4 collective-permute-start.1
  8.5 1.4 collective-permute-start.3
  9.9 1.5 collective-permute-start.2
  11.3 1.3 collective-permute-done.3
  12.7 2.7 %collective-permute-done.2 = bf16[72,96]{1,0:T(8,128)(2,1)S(1)} collective-permute-done((bf16[72,96]{1,0:T(8,128)(2,1)}, bf16[72,96]{1,0:T(8,128)(2,1)S(1)}, u32[]{:S(2)}, u32[]{:S(2)}) %collective-permute-start.2) | collective-permute-done | bytes 13856 | tf_op jit(solution)/shard_map/ppermute | solution.py:34
  15.4 0.7 fusion
  16.1 1.8 collective-permute-start.5
  17.9 1.1 collective-permute-start.4
  19.0 0.9 collective-permute-start.6
  19.9 5.6 %pack.1 = bf16[8,2928,128]{2,1,0:T(8,128)(2,1)} custom-call(bf16[7776,128]{1,0:T(8,128)(2,1)} %bitcast.39, bf16[7776,128]{1,0:T(8,128)(2,1)} %bitcast.47, bf16[7776,128]{1,0:T(8,128)(2,1)} %bitcast.48), custom_call_target="tpu_custom_call" | custom-call | flops 2000000 | bytes 12000000 | tf_op jit(solution)/shard_map/pack/pallas_call | solution.py:161
  25.5 0.8 pad_maximum_fusion
  26.3 5.0 %all-to-all-start = ((bf16[8,2928,128]{2,1,0:T(8,128)(2,1)}), bf16[8,2928,128]{2,1,0:T(8,128)(2,1)}, u32[]{:S(2)}, u32[]{:S(2)}) async-start(bf16[8,2928,128]{2,1,0:T(8,128)(2,1)} %pack.1), calls=%async_computation | async-start | bytes 11993088 | tf_op jit(solution)/shard_map/all_to_all | solution.py:443
  31.4 0.7 all-gather.3.cloned.1.call-update
  32.1 47.7 %all-gather.3.cloned.1.call-done = bf16[32,4,72,96]{3,2,1,0:T(8,128)(2,1)} async-done(((bf16[4,4,72,96]{3,2,1,0:T(8,128)(2,1)}), bf16[32,4,72,96]{3,2,1,0:T(8,128)(2,1)}) %all-gather.3.cloned.1.call-update) | async-done | bytes 1769488 | tf_op jit(solution)/shard_map/all_gather | solution.py:445
  79.8 0.8 slice.12
  80.6 0.9 slice.13
  81.5 0.5 collective-permute-start.8
  82.0 4.9 %collective-permute-start.7 = (bf16[18,96,128]{2,1,0:T(8,128)(2,1)}, bf16[18,96,128]{2,1,0:T(8,128)(2,1)S(1)}, u32[]{:S(2)}, u32[]{:S(2)}) collective-permute-start(bf16[18,96,128]{2,1,0:T(8,128)(2,1)} %get-tuple-element.12), channel_id=1, source_target_pairs={{0,248},{8,0},{16,8},{24,16},{32,24},{40,32},{48,40},{56,48},{64,5... | collective-permute-start | bytes 1327112 | tf_op jit(solution)/shard_map/ppermute | solution.py:39
  86.9 0.1 collective-permute-start
  87.0 0.6 reshape.30.eps_ref
  87.7 0.7 stack.63.place_ref
  88.3 15.0 %collective-permute-done = s32[1,9,128]{2,0,1:T(1,128)S(1)} collective-permute-done((s32[1,9,128]{2,0,1:T(1,128)S(1)}, s32[1,9,128]{2,0,1:T(1,128)S(1)}, u32[]{:S(2)}, u32[]{:S(2)}) %collective-permute-start) | collective-permute-done | bytes 4640 | tf_op jit(solution)/shard_map/ppermute | solution.py:39
  103.3 0.6 reshape.31.mat_ref
  103.9 0.7 copy-done.4
  104.7 0.2 copy-done.3
  104.9 6.1 %curls.1 = (bf16[81,96,128]{2,1,0:T(8,128)(2,1)}, f32[8,128]{1,0:T(8,128)}) custom-call(f32[4,9]{1,0:T(4,128)} %reshape.30.eps_ref, s32[36,128]{1,0:T(8,128)} %reshape.31.mat_ref, bf16[81,96,128]{2,1,0:T(8,128)(2,1)} %bitcast.40, bf16[18,96,128]{2,1,0:T(8,128)(2,1)} %copy-done.4, bf16[27,96,128]{2,1,0:T(8,128)(2,1)} %copy-done.3), custom_call_target="tpu_custom_call" | custom-call | flops 60000000 | bytes 5000000 | tf_op jit(solution)/shard_map/curls/pallas_call | solution.py:399
  111.0 7.9 %assemble.1.coef_ref = bf16[768,2304]{1,0:T(8,128)(2,1)} custom-call(s32[5]{0:T(128)} %stack.63.place_ref, bf16[8,4,2,2,72,96]{5,4,3,2,1,0:T(8,128)(2,1)} %bitcast.45, bf16[8,4,2,2,72,96]{5,4,3,2,1,0:T(8,128)(2,1)} %bitcast.26.other_ref), custom_call_target="tpu_custom_call" | custom-call | flops 10000000 | bytes 8000000 | tf_op jit(solution)/shard_map/assemble/pallas_call | solution.py:80
  118.9 0.0 all-to-all-done.cells_ref
  118.9 2.0 %copy-done = bf16[768,2304]{1,0:T(8,128)(2,1)S(1)} copy-done((bf16[768,2304]{1,0:T(8,128)(2,1)S(1)}, bf16[768,2304]{1,0:T(8,128)(2,1)}, u32[]{:S(2)}) %copy-start) | copy-done | bytes 3538968
  120.9 9.0 %rotate.1 = bf16[8,1968,128]{2,1,0:T(8,128)(2,1)S(1)} custom-call(bf16[8,2928,128]{2,1,0:T(8,128)(2,1)} %all-to-all-done.cells_ref, bf16[768,2304]{1,0:T(8,128)(2,1)S(1)} %copy-done, f32[8,128]{1,0:T(8,128)S(1)} %copy-done.1), custom_call_target="tpu_custom_call" | custom-call | flops 4982833152 | bytes 14000000 | tf_op jit(solution)/shard_map/rotate/pallas_call | solution.py:260
  129.9 48.3 %all_to_all.10.parts = bf16[8,1968,128]{2,1,0:T(8,128)(2,1)S(1)} all-to-all(bf16[8,1968,128]{2,1,0:T(8,128)(2,1)S(1)} %rotate.1), channel_id=1, replica_groups=mesh['slab'=32,'blk'=8] {'blk'}, dimensions={0} | all-to-all | bytes 8060928 | tf_op jit(solution)/shard_map/all_to_all | solution.py:456
  178.3 2.1 %unpack.1 = (bf16[7776,128]{1,0:T(8,128)(2,1)}, bf16[7776,128]{1,0:T(8,128)(2,1)}) custom-call(bf16[8,1968,128]{2,1,0:T(8,128)(2,1)S(1)} %all_to_all.10.parts), custom_call_target="tpu_custom_call" | custom-call | tf_op jit(solution)/shard_map/unpack/pallas_call | solution.py:308
  (25 shorter events, 0.1 us)
Async XLA Ops:
  7.2 4.2 %collective-permute-start.1 = (bf16[72,96]{1,0:T(8,128)(2,1)}, bf16[72,96]{1,0:T(8,128)(2,1)S(1)}, u32[]{:S(2)}, u32[]{:S(2)}) collective-permute-start(bf16[72,96]{1,0:T(8,128)(2,1)} %param.9), channel_id=1, source_target_pairs={{0,1},{1,0},{2,3},{3,2},{4,5},{5,4},{6,7},{7,6},{8,9},{9,8},{10,11... | collective-permute-start | bytes 41480 | tf_op jit(solution)/shard_map/ppermute | solution.py:34
  8.5 4.2 %collective-permute-start.3 = (bf16[72,96]{1,0:T(8,128)(2,1)}, bf16[72,96]{1,0:T(8,128)(2,1)S(1)}, u32[]{:S(2)}, u32[]{:S(2)}) collective-permute-start(bf16[72,96]{1,0:T(8,128)(2,1)} %param.9), channel_id=1, source_target_pairs={{0,129},{1,128},{2,131},{3,130},{4,133},{5,132},{6,135},{7,134},{8... | collective-permute-start | bytes 41480 | tf_op jit(solution)/shard_map/ppermute | solution.py:47
  9.9 5.5 %collective-permute-start.2 = (bf16[72,96]{1,0:T(8,128)(2,1)}, bf16[72,96]{1,0:T(8,128)(2,1)S(1)}, u32[]{:S(2)}, u32[]{:S(2)}) collective-permute-start(bf16[72,96]{1,0:T(8,128)(2,1)} %param.9), channel_id=1, source_target_pairs={{0,128},{8,136},{16,144},{24,152},{32,160},{40,168},{48,176},{56,1... | collective-permute-start | bytes 41480 | tf_op jit(solution)/shard_map/ppermute | solution.py:34
  16.1 9.4 %collective-permute-start.5 = (bf16[4,72,96]{2,1,0:T(8,128)(2,1)S(1)}, bf16[4,72,96]{2,1,0:T(8,128)(2,1)S(1)}, u32[]{:S(2)}, u32[]{:S(2)}) collective-permute-start(bf16[4,72,96]{2,1,0:T(8,128)(2,1)S(1)} %get-tuple-element.20), channel_id=1, source_target_pairs={{0,4},{1,5},{2,6},{3,7},{4,0},{5,1},{6,2},{7,3},{8,12},{9,13},{10,... | collective-permute-start | bytes 165896 | tf_op jit(solution)/shard_map/ppermute | solution.py:34
  17.9 7.7 %collective-permute-start.4 = (bf16[4,72,96]{2,1,0:T(8,128)(2,1)S(1)}, bf16[4,72,96]{2,1,0:T(8,128)(2,1)S(1)}, u32[]{:S(2)}, u32[]{:S(2)}) collective-permute-start(bf16[4,72,96]{2,1,0:T(8,128)(2,1)S(1)} %get-tuple-element.20), channel_id=1, source_target_pairs={{0,6},{1,7},{2,0},{3,1},{4,2},{5,3},{6,4},{7,5},{8,14},{9,15},{10,... | collective-permute-start | bytes 165896 | tf_op jit(solution)/shard_map/ppermute | solution.py:34
  19.0 6.5 %collective-permute-start.6 = (bf16[4,72,96]{2,1,0:T(8,128)(2,1)S(1)}, bf16[4,72,96]{2,1,0:T(8,128)(2,1)S(1)}, u32[]{:S(2)}, u32[]{:S(2)}) collective-permute-start(bf16[4,72,96]{2,1,0:T(8,128)(2,1)S(1)} %get-tuple-element.20), channel_id=1, source_target_pairs={{0,2},{1,3},{2,4},{3,5},{4,6},{5,7},{6,0},{7,1},{8,10},{9,11},{10,... | collective-permute-start | bytes 165896 | tf_op jit(solution)/shard_map/ppermute | solution.py:34
  26.3 53.5 %copy-start.2 = (bf16[96,3,3,9,128]{4,0,3,2,1:T(8,128)(2,1)S(1)}, bf16[96,3,3,9,128]{4,0,3,2,1:T(8,128)(2,1)}, u32[]{:S(2)}) copy-start(bf16[96,3,3,9,128]{4,0,3,2,1:T(8,128)(2,1)} %param.7) | copy-start | bytes 5971972
  26.3 92.6 %all-to-all-start = ((bf16[8,2928,128]{2,1,0:T(8,128)(2,1)}), bf16[8,2928,128]{2,1,0:T(8,128)(2,1)}, u32[]{:S(2)}, u32[]{:S(2)}) async-start(bf16[8,2928,128]{2,1,0:T(8,128)(2,1)} %pack.1), calls=%async_computation | async-start | bytes 11993088 | tf_op jit(solution)/shard_map/all_to_all | solution.py:443
  31.3 48.5 %all-gather.3.cloned.1.call-start = ((), (), s32[]{:S(2)}) async-start(), calls=%async_computation.2 | async-start | bytes 2654208 | tf_op jit(solution)/shard_map/all_gather | solution.py:445
  79.8 31.1 %collective-permute-start.9 = (bf16[8,4,4,72,96]{4,3,2,1,0:T(8,128)(2,1)}, bf16[8,4,4,72,96]{4,3,2,1,0:T(8,128)(2,1)}, u32[]{:S(2)}, u32[]{:S(2)}) collective-permute-start(bf16[8,4,4,72,96]{4,3,2,1,0:T(8,128)(2,1)} %bitcast.43), channel_id=1, source_target_pairs={{0,8},{8,0},{16,24},{24,16},{32,40},{40,32},{48,56},{56,48},{64,72... | collective-permute-start | bytes 5308424 | tf_op jit(solution)/shard_map/ppermute | solution.py:34
  80.6 6.2 %copy-start.5 = (s32[3,9,128]{2,0,1:T(4,128)S(1)}, s32[3,9,128]{2,0,1:T(4,128)}, u32[]{:S(2)}) copy-start(s32[3,9,128]{2,0,1:T(4,128)} %param.10) | copy-start | bytes 41476
  80.6 6.4 %copy-start.6 = (f32[4,3,3]{2,0,1:T(4,128)S(1)}, f32[4,3,3]{2,0,1:T(4,128)}, u32[]{:S(2)}) copy-start(f32[4,3,3]{2,0,1:T(4,128)} %param.11) | copy-start | bytes 436
  81.5 22.4 %collective-permute-start.8 = (bf16[27,96,128]{2,1,0:T(8,128)(2,1)}, bf16[27,96,128]{2,1,0:T(8,128)(2,1)S(1)}, u32[]{:S(2)}, u32[]{:S(2)}) collective-permute-start(bf16[27,96,128]{2,1,0:T(8,128)(2,1)} %get-tuple-element.13), channel_id=1, source_target_pairs={{0,8},{8,16},{16,24},{24,32},{32,40},{40,48},{48,56},{56,64},{64,7... | collective-permute-start | bytes 1990664 | tf_op jit(solution)/shard_map/ppermute | solution.py:39
  82.0 21.9 %collective-permute-start.7 = (bf16[18,96,128]{2,1,0:T(8,128)(2,1)}, bf16[18,96,128]{2,1,0:T(8,128)(2,1)S(1)}, u32[]{:S(2)}, u32[]{:S(2)}) collective-permute-start(bf16[18,96,128]{2,1,0:T(8,128)(2,1)} %get-tuple-element.12), channel_id=1, source_target_pairs={{0,248},{8,0},{16,8},{24,16},{32,24},{40,32},{48,40},{56,48},{64,5... | collective-permute-start | bytes 1327112 | tf_op jit(solution)/shard_map/ppermute | solution.py:39
  86.9 16.4 %collective-permute-start = (s32[1,9,128]{2,0,1:T(1,128)S(1)}, s32[1,9,128]{2,0,1:T(1,128)S(1)}, u32[]{:S(2)}, u32[]{:S(2)}) collective-permute-start(s32[1,9,128]{2,0,1:T(1,128)S(1)} %slice.9), channel_id=1, source_target_pairs={{0,8},{8,16},{16,24},{24,32},{32,40},{40,48},{48,56},{56,64},{64,7... | collective-permute-start | bytes 13832 | tf_op jit(solution)/shard_map/ppermute | solution.py:39
  103.9 0.8 copy-start.4
  103.9 1.0 copy-start.3
  110.9 8.0 %copy-start.1 = (f32[8,128]{1,0:T(8,128)S(1)}, f32[8,128]{1,0:T(8,128)}, u32[]{:S(2)}) copy-start(f32[8,128]{1,0:T(8,128)} %get-tuple-element.16.after_ref) | copy-start | bytes 12292
  118.9 2.0 %copy-start = (bf16[768,2304]{1,0:T(8,128)(2,1)S(1)}, bf16[768,2304]{1,0:T(8,128)(2,1)}, u32[]{:S(2)}) copy-start(bf16[768,2304]{1,0:T(8,128)(2,1)} %assemble.1.coef_ref) | copy-start | bytes 10616836
Sparse Core Ops, SparseCore 0:
  34.5 45.2 all-gather.2

commit v8 on v7

--- a/solution.py
+++ b/solution.py
@@ -92,6 +92,24 @@
         ),
         name="assemble",
     )(place, mine, other)
+
+
+def from_below(x, z, core, y_lo):
+    both = ("slab", "blk")
+    straight, first, second = [], [], []
+    for h, k, c, b in itertools.product(range(2), range(8), range(2), range(NB)):
+        s = h * 16 + k * 2 + c
+        if k == 7 and c == 1 and b % 2 == 1:
+            target = ((1 - h) * 16) * NB + b
+            first.append((s * NB + b, (h * 16) * NB + b - 1))
+            second.append(((h * 16) * NB + b - 1, target))
+        else:
+            straight.append((s * NB + b, (s + 1) % 32 * NB + b))
+    half_way = lax.ppermute(x, both, first)
+    direct = lax.ppermute(x, both, straight)
+    round_about = lax.ppermute(half_way, both, second)
+    other_way = (z == 0) & (core == 0) & (y_lo == 1)
+    return jnp.where(other_way, round_about, direct)
 
 
 def lane_index(shape):
@@ -450,7 +468,7 @@
     high = layers[:, NZ - 1].reshape(3 * NY, V, 128)
     low, high = hold([low, high], [mine])
     above = ring_shift(low, "slab", -1)
-    below = ring_shift(high, "slab", 1)
+    below = from_below(high, place[1], place[2], place[4])
     applied, token = apply_curls(w, above, below, marks, inverse_permittivity.reshape(NMAT, 9))
     parts = rotate(cells, coef, token)
     back = lax.all_to_all(parts, "blk", split_axis=0, concat_axis=0, tiled=True)

time: 189 us -> 194 us (1.026)
  waiting for transfers between devices: 67.5 us -> 75.9 us
  blocking collectives: 48.3 us -> 45 us
    ppermute x0 -> x3, waiting for transfers between devices: none -> 18.6 us  [the longest x1 17.9 us: from_below(): half_way = lax.ppermute(x, both, first)]
    ppermute x3 -> x2, waiting for transfers between devices: 15 us -> 4.86 us  [ring_shift(): return lax.ppermute(x, axis, [(i, (i + by) % count) for i in range(count)])]
    ppermute x3 -> x2, starting transfers between devices: 5.44 us -> 0.64 us  [ring_shift(): return lax.ppermute(x, axis, [(i, (i + by) % count) for i in range(count)])]
    ppermute x0 -> x3, starting transfers between devices: none -> 4.52 us  [the longest x1 1.92 us: from_below(): direct = lax.ppermute(x, both, straight)]
    all_to_all x1, blocking collectives: 48.3 us -> 45 us  [per_device(): back = lax.all_to_all(parts, 'blk', split_axis=0, concat_axis=0, tiled=True)]
  transfers between devices with their start and end apart: 12 -> 14, of which waited for: 4 -> 6; matrix products, arithmetic and copies ran while one was open for 2% -> 2% of each run, Pallas kernels for 10% -> 10%
where the time goes in v8:
time: 194 us; the launch traced here: 193 us
  waiting for transfers between devices  75.9 us (39%)
  blocking collectives  45 us (23%)
  Pallas kernels  30.6 us (16%)
  starting transfers between devices  18.2 us (9%)
  between operations  14.2 us (7%)
  local copies, waits for them, and re-layouts  6.37 us (3%)
  other arithmetic  2.48 us (1%)
    all_gather x1, waiting for transfers between devices, per_device(): mine = lax.all_gather(plane, 'slab', axis_index_groups=groups)  47.7 us
    all_to_all x1, blocking collectives, per_device(): back = lax.all_to_all(parts, 'blk', split_axis=0, concat_axis=0, tiled=True)  45 us
    ppermute x1, waiting for transfers between devices, from_below(): half_way = lax.ppermute(x, both, first)  17.9 us
    pallas_call x1, Pallas kernels, rotate(): pl.pallas_call(rotate_kernel, out_shape=jax.ShapeDtypeStruct((NB, 2 * PAR...  8.99 us
    pallas_call x1, Pallas kernels, assemble(): pl.pallas_call(assemble_kernel, out_shape=jax.ShapeDtypeStruct((M, 3 * M)...  7.92 us
    ppermute x6, starting transfers between devices, move(): return lax.ppermute(x, axis, pairs)  6.62 us
    pallas_call x1, Pallas kernels, apply_curls(): pl.pallas_call(curl_kernel, out_shape=(jax.ShapeDtypeStruct((ROWS, V, 128...  6.05 us
    pallas_call x1, Pallas kernels, pack(): pl.pallas_call(pack_kernel, out_shape=jax.ShapeDtypeStruct(shape, jnp.bfl...  5.6 us
  transfers between devices with their start and end apart: 14, of which 6 were waited for; matrix products, arithmetic and copies ran while one was open for 2% of the time, Pallas kernels for 10%

profile of v8, /device:TPU:16, one launch (start us, length us, event | category | flops | bytes accessed | tf_op | source)
XLA Modules:
  0.0 192.7 jit_solution(14800618196851722349)
XLA Ops:
  7.2 1.4 collective-permute-start.1
  8.5 1.4 collective-permute-start.3
  9.9 1.5 collective-permute-start.2
  11.3 1.3 collective-permute-done.3
  12.7 2.7 %collective-permute-done.2 = bf16[72,96]{1,0:T(8,128)(2,1)S(1)} collective-permute-done((bf16[72,96]{1,0:T(8,128)(2,1)}, bf16[72,96]{1,0:T(8,128)(2,1)S(1)}, u32[]{:S(2)}, u32[]{:S(2)}) %collective-permute-start.2) | collective-permute-done | bytes 13856 | tf_op jit(solution)/shard_map/ppermute | solution.py:34
  15.4 0.7 fusion
  16.1 1.8 collective-permute-start.5
  17.9 1.1 collective-permute-start.4
  19.0 0.9 collective-permute-start.6
  19.9 5.6 %pack.1 = bf16[8,2928,128]{2,1,0:T(8,128)(2,1)} custom-call(bf16[7776,128]{1,0:T(8,128)(2,1)} %bitcast.39, bf16[7776,128]{1,0:T(8,128)(2,1)} %bitcast.47, bf16[7776,128]{1,0:T(8,128)(2,1)} %bitcast.48), custom_call_target="tpu_custom_call" | custom-call | flops 2000000 | bytes 12000000 | tf_op jit(solution)/shard_map/pack/pallas_call | solution.py:179
  25.5 0.8 pad_maximum_fusion
  26.3 5.0 %all-to-all-start = ((bf16[8,2928,128]{2,1,0:T(8,128)(2,1)}), bf16[8,2928,128]{2,1,0:T(8,128)(2,1)}, u32[]{:S(2)}, u32[]{:S(2)}) async-start(bf16[8,2928,128]{2,1,0:T(8,128)(2,1)} %pack.1), calls=%async_computation | async-start | bytes 11993088 | tf_op jit(solution)/shard_map/all_to_all | solution.py:461
  31.4 0.7 all-gather.3.cloned.1.call-update
  32.1 47.7 %all-gather.3.cloned.1.call-done = bf16[32,4,72,96]{3,2,1,0:T(8,128)(2,1)} async-done(((bf16[4,4,72,96]{3,2,1,0:T(8,128)(2,1)}), bf16[32,4,72,96]{3,2,1,0:T(8,128)(2,1)}) %all-gather.3.cloned.1.call-update) | async-done | bytes 1769488 | tf_op jit(solution)/shard_map/all_gather | solution.py:463
  79.8 0.8 slice.12
  80.6 0.9 slice.13
  81.5 1.3 collective-permute-start.8
  82.8 1.9 collective-permute-start.10
  84.7 17.9 %collective-permute-done.8 = bf16[27,96,128]{2,1,0:T(8,128)(2,1)S(1)} collective-permute-done((bf16[27,96,128]{2,1,0:T(8,128)(2,1)}, bf16[27,96,128]{2,1,0:T(8,128)(2,1)S(1)}, u32[]{:S(2)}, u32[]{:S(2)}) %collective-permute-start.8) | collective-permute-done | bytes 663584 | tf_op jit(solution)/shard_map/ppermute | solution.py:108
  102.6 1.3 collective-permute-start.9
  104.6 0.7 reshape.30.eps_ref
  105.2 0.6 stack.63.place_ref
  105.9 4.9 %collective-permute-done = s32[1,9,128]{2,0,1:T(1,128)S(1)} collective-permute-done((s32[1,9,128]{2,0,1:T(1,128)S(1)}, s32[1,9,128]{2,0,1:T(1,128)S(1)}, u32[]{:S(2)}, u32[]{:S(2)}) %collective-permute-start) | collective-permute-done | bytes 4640 | tf_op jit(solution)/shard_map/ppermute | solution.py:39
  111.4 0.7 collective-permute-done.9
  112.1 0.9 broadcast_select_fusion.below_ref
  113.0 0.8 copy-done.3
  113.8 6.1 %curls.1 = (bf16[81,96,128]{2,1,0:T(8,128)(2,1)}, f32[8,128]{1,0:T(8,128)}) custom-call(f32[4,9]{1,0:T(4,128)} %reshape.30.eps_ref, s32[36,128]{1,0:T(8,128)} %reshape.31.mat_ref, bf16[81,96,128]{2,1,0:T(8,128)(2,1)} %bitcast.40, bf16[18,96,128]{2,1,0:T(8,128)(2,1)} %copy-done.3, bf16[27,96,128]{2,1,0:T(8,128)(2,1)} %broadcast_select_fusion.below_ref), custom_call_target="tpu_custom_call" | custom-call | flops 60000000 | bytes 5000000 | tf_op jit(solution)/shard_map/curls/pallas_call | solution.py:417
  119.8 7.9 %assemble.1.coef_ref = bf16[768,2304]{1,0:T(8,128)(2,1)} custom-call(s32[5]{0:T(128)} %stack.63.place_ref, bf16[8,4,2,2,72,96]{5,4,3,2,1,0:T(8,128)(2,1)} %bitcast.45, bf16[8,4,2,2,72,96]{5,4,3,2,1,0:T(8,128)(2,1)} %bitcast.26.other_ref), custom_call_target="tpu_custom_call" | custom-call | flops 10000000 | bytes 8000000 | tf_op jit(solution)/shard_map/assemble/pallas_call | solution.py:80
  127.8 2.0 %copy-done = bf16[768,2304]{1,0:T(8,128)(2,1)S(1)} copy-done((bf16[768,2304]{1,0:T(8,128)(2,1)S(1)}, bf16[768,2304]{1,0:T(8,128)(2,1)}, u32[]{:S(2)}) %copy-start) | copy-done | bytes 3538968
  129.8 9.0 %rotate.1 = bf16[8,1968,128]{2,1,0:T(8,128)(2,1)S(1)} custom-call(bf16[8,2928,128]{2,1,0:T(8,128)(2,1)} %all-to-all-done.cells_ref, bf16[768,2304]{1,0:T(8,128)(2,1)S(1)} %copy-done, f32[8,128]{1,0:T(8,128)S(1)} %copy-done.1), custom_call_target="tpu_custom_call" | custom-call | flops 4982833152 | bytes 14000000 | tf_op jit(solution)/shard_map/rotate/pallas_call | solution.py:278
  138.8 45.0 %all_to_all.10.parts = bf16[8,1968,128]{2,1,0:T(8,128)(2,1)S(1)} all-to-all(bf16[8,1968,128]{2,1,0:T(8,128)(2,1)S(1)} %rotate.1), channel_id=1, replica_groups=mesh['slab'=32,'blk'=8] {'blk'}, dimensions={0} | all-to-all | bytes 8060928 | tf_op jit(solution)/shard_map/all_to_all | solution.py:474
  183.8 2.1 %unpack.1 = (bf16[7776,128]{1,0:T(8,128)(2,1)}, bf16[7776,128]{1,0:T(8,128)(2,1)}) custom-call(bf16[8,1968,128]{2,1,0:T(8,128)(2,1)S(1)} %all_to_all.10.parts), custom_call_target="tpu_custom_call" | custom-call | tf_op jit(solution)/shard_map/unpack/pallas_call | solution.py:326
  (28 shorter events, 1.4 us)
Async XLA Ops:
  7.2 4.2 %collective-permute-start.1 = (bf16[72,96]{1,0:T(8,128)(2,1)}, bf16[72,96]{1,0:T(8,128)(2,1)S(1)}, u32[]{:S(2)}, u32[]{:S(2)}) collective-permute-start(bf16[72,96]{1,0:T(8,128)(2,1)} %param.9), channel_id=1, source_target_pairs={{0,1},{1,0},{2,3},{3,2},{4,5},{5,4},{6,7},{7,6},{8,9},{9,8},{10,11... | collective-permute-start | bytes 41480 | tf_op jit(solution)/shard_map/ppermute | solution.py:34
  8.5 4.2 %collective-permute-start.3 = (bf16[72,96]{1,0:T(8,128)(2,1)}, bf16[72,96]{1,0:T(8,128)(2,1)S(1)}, u32[]{:S(2)}, u32[]{:S(2)}) collective-permute-start(bf16[72,96]{1,0:T(8,128)(2,1)} %param.9), channel_id=1, source_target_pairs={{0,129},{1,128},{2,131},{3,130},{4,133},{5,132},{6,135},{7,134},{8... | collective-permute-start | bytes 41480 | tf_op jit(solution)/shard_map/ppermute | solution.py:47
  9.9 5.5 %collective-permute-start.2 = (bf16[72,96]{1,0:T(8,128)(2,1)}, bf16[72,96]{1,0:T(8,128)(2,1)S(1)}, u32[]{:S(2)}, u32[]{:S(2)}) collective-permute-start(bf16[72,96]{1,0:T(8,128)(2,1)} %param.9), channel_id=1, source_target_pairs={{0,128},{8,136},{16,144},{24,152},{32,160},{40,168},{48,176},{56,1... | collective-permute-start | bytes 41480 | tf_op jit(solution)/shard_map/ppermute | solution.py:34
  16.1 9.4 %collective-permute-start.5 = (bf16[4,72,96]{2,1,0:T(8,128)(2,1)S(1)}, bf16[4,72,96]{2,1,0:T(8,128)(2,1)S(1)}, u32[]{:S(2)}, u32[]{:S(2)}) collective-permute-start(bf16[4,72,96]{2,1,0:T(8,128)(2,1)S(1)} %get-tuple-element.20), channel_id=1, source_target_pairs={{0,4},{1,5},{2,6},{3,7},{4,0},{5,1},{6,2},{7,3},{8,12},{9,13},{10,... | collective-permute-start | bytes 165896 | tf_op jit(solution)/shard_map/ppermute | solution.py:34
  17.9 7.6 %collective-permute-start.4 = (bf16[4,72,96]{2,1,0:T(8,128)(2,1)S(1)}, bf16[4,72,96]{2,1,0:T(8,128)(2,1)S(1)}, u32[]{:S(2)}, u32[]{:S(2)}) collective-permute-start(bf16[4,72,96]{2,1,0:T(8,128)(2,1)S(1)} %get-tuple-element.20), channel_id=1, source_target_pairs={{0,6},{1,7},{2,0},{3,1},{4,2},{5,3},{6,4},{7,5},{8,14},{9,15},{10,... | collective-permute-start | bytes 165896 | tf_op jit(solution)/shard_map/ppermute | solution.py:34
  19.0 6.5 %collective-permute-start.6 = (bf16[4,72,96]{2,1,0:T(8,128)(2,1)S(1)}, bf16[4,72,96]{2,1,0:T(8,128)(2,1)S(1)}, u32[]{:S(2)}, u32[]{:S(2)}) collective-permute-start(bf16[4,72,96]{2,1,0:T(8,128)(2,1)S(1)} %get-tuple-element.20), channel_id=1, source_target_pairs={{0,2},{1,3},{2,4},{3,5},{4,6},{5,7},{6,0},{7,1},{8,10},{9,11},{10,... | collective-permute-start | bytes 165896 | tf_op jit(solution)/shard_map/ppermute | solution.py:34
  26.3 53.5 %copy-start.2 = (bf16[96,3,3,9,128]{4,0,3,2,1:T(8,128)(2,1)S(1)}, bf16[96,3,3,9,128]{4,0,3,2,1:T(8,128)(2,1)}, u32[]{:S(2)}) copy-start(bf16[96,3,3,9,128]{4,0,3,2,1:T(8,128)(2,1)} %param.7) | copy-start | bytes 5971972
  26.3 101.4 %all-to-all-start = ((bf16[8,2928,128]{2,1,0:T(8,128)(2,1)}), bf16[8,2928,128]{2,1,0:T(8,128)(2,1)}, u32[]{:S(2)}, u32[]{:S(2)}) async-start(bf16[8,2928,128]{2,1,0:T(8,128)(2,1)} %pack.1), calls=%async_computation | async-start | bytes 11993088 | tf_op jit(solution)/shard_map/all_to_all | solution.py:461
  31.3 48.5 %all-gather.3.cloned.1.call-start = ((), (), s32[]{:S(2)}) async-start(), calls=%async_computation.2 | async-start | bytes 2654208 | tf_op jit(solution)/shard_map/all_gather | solution.py:463
  79.8 40.0 %collective-permute-start.11 = (bf16[8,4,4,72,96]{4,3,2,1,0:T(8,128)(2,1)}, bf16[8,4,4,72,96]{4,3,2,1,0:T(8,128)(2,1)}, u32[]{:S(2)}, u32[]{:S(2)}) collective-permute-start(bf16[8,4,4,72,96]{4,3,2,1,0:T(8,128)(2,1)} %bitcast.43), channel_id=1, source_target_pairs={{0,8},{8,0},{16,24},{24,16},{32,40},{40,32},{48,56},{56,48},{64,72... | collective-permute-start | bytes 5308424 | tf_op jit(solution)/shard_map/ppermute | solution.py:34
  80.6 23.4 %copy-start.4 = (s32[3,9,128]{2,0,1:T(4,128)S(1)}, s32[3,9,128]{2,0,1:T(4,128)}, u32[]{:S(2)}) copy-start(s32[3,9,128]{2,0,1:T(4,128)} %param.10) | copy-start | bytes 41476
  80.6 24.0 %copy-start.5 = (f32[4,3,3]{2,0,1:T(4,128)S(1)}, f32[4,3,3]{2,0,1:T(4,128)}, u32[]{:S(2)}) copy-start(f32[4,3,3]{2,0,1:T(4,128)} %param.11) | copy-start | bytes 436
  81.5 21.1 %collective-permute-start.8 = (bf16[27,96,128]{2,1,0:T(8,128)(2,1)}, bf16[27,96,128]{2,1,0:T(8,128)(2,1)S(1)}, u32[]{:S(2)}, u32[]{:S(2)}) collective-permute-start(bf16[27,96,128]{2,1,0:T(8,128)(2,1)} %get-tuple-element.13), channel_id=1, source_target_pairs={{121,0},{123,2},{125,4},{127,6},{249,128},{251,130},{253,132},{255... | collective-permute-start | bytes 1990664 | tf_op jit(solution)/shard_map/ppermute | solution.py:108
  82.8 28.6 %collective-permute-start.10 = (bf16[27,96,128]{2,1,0:T(8,128)(2,1)}, bf16[27,96,128]{2,1,0:T(8,128)(2,1)S(1)}, u32[]{:S(2)}, u32[]{:S(2)}) collective-permute-start(bf16[27,96,128]{2,1,0:T(8,128)(2,1)} %get-tuple-element.13), channel_id=1, source_target_pairs={{0,8},{1,9},{2,10},{3,11},{4,12},{5,13},{6,14},{7,15},{8,16},{9,17... | collective-permute-start | bytes 1990664 | tf_op jit(solution)/shard_map/ppermute | solution.py:109
  102.6 9.5 %collective-permute-start.9 = (bf16[27,96,128]{2,1,0:T(8,128)(2,1)S(1)}, bf16[27,96,128]{2,1,0:T(8,128)(2,1)S(1)}, u32[]{:S(2)}, u32[]{:S(2)}) collective-permute-start(bf16[27,96,128]{2,1,0:T(8,128)(2,1)S(1)} %collective-permute-done.8), channel_id=1, source_target_pairs={{0,129},{2,131},{4,133},{6,135},{128,1},{130,3},{132,5},{134,7}} | collective-permute-start | bytes 1990664 | tf_op jit(solution)/shard_map/ppermute | solution.py:110
  103.9 9.1 %collective-permute-start.7 = (bf16[18,96,128]{2,1,0:T(8,128)(2,1)}, bf16[18,96,128]{2,1,0:T(8,128)(2,1)S(1)}, u32[]{:S(2)}, u32[]{:S(2)}) collective-permute-start(bf16[18,96,128]{2,1,0:T(8,128)(2,1)} %get-tuple-element.12), channel_id=1, source_target_pairs={{0,248},{8,0},{16,8},{24,16},{32,24},{40,32},{48,40},{56,48},{64,5... | collective-permute-start | bytes 1327112 | tf_op jit(solution)/shard_map/ppermute | solution.py:39
  104.0 6.7 %collective-permute-start = (s32[1,9,128]{2,0,1:T(1,128)S(1)}, s32[1,9,128]{2,0,1:T(1,128)S(1)}, u32[]{:S(2)}, u32[]{:S(2)}) collective-permute-start(s32[1,9,128]{2,0,1:T(1,128)S(1)} %slice.9), channel_id=1, source_target_pairs={{0,8},{8,16},{16,24},{24,32},{32,40},{40,48},{48,56},{56,64},{64,7... | collective-permute-start | bytes 13832 | tf_op jit(solution)/shard_map/ppermute | solution.py:39
  113.0 0.8 copy-start.3
  119.8 7.9 %copy-start.1 = (f32[8,128]{1,0:T(8,128)S(1)}, f32[8,128]{1,0:T(8,128)}, u32[]{:S(2)}) copy-start(f32[8,128]{1,0:T(8,128)} %get-tuple-element.16.after_ref) | copy-start | bytes 12292
  127.8 2.0 %copy-start = (bf16[768,2304]{1,0:T(8,128)(2,1)S(1)}, bf16[768,2304]{1,0:T(8,128)(2,1)}, u32[]{:S(2)}) copy-start(bf16[768,2304]{1,0:T(8,128)(2,1)} %assemble.1.coef_ref) | copy-start | bytes 10616836
Sparse Core Ops, SparseCore 0:
  34.5 45.2 all-gather.2
